TPU v7x, 256 devices: a whole 4x4x8 slice. The times are simulated.
256 devices in a mesh: replica: 16 (over z, core), mp: 16 (over y, x).
Axes of the slice: x: 4, y: 4, z: 8, core: 2. Of those that a mesh axis runs over, the one named last changes fastest.
Arguments:
- pre_act: bfloat16 [2400, 32768], P('mp', 'replica'), may hold values from -6 to 6
- out_grad: bfloat16 [32768, 4800], P(('replica', 'mp')), may hold values from -6 to 6
- weight: bfloat16 [2400, 4800], P('mp'), may hold values from -0.09375 to 0.09375
- error: float32 [16, 2400, 4800], P('replica', 'mp'), may hold values from -96 to 96
- q_init: float32 [4800, 32], replicated, may hold values from -6 to 6
Outputs:
- pre_grad: bfloat16 [2400, 32768], P('mp', 'replica')
- new_error: float32 [16, 2400, 4800], P('replica', 'mp')
- q_new: float32 [4800, 32], replicated
All inputs are finite; a program needn't handle non-finite values.
Results may differ from a plain program's by a relative error of at most 0.013.
Values may be sent and summed in bfloat16 or wider, within the bound.
No kernel may reach another device: no remote copies, remote signals or barrier semaphores. Data moves between devices by JAX's collectives and lax.ppermute only.
A program may use at most 128 MiB of HBM per device.

v0:
```python
import jax
import jax.numpy as jnp
from jax import lax
from jax.sharding import PartitionSpec as P


def gelu_back(pre, grad):
    _, pull = jax.vjp(jax.nn.gelu, pre)
    return pull(grad)[0]


def shards(pre_act, out_grad, weight, error, q_init):
    hi = lax.Precision.HIGHEST
    groups = lax.axis_size("replica")
    act = jax.nn.gelu(pre_act.astype(jnp.float32)).astype(jnp.bfloat16)
    piece = lax.all_gather(out_grad, "mp", axis=0, tiled=True)
    back = jnp.einsum("kf,hf->hk", piece, weight, preferred_element_type=jnp.float32)
    pre_slice = pre_act.astype(jnp.float32)
    update = gelu_back(pre_slice, back).astype(jnp.bfloat16)
    pre_grad = update
    grad = jnp.dot(act, piece, preferred_element_type=jnp.float32)
    grad, pre_grad = (grad, pre_grad)
    mat = grad + error[0]
    p_local = jnp.dot(mat, q_init, precision=hi)
    pbar = lax.psum(p_local, "replica") / groups
    gram = lax.psum(jnp.dot(pbar.T, pbar, precision=hi), "mp")
    lower = jnp.linalg.cholesky(gram)
    phat = jax.scipy.linalg.solve_triangular(lower, pbar.T, lower=True).T
    q_local = jnp.dot(mat.T, phat, precision=hi)
    q_new = lax.psum(q_local, ("replica", "mp")) / groups
    approx = jnp.dot(phat, q_new.T, precision=hi)
    new_error = (mat - approx)[None]
    return (pre_grad, new_error, q_new)


def solution(mesh):
    return jax.shard_map(
        shards,
        mesh=mesh,
        in_specs=(
            P("mp", "replica"),
            P(("replica", "mp"), None),
            P("mp", None),
            P("replica", "mp", None),
            P(),
        ),
        out_specs=(P("mp", "replica"), P("replica", "mp", None), P()),
        check_vma=False,
    )
```

profile of v0, /device:TPU:1, one launch (start us, length us, event | category | flops | bytes accessed | tf_op | source)
XLA Modules:
  0.0 564.1 jit_solution(16882801023573134399)
XLA Ops:
  7.2 0.0 copy-start
  7.2 0.0 all-gather.2.cloned.1.call-start
  7.2 0.7 all-gather.2.cloned.1.call-update
  7.9 0.0 copy-start.3
  7.9 0.0 all-reduce.2.cloned.1.call-start
  8.0 146.1 %all-gather.2.cloned.1.call-done = bf16[2048,4800]{0,1:T(8,128)(2,1)} async-done(((bf16[128,4800]{0,1:T(8,128)(2,1)}), bf16[2048,4800]{0,1:T(8,128)(2,1)}) %all-gather.2.cloned.1.call-update) | async-done | bytes 19660816 | tf_op jit(solution)/shard_map/all_gather | solution.py:16
  154.1 11.3 %convolution_add_fusion = f32[150,4800]{1,0:T(8,128)S(1)} fusion(bf16[2048,4800]{0,1:T(8,128)(2,1)} %all-gather.2.cloned.1.call-done, f32[1,150,4800]{2,0,1:T(1,128)} %param.8, bf16[150,2048]{1,0:T(8,128)(2,1)} %param.5), kind=kOutput, calls=%fused_computation.2 | convolution fusion | flops 2952911872 | bytes 26035200 | tf_op jit(solution)/shard_map/dot_general | solution.py:21
  165.5 0.0 copy-start.1
  165.5 1.6 copy-done.1
  167.1 0.0 copy-done.3
  167.1 2.8 fusion.31
  169.9 45.4 %psum.21 = f32[150,32]{0,1:T(8,128)S(1)} all-reduce(f32[150,32]{0,1:T(8,128)S(1)} %fusion.31), channel_id=1, replica_groups=mesh['replica'=16,'mp'=16] {'replica'}, use_global_device_ids=true, to_apply=%region_0.0 | all-reduce | flops 4800 | bytes 38400 | tf_op jit(solution)/shard_map/psum | solution.py:25
  215.4 0.2 fusion.18
  215.5 58.2 %psum.22 = f32[32,32]{0,1:T(8,128)S(1)} all-reduce(f32[32,32]{0,1:T(8,128)S(1)} %fusion.18), channel_id=1, replica_groups=mesh['replica'=16,'mp'=16] {'mp'}, use_global_device_ids=true, to_apply=%region_1.0 | all-reduce | flops 1024 | bytes 8192 | tf_op jit(solution)/shard_map/psum | solution.py:26
  273.8 0.1 copy.9
  273.8 2.9 cholesky.16
  276.8 0.6 compare_reduce_fusion
  277.4 0.7 fusion.20
  278.1 2.4 custom-call.7
  280.5 0.2 fusion.16
  280.8 0.0 copy-start.4
  280.8 4.7 fusion.32
  285.5 0.0 all-reduce.2.cloned.1.call-update
  285.6 0.0 copy-done
  285.6 0.0 copy-done.4
  285.6 11.3 %fusion.4 = bf16[150,2048]{1,0:T(8,128)(2,1)} fusion(bf16[150,2048]{1,0:T(8,128)(2,1)S(1)} %copy-done.4, bf16[150,4800]{1,0:T(8,128)(2,1)S(1)} %copy-done, bf16[2048,4800]{0,1:T(8,128)(2,1)} %all-gather.2.cloned.1.call-done), kind=kOutput, calls=%fused_computation.11 | convolution fusion | flops 2955571200 | bytes 22329600 | tf_op jit(solution)/shard_map/kf,hf->hk/dot_general | solution.py:17
  296.9 250.0 %all-reduce.2.cloned.1.call-done = f32[4800,32]{0,1:T(8,128)} async-done(((f32[4800,32]{0,1:T(8,128)}), f32[4800,32]{0,1:T(8,128)}) %all-reduce.2.cloned.1.call-update) | async-done | bytes 614416 | tf_op jit(solution)/shard_map/psum | solution.py:30
  546.9 1.1 broadcast_multiply_fusion
  548.0 0.0 copy-start.2
  548.0 4.6 fusion
  552.6 0.0 copy-done.2
  552.6 4.6 copy.10
  (2 shorter events, 0.0 us)
Async XLA Ops:
  7.2 278.4 %copy-start = (bf16[150,4800]{1,0:T(8,128)(2,1)S(1)}, bf16[150,4800]{1,0:T(8,128)(2,1)}, u32[]{:S(2)}) copy-start(bf16[150,4800]{1,0:T(8,128)(2,1)} %param.7) | copy-start | bytes 4320004
  7.2 146.9 %all-gather.2.cloned.1.call-start = ((), (), s32[]{:S(2)}) async-start(), calls=%async_computation | async-start | bytes 20889600 | tf_op jit(solution)/shard_map/all_gather | solution.py:16
  7.9 159.2 %copy-start.3 = (f32[4800,32]{0,1:T(8,128)S(1)}, f32[4800,32]{0,1:T(8,128)}, u32[]{:S(2)}) copy-start(f32[4800,32]{0,1:T(8,128)} %param.9) | copy-start | bytes 1843204
  7.9 538.9 %all-reduce.2.cloned.1.call-start = ((), (), s32[]{:S(2)}) async-start(), calls=%async_computation.1 | async-start | bytes 1245184 | tf_op jit(solution)/shard_map/psum | solution.py:30
  165.5 1.7 copy-start.1
  280.8 4.8 copy-start.4
  548.0 4.7 copy-start.2
Sparse Core Ops, SparseCore 0:
  10.4 143.6 all-gather.1
  285.7 261.1 all-reduce.1
where the time goes:
time: 565 us; the launch traced here: 564 us
  waiting for transfers between devices  397 us (70%)
  blocking collectives  104 us (18%)
  matrix products  35.2 us (6%)
  between operations  14.2 us (3%)
  other arithmetic  7.8 us (1%)
  local copies, waits for them, and re-layouts  6.33 us (1%)
    psum x1, waiting for transfers between devices, shards(): q_new = lax.psum(q_local, ('replica', 'mp')) / groups  250 us
    all_gather x1, waiting for transfers between devices, shards(): piece = lax.all_gather(out_grad, 'mp', axis=0, tiled=True)  146 us
    psum x1, blocking collectives, shards(): gram = lax.psum(jnp.dot(pbar.T, pbar, precision=hi), 'mp')  58.2 us
    psum x1, blocking collectives, shards(): pbar = lax.psum(p_local, 'replica') / groups  45.4 us
    dot_general x1, matrix products, shards(): grad = jnp.dot(act, piece, preferred_element_type=jnp.float32)  11.3 us
    dot_general x1, matrix products, shards(): jnp.einsum('kf,hf->hk', piece, weight, preferred_element_type=jnp.float32)  11.3 us
  transfers between devices with their start and end apart: 2, of which 2 were waited for; matrix products, arithmetic and copies ran while one was open for 2% of the time, Pallas kernels for 0%

commit v1 on v0

v1 whole, which is shorter than its diff:
```python
import jax
import jax.numpy as jnp
from jax import lax
from jax.sharding import PartitionSpec as P

F32 = jnp.float32
BF16 = jnp.bfloat16


def gelu_back(pre, grad):
    _, pull = jax.vjp(jax.nn.gelu, pre)
    return pull(grad)[0]


def gelu16(pre):
    return jax.nn.gelu(pre.astype(F32)).astype(BF16)


def split(x, parts):
    out = []
    for _ in range(parts):
        top = lax.reduce_precision(x, 8, 7)
        out.append(top.astype(BF16))
        x = x - top
    return out


def dot(a, b, ca, cb):
    return lax.dot_general(a, b, (((ca,), (cb,)), ((), ())), preferred_element_type=F32)


def fold(x, parts, axis=0):
    n = x.shape[axis] // parts
    return sum(lax.slice_in_dim(x, i * n, (i + 1) * n, axis=axis) for i in range(parts))


def spread(x, axis):
    n = lax.axis_size(axis)
    return lax.all_to_all(jnp.broadcast_to(x, (n,) + x.shape), axis, 0, 0, tiled=True)


def shards(pre_act, out_grad, weight, error, q_init):
    hi = lax.Precision.HIGHEST
    groups = lax.axis_size("replica")
    mp = lax.axis_size("mp")
    rank = q_init.shape[1]
    hid, toks = pre_act.shape
    own, feat = out_grad.shape
    error = error[0]

    cut = feat // 256 * 128
    blocks = [(0, cut), (cut, feat)]
    pieces = [lax.all_gather(out_grad[:, lo:up], "mp", axis=0, tiled=True) for lo, up in blocks]

    q3 = jnp.concatenate(split(q_init, 3), axis=1)
    y = fold(dot(q3, out_grad, 0, 1), 3)
    y3 = jnp.concatenate(split(y, 3), axis=0)
    mine = pre_act.reshape(hid, mp, own).transpose(1, 0, 2)
    room = -(-hid // 16) * 16
    sent = jnp.concatenate(
        [mine, jnp.zeros((mp, room - hid, own), BF16), jnp.broadcast_to(y3, (mp,) + y3.shape)], axis=1
    )
    got = lax.all_to_all(sent, "mp", 0, 0, tiled=True)
    act_own = gelu16(got[:, :hid])
    y_all = got[:, room:].transpose(1, 0, 2).reshape(3 * rank, toks)
    act = gelu16(pre_act)
    e2 = split(error, 2)
    p_err = sum(fold(dot(q3, e, 0, 1), 3) for e in e2)
    p_local = fold(dot(y_all, act, 1, 1), 3) + p_err
    pbar = jnp.sum(spread(p_local, "replica"), axis=0) / groups
    p_all = spread(pbar, "mp")

    gram = jnp.einsum("mih,mjh->ij", p_all, p_all, precision=hi)
    lower = jnp.linalg.cholesky(gram)
    inv = jax.scipy.linalg.solve_triangular(lower, jnp.eye(rank, dtype=F32), lower=True)

    p3 = jnp.concatenate(split(p_all, 3), axis=1)
    z = fold(lax.dot_general(p3, act_own, (((2,), (1,)), ((0,), (0,))), preferred_element_type=F32).sum(0), 3)
    z3 = jnp.concatenate(split(z, 3), axis=0)
    l3 = jnp.concatenate(split(pbar, 3), axis=0)
    r_local = fold(dot(z3, out_grad, 1, 0), 3) + sum(fold(dot(l3, e, 1, 0), 3) for e in e2)
    rows = r_local.reshape(mp, rank // mp, feat)
    r_part = jnp.sum(lax.all_to_all(rows, "mp", 0, 0, tiled=True), axis=0)
    r_part = jnp.sum(spread(r_part, "replica"), axis=0) / groups
    r_all = spread(r_part, "mp").reshape(rank, feat)
    q_t = jnp.dot(inv, r_all, precision=hi)
    phat = jnp.dot(inv, pbar, precision=hi)

    ph, pl = split(phat, 2)
    qh, ql = split(q_t, 2)
    left = jnp.concatenate([ph, ph, pl], axis=0)
    right = jnp.concatenate([qh, ql, qh], axis=0)
    back = 0.0
    errs = []
    for (lo, up), piece in zip(blocks, pieces):
        back = back + dot(weight[:, lo:up], piece, 1, 1)
        mat = dot(act, piece, 1, 0) + error[:, lo:up]
        errs.append(mat - dot(left, right[:, lo:up], 0, 0))
    pre_grad = gelu_back(pre_act.astype(F32), back).astype(BF16)
    new_error = jnp.concatenate(errs, axis=1)[None]
    return (pre_grad, new_error, q_t.T)


def solution(mesh):
    return jax.shard_map(
        shards,
        mesh=mesh,
        in_specs=(
            P("mp", "replica"),
            P(("replica", "mp"), None),
            P("mp", None),
            P("replica", "mp", None),
            P(),
        ),
        out_specs=(P("mp", "replica"), P("replica", "mp", None), P()),
        check_vma=False,
    )
```

time: 565 us -> 247 us (0.44)
  waiting for transfers between devices: 397 us -> 95 us
  blocking collectives: 104 us -> 51.8 us
  starting transfers between devices: 0.08 us -> 19.6 us
  local copies, waits for them, and re-layouts: 6.33 us -> 19.4 us
    psum x1 -> x0, waiting for transfers between devices: 250 us -> none  [shards(): q_new = lax.psum(q_local, ('replica', 'mp')) / groups]
    psum x2 -> x0, blocking collectives: 104 us -> none  [the longest x1 58.2 us: shards(): gram = lax.psum(jnp.dot(pbar.T, pbar, precision=hi), 'mp')]
    all_gather x1 -> x2, waiting for transfers between devices: 146 us -> 43.7 us  [shards(): lax.all_gather(out_grad[:, lo:up], 'mp', axis=0, tiled=True)]
    all_to_all x0 -> x2, blocking collectives: none -> 51.8 us  [the longest x1 29.8 us: spread(): lax.all_to_all(jnp.broadcast_to(x, (n,) + x.shape), axis, 0, 0, tiled=True)]
    all_to_all x0 -> x4, waiting for transfers between devices: none -> 51.3 us  [the longest x3 34.4 us: spread(): lax.all_to_all(jnp.broadcast_to(x, (n,) + x.shape), axis, 0, 0, tiled=True)]
    all_to_all x0 -> x4, starting transfers between devices: none -> 19.5 us  [the longest x3 11.7 us: spread(): lax.all_to_all(jnp.broadcast_to(x, (n,) + x.shape), axis, 0, 0, tiled=True)]
    dot_general x6 -> x17, matrix products: 35 us -> 34.6 us  [the longest x13 30.4 us: dot(): lax.dot_general(a, b, (((ca,), (cb,)), ((), ())), preferred_element_type=...]
  transfers between devices with their start and end apart: 2 -> 6, of which waited for: 2 -> 5; matrix products, arithmetic and copies ran while one was open for 2% -> 18% of each run, Pallas kernels for 0% -> 0%
where the time goes in v1:
time: 247 us; the launch traced here: 246 us
  waiting for transfers between devices  95 us (38%)
  blocking collectives  51.8 us (21%)
  matrix products  34.8 us (14%)
  starting transfers between devices  19.6 us (8%)
  local copies, waits for them, and re-layouts  19.4 us (8%)
  between operations  14.5 us (6%)
  other arithmetic  11.4 us (5%)
    all_gather x2, waiting for transfers between devices, shards(): lax.all_gather(out_grad[:, lo:up], 'mp', axis=0, tiled=True)  43.7 us
    all_to_all x3, waiting for transfers between devices, spread(): lax.all_to_all(jnp.broadcast_to(x, (n,) + x.shape), axis, 0, 0, tiled=True)  34.4 us
    dot_general x13, matrix products, dot(): lax.dot_general(a, b, (((ca,), (cb,)), ((), ())), preferred_element_type=...  30.4 us
    all_to_all x1, blocking collectives, spread(): lax.all_to_all(jnp.broadcast_to(x, (n,) + x.shape), axis, 0, 0, tiled=True)  29.8 us
    all_to_all x1, blocking collectives, shards(): r_part = jnp.sum(lax.all_to_all(rows, 'mp', 0, 0, tiled=True), axis=0)  21.9 us
    all_to_all x1, waiting for transfers between devices, shards(): got = lax.all_to_all(sent, 'mp', 0, 0, tiled=True)  16.9 us
    all_to_all x3, starting transfers between devices, spread(): lax.all_to_all(jnp.broadcast_to(x, (n,) + x.shape), axis, 0, 0, tiled=True)  11.7 us
    unnamed x41, local copies, waits for them, and re-layouts  9.28 us
  transfers between devices with their start and end apart: 6, of which 5 were waited for; matrix products, arithmetic and copies ran while one was open for 18% of the time, Pallas kernels for 0%

profile of v1, /device:TPU:1, one launch (start us, length us, event | category | flops | bytes accessed | tf_op | source)
XLA Modules:
  0.0 246.4 jit_solution(8934448072027616238)
XLA Ops:
  7.2 2.0 slice.115
  9.3 0.9 slice.117
  10.9 0.4 fusion.85
  11.3 0.3 copy-done.12
  11.9 0.3 pad_maximum_fusion
  12.3 1.2 copy.35
  13.5 7.8 %all-to-all-start = ((bf16[16,256,128]{2,1,0:T(8,128)(2,1)}), bf16[16,256,128]{2,1,0:T(8,128)(2,1)}, u32[]{:S(2)}, u32[]{:S(2)}) async-start(bf16[16,256,128]{2,1,0:T(8,128)(2,1)} %copy.35), calls=%async_computation | async-start | bytes 2097152 | tf_op jit(solution)/shard_map/all_to_all | solution.py:63
  21.3 1.7 fusion.38
  23.0 0.6 fusion.52
  23.6 16.9 %all-to-all-done = bf16[16,256,128]{2,1,0:T(8,128)(2,1)} async-done(((bf16[16,256,128]{2,1,0:T(8,128)(2,1)}), bf16[16,256,128]{2,1,0:T(8,128)(2,1)}, u32[]{:S(2)}, u32[]{:S(2)}) %all-to-all-start) | async-done | bytes 1048608 | tf_op jit(solution)/shard_map/all_to_all | solution.py:63
  40.5 1.8 fusion.47
  42.6 29.8 %all_to_all.30 = f32[16,32,150]{2,1,0:T(8,128)S(1)} all-to-all(f32[16,32,150]{2,1,0:T(8,128)S(1)} %broadcast_in_dim.25), channel_id=1, replica_groups=mesh['replica'=16,'mp'=16] {'replica'}, dimensions={0} | all-to-all | bytes 614400 | tf_op jit(solution)/shard_map/all_to_all | solution.py:39
  72.5 0.8 broadcast_in_dim.26
  73.3 3.6 %all-to-all-start.2 = ((f32[16,32,150]{2,1,0:T(8,128)}), f32[16,32,150]{2,1,0:T(8,128)S(1)}, u32[]{:S(2)}, u32[]{:S(2)}) async-start(f32[16,32,150]{2,1,0:T(8,128)} %broadcast_in_dim.26), calls=%async_computation.2 | async-start | bytes 1048576 | tf_op jit(solution)/shard_map/all_to_all | solution.py:39
  76.9 1.7 fusion.50
  78.7 1.8 fusion.37
  80.4 12.7 %all-to-all-done.2 = f32[16,32,150]{2,1,0:T(8,128)S(1)} async-done(((f32[16,32,150]{2,1,0:T(8,128)}), f32[16,32,150]{2,1,0:T(8,128)S(1)}, u32[]{:S(2)}, u32[]{:S(2)}) %all-to-all-start.2) | async-done | bytes 307232 | tf_op jit(solution)/shard_map/all_to_all | solution.py:39
  93.3 2.0 convolution_bitcast_fusion
  95.3 0.5 fusion.60
  95.8 1.0 copy-done.2
  96.8 1.1 fusion.31
  97.9 2.3 reshape.30
  100.1 21.9 %all_to_all.31 = f32[16,2,4800]{2,1,0:T(2,128)} all-to-all(f32[16,2,4800]{2,1,0:T(2,128)} %reshape.30), channel_id=1, replica_groups=mesh['replica'=16,'mp'=16] {'mp'}, dimensions={0} | all-to-all | bytes 1228800 | tf_op jit(solution)/shard_map/all_to_all | solution.py:83
  122.1 1.3 reduce_sum.32
  123.4 1.0 broadcast_in_dim.27
  124.4 4.4 %all-to-all-start.4 = ((f32[16,2,4800]{2,1,0:T(2,128)}), f32[16,2,4800]{2,1,0:T(2,128)}, u32[]{:S(2)}, u32[]{:S(2)}) async-start(f32[16,2,4800]{2,1,0:T(2,128)} %broadcast_in_dim.27), calls=%async_computation.4 | async-start | bytes 1245184 | tf_op jit(solution)/shard_map/all_to_all | solution.py:39
  128.7 1.8 copy.64
  130.5 0.6 convolution_bitcast_fusion.1
  131.2 2.9 %cholesky.17 = f32[32,32]{1,0:T(8,128)S(1)} custom-call(f32[32,32]{1,0:T(8,128)S(1)} %fusion.73), custom_call_target="Cholesky" | custom-call | tf_op jit(solution)/shard_map/jit(cholesky)/cholesky | solution.py:74
  134.1 0.6 compare_reduce_fusion
  134.8 13.4 %all-to-all-done.4 = f32[16,2,4800]{2,1,0:T(2,128)} async-done(((f32[16,2,4800]{2,1,0:T(2,128)}), f32[16,2,4800]{2,1,0:T(2,128)}, u32[]{:S(2)}, u32[]{:S(2)}) %all-to-all-start.4) | async-done | bytes 614432 | tf_op jit(solution)/shard_map/all_to_all | solution.py:39
  148.2 1.3 reduce_sum.33
  149.5 1.0 broadcast_in_dim.28
  150.4 3.8 %all-to-all-start.5 = ((f32[16,2,4800]{2,1,0:T(2,128)}), f32[16,2,4800]{2,1,0:T(2,128)S(1)}, u32[]{:S(2)}, u32[]{:S(2)}) async-start(f32[16,2,4800]{2,1,0:T(2,128)} %broadcast_in_dim.28), calls=%async_computation.5 | async-start | bytes 1245184 | tf_op jit(solution)/shard_map/all_to_all | solution.py:39
  154.2 0.7 fusion.66
  154.9 2.4 custom-call.7
  157.7 8.3 %all-to-all-done.5 = f32[16,2,4800]{2,1,0:T(2,128)S(1)} async-done(((f32[16,2,4800]{2,1,0:T(2,128)}), f32[16,2,4800]{2,1,0:T(2,128)S(1)}, u32[]{:S(2)}, u32[]{:S(2)}) %all-to-all-start.5) | async-done | bytes 614432 | tf_op jit(solution)/shard_map/all_to_all | solution.py:39
  166.1 0.4 reshape.31
  166.5 1.5 fusion.29
  168.0 7.6 %convolution_add_fusion = f32[150,2304]{1,0:T(8,128)S(1)} fusion(bf16[2048,2304]{0,1:T(8,128)(2,1)} %all-gather.3.cloned.1.call-done, f32[150,4800]{1,0:T(8,128)} %bitcast.55, bf16[150,2048]{1,0:T(8,128)(2,1)S(1)} %copy-done.10), kind=kOutput, calls=%fused_computation.4 | convolution fusion | flops 1418995200 | bytes 12816384 | tf_op jit(solution)/shard_map/dot_general | solution.py:29
  175.6 0.4 convolution_subtract_fusion
  176.0 1.0 copy-done.6
  177.0 1.7 fusion.24
  178.7 43.7 %all-gather.5.cloned.1.call-done = bf16[2048,2496]{0,1:T(8,128)(2,1)} async-done(((bf16[128,2496]{0,1:T(8,128)(2,1)}), bf16[2048,2496]{0,1:T(8,128)(2,1)}) %all-gather.5.cloned.1.call-update) | async-done | bytes 10223632 | tf_op jit(solution)/shard_map/all_gather | solution.py:53
  222.4 8.1 %convolution_add_fusion.1 = f32[150,2496]{1,0:T(8,128)S(1)} fusion(bf16[2048,2496]{0,1:T(8,128)(2,1)} %all-gather.5.cloned.1.call-done, f32[150,4800]{1,0:T(8,128)} %bitcast.56, bf16[150,2048]{1,0:T(8,128)(2,1)} %param.5), kind=kOutput, calls=%fused_computation.5 | convolution fusion | flops 1536988800 | bytes 13833216 | tf_op jit(solution)/shard_map/dot_general | solution.py:29
  230.6 0.4 convolution_subtract_fusion.1
  231.2 4.6 %copy.41 = f32[1,150,4800]{2,0,1:T(1,128)} copy(f32[1,150,4800]{2,1,0:T(8,128)S(1)} %maximum_bitcast_fusion) | data formatting | bytes 5760000
  235.8 3.7 %fusion.5 = bf16[150,2048]{1,0:T(8,128)(2,1)} fusion(bf16[150,2048]{1,0:T(8,128)(2,1)S(1)} %copy-done.11, f32[150,2048]{1,0:T(8,128)S(1)} %fusion.24, bf16[2048,2496]{0,1:T(8,128)(2,1)S(1)} %bitcast.61, bf16[150,4800]{1,0:T(8,128)(2,1)S(1)} %copy-done.7), kind=kOutput, calls=%fused_computation.23 | convolution fusion | flops 1540300800 | bytes 13484032 | tf_op jit(solution)/shard_map/dot_general | solution.py:29
  (65 shorter events, 2.3 us)
Async XLA Ops:
  7.2 2.2 copy-start.4
  7.2 160.8 %all-gather.3.cloned.1.call-start = ((), (), s32[]{:S(2)}) async-start(), calls=%async_computation.6 | async-start | bytes 10027008 | tf_op jit(solution)/shard_map/all_gather | solution.py:53
  9.2 1.1 copy-start.9
  9.3 1.5 copy-start.8
  9.3 213.1 %all-gather.5.cloned.1.call-start = ((), (), s32[]{:S(2)}) async-start(), calls=%async_computation.7 | async-start | bytes 10862592 | tf_op jit(solution)/shard_map/all_gather | solution.py:53
  10.9 0.7 copy-start.12
  10.9 0.8 copy-start.14
  12.3 9.0 %copy-start = (f32[1,150,4800]{2,0,1:T(1,128)S(1)}, f32[1,150,4800]{2,0,1:T(1,128)}, u32[]{:S(2)}) copy-start(f32[1,150,4800]{2,0,1:T(1,128)} %param.8) | copy-start | bytes 8640004
  13.5 27.0 %all-to-all-start = ((bf16[16,256,128]{2,1,0:T(8,128)(2,1)}), bf16[16,256,128]{2,1,0:T(8,128)(2,1)}, u32[]{:S(2)}, u32[]{:S(2)}) async-start(bf16[16,256,128]{2,1,0:T(8,128)(2,1)} %copy.35), calls=%async_computation | async-start | bytes 2097152 | tf_op jit(solution)/shard_map/all_to_all | solution.py:63
  21.3 1.7 copy-start.13
  21.3 1.7 copy-start.15
  73.3 19.8 %all-to-all-start.2 = ((f32[16,32,150]{2,1,0:T(8,128)}), f32[16,32,150]{2,1,0:T(8,128)S(1)}, u32[]{:S(2)}, u32[]{:S(2)}) async-start(f32[16,32,150]{2,1,0:T(8,128)} %broadcast_in_dim.26), calls=%async_computation.2 | async-start | bytes 1048576 | tf_op jit(solution)/shard_map/all_to_all | solution.py:39
  93.3 2.0 copy-start.5
  93.3 2.6 %copy-start.3 = (f32[96,4800]{1,0:T(8,128)S(1)}, f32[96,4800]{1,0:T(8,128)}, u32[]{:S(2)}) copy-start(f32[96,4800]{1,0:T(8,128)} %fusion.37) | copy-start | bytes 5529604
  95.3 1.5 copy-start.2
  124.4 23.8 %all-to-all-start.4 = ((f32[16,2,4800]{2,1,0:T(2,128)}), f32[16,2,4800]{2,1,0:T(2,128)}, u32[]{:S(2)}, u32[]{:S(2)}) async-start(f32[16,2,4800]{2,1,0:T(2,128)} %broadcast_in_dim.27), calls=%async_computation.4 | async-start | bytes 1245184 | tf_op jit(solution)/shard_map/all_to_all | solution.py:39
  150.4 15.6 %all-to-all-start.5 = ((f32[16,2,4800]{2,1,0:T(2,128)}), f32[16,2,4800]{2,1,0:T(2,128)S(1)}, u32[]{:S(2)}, u32[]{:S(2)}) async-start(f32[16,2,4800]{2,1,0:T(2,128)} %broadcast_in_dim.28), calls=%async_computation.5 | async-start | bytes 1245184 | tf_op jit(solution)/shard_map/all_to_all | solution.py:39
  157.7 10.3 %copy-start.10 = (bf16[150,2048]{1,0:T(8,128)(2,1)S(1)}, bf16[150,2048]{1,0:T(8,128)(2,1)}, u32[]{:S(2)}) copy-start(bf16[150,2048]{1,0:T(8,128)(2,1)} %param.5) | copy-start | bytes 1843204
  168.0 8.0 %copy-start.1 = (bf16[2048,2304]{0,1:T(8,128)(2,1)S(1)}, bf16[2048,2304]{0,1:T(8,128)(2,1)}, u32[]{:S(2)}) copy-start(bf16[2048,2304]{0,1:T(8,128)(2,1)} %all-gather.3.cloned.1.call-done) | copy-start | bytes 28311556
  175.6 1.4 copy-start.6
  222.4 13.4 %slice-start = ((s8[10223616]{0:T(1024)(128)(4,1)}), s8[4194304]{0:T(1024)(128)(4,1)S(1)}, s32[]{:S(2)}) async-start(s8[10223616]{0:T(1024)(128)(4,1)} %bitcast.60), calls=%async_computation.8 | async-start | bytes 8388608
  222.4 13.4 %slice-start.1 = ((s8[10223616]{0:T(1024)(128)(4,1)}), s8[4194304]{0:T(1024)(128)(4,1)S(1)}, s32[]{:S(2)}) async-start(s8[10223616]{0:T(1024)(128)(4,1)} %bitcast.60), calls=%async_computation.9 | async-start | bytes 8388608
  231.0 4.8 %slice-start.2 = ((s8[10223616]{0:T(1024)(128)(4,1)}), s8[1835008]{0:T(1024)(128)(4,1)S(1)}, s32[]{:S(2)}) async-start(s8[10223616]{0:T(1024)(128)(4,1)} %bitcast.60), calls=%async_computation.10 | async-start | bytes 3670016
  231.2 4.6 %copy-start.7 = (bf16[150,4800]{1,0:T(8,128)(2,1)S(1)}, bf16[150,4800]{1,0:T(8,128)(2,1)}, u32[]{:S(2)}) copy-start(bf16[150,4800]{1,0:T(8,128)(2,1)} %param.7) | copy-start | bytes 4320004
  231.2 4.6 %copy-start.11 = (bf16[150,2048]{1,0:T(8,128)(2,1)S(1)}, bf16[150,2048]{1,0:T(8,128)(2,1)}, u32[]{:S(2)}) copy-start(bf16[150,2048]{1,0:T(8,128)(2,1)} %param.5) | copy-start | bytes 1843204
Sparse Core Ops, SparseCore 0:
  10.4 111.0 all-gather.2
  124.0 98.4 all-gather.4

commit v2 on v1

v2 whole, which is shorter than its diff:
```python
import jax
import jax.numpy as jnp
import numpy as np
from jax import lax
from jax.experimental import pallas as pl
from jax.experimental.pallas import tpu as pltpu
from jax.sharding import Mesh, PartitionSpec as P

F32 = jnp.float32
BF16 = jnp.bfloat16
MP = ("y", "x")
ALL = ("z", "core", "y", "x")


def gelu_back(pre, grad):
    _, pull = jax.vjp(jax.nn.gelu, pre)
    return pull(grad)[0]


def gelu16(pre):
    return jax.nn.gelu(pre.astype(F32)).astype(BF16)


def split(x, parts):
    out = []
    for _ in range(parts):
        top = lax.reduce_precision(x, 8, 7)
        out.append(top.astype(BF16))
        x = x - top
    return out


def dot(a, b, ca, cb):
    return lax.dot_general(a, b, (((ca,), (cb,)), ((), ())), preferred_element_type=F32)


def fold(x, parts, axis=0):
    n = x.shape[axis] // parts
    return sum(lax.slice_in_dim(x, i * n, (i + 1) * n, axis=axis) for i in range(parts))


def spread(x, axis):
    n = lax.axis_size(axis)
    return lax.all_to_all(jnp.broadcast_to(x, (n,) + x.shape), axis, 0, 0, tiled=True)


def other_core(x):
    return lax.ppermute(x, "core", [(0, 1), (1, 0)])


def shift(x, sizes, along_b, step):
    nz, nc, ny, nx = sizes
    at = lambda z, c, y, w: ((z * nc + c) * ny + y % ny) * nx + w % nx
    perm = []
    for z, c, y, w in np.ndindex(*sizes):
        along_x = along_b == (c == 0)
        src = at(z, c, y, w + step) if along_x else at(z, c, y + step, w)
        perm.append((src, at(z, c, y, w)))
    return lax.ppermute(x, ALL, perm)


def products(where, pre_ref, weight_ref, b0, b1, b2, b3, mat_in, grad_in, mat_ref, grad_ref):
    grad_ref[...] = grad_in[...]
    own = b0.shape[1]
    blocks = (b0, b1, b2, b3)
    spots = [pl.ds(pl.multiple_of(where[i] * own, own), own) for i in range(4)]
    pre = jnp.concatenate([pre_ref[:, s] for s in spots], axis=1).astype(F32)
    act, pull = jax.vjp(jax.nn.gelu, pre)
    act = act.astype(BF16)
    feat = weight_ref.shape[1]
    back = jnp.zeros(pre.shape, F32)
    for lo in range(0, feat, 512):
        part = slice(lo, min(feat, lo + 512))
        piece = jnp.concatenate([b[part, :] for b in blocks], axis=1)
        back = back + dot(weight_ref[:, part], piece, 1, 0)
        mat_ref[:, part] = mat_in[:, part] + dot(act, piece, 1, 1)
    out = pull(back)[0].astype(BF16)
    for i, s in enumerate(spots):
        grad_ref[:, s] = out[:, i * own:(i + 1) * own]


def add_products(where, pre_act, weight, blocks, mat, pre_grad):
    vmem = pl.BlockSpec(memory_space=pltpu.VMEM)
    return pl.pallas_call(
        products,
        out_shape=(jax.ShapeDtypeStruct(mat.shape, F32), jax.ShapeDtypeStruct(pre_grad.shape, BF16)),
        in_specs=[pl.BlockSpec(memory_space=pltpu.SMEM)] + [vmem] * 8,
        out_specs=(vmem, vmem),
        input_output_aliases={7: 0, 8: 1},
        compiler_params=pltpu.CompilerParams(vmem_limit_bytes=40 * 2**20),
    )(where, pre_act, weight, *blocks, mat, pre_grad)


def shards(sizes, pre_act, out_grad, weight, error, q_init):
    hi = lax.Precision.HIGHEST
    nz, nc, ny, nx = sizes
    groups = nz * nc
    mp = ny * nx
    rank = q_init.shape[1]
    half = rank // 2
    hid, toks = pre_act.shape
    own, feat = out_grad.shape
    error = error[0]
    core = lax.axis_index("core")

    got = {(0, 0): out_grad.T}
    along_a = lambda k, step: shift(got[k], sizes, False, step)
    along_b = lambda k, step: shift(got[k], sizes, True, step)

    def tie(value, keys):
        out = lax.optimization_barrier([value] + [got[k] for k in keys])
        got.update(zip(keys, out[1:]))
        return out[0]

    for step in (1, -1):
        got[0, step] = along_b((0, 0), step)
        got[step, 0] = along_a((0, 0), step)

    act = gelu16(pre_act)
    q3 = jnp.concatenate(split(q_init, 3), axis=1)
    y = fold(dot(q3, out_grad, 0, 1), 3)
    y_all = spread(y, MP).transpose(1, 0, 2).reshape(rank, toks)
    y3 = jnp.concatenate(split(y_all, 3), axis=0)
    e2 = split(error, 2)
    p_err = sum(fold(dot(q3, e, 0, 1), 3) for e in e2)
    p_local = fold(dot(y3, act, 1, 1), 3) + p_err
    p_local = tie(p_local, [(0, 1), (0, -1), (1, 0), (-1, 0)])
    got[0, 2] = along_b((0, 1), 1)
    got[2, 0] = along_a((1, 0), 1)
    for db in (1, -1):
        for da in (1, -1):
            got[da, db] = along_a((0, db), da)
    pbar = jnp.sum(spread(p_local, "z"), axis=0)
    pbar = (pbar + other_core(pbar)) / groups

    l3 = jnp.concatenate(split(pbar, 3), axis=0)
    z_part = fold(dot(l3, act, 1, 0), 3)
    gram_part = jnp.dot(pbar, pbar.T, precision=hi)
    side = 128 // rank
    flat = jnp.concatenate(jnp.split(gram_part, side, axis=0), axis=1)
    sent = jnp.concatenate(
        [
            z_part.reshape(rank, mp, own).transpose(1, 0, 2),
            jnp.broadcast_to(flat, (mp,) + flat.shape),
        ],
        axis=1,
    )
    took = jnp.sum(lax.all_to_all(sent, MP, 0, 0, tiled=True), axis=0)
    z = took[:rank]
    gram = jnp.concatenate(jnp.split(took[rank:], side, axis=1), axis=0)

    z3 = jnp.concatenate(split(z, 3), axis=0)
    r_local = fold(dot(z3, out_grad, 1, 0), 3) + sum(fold(dot(l3, e, 1, 0), 3) for e in e2)
    low, high = r_local[:half], r_local[half:]
    keep = jnp.where(core == 0, low, high) + other_core(jnp.where(core == 0, high, low))
    r_part = lax.all_to_all(keep.reshape(mp, half // mp, feat), MP, 0, 0, tiled=True)
    r_part = jnp.sum(r_part, axis=0)
    r_part = tie(r_part, [(0, 2), (2, 0), (1, 1), (-1, 1), (1, -1), (-1, -1)])
    got[1, 2] = along_a((0, 2), 1)
    got[-1, 2] = along_a((0, 2), -1)
    got[2, 1] = along_a((1, 1), 1)
    got[2, -1] = along_a((-1, -1), -1)
    r_part = jnp.sum(spread(r_part, "z"), axis=0) / groups
    mine = spread(r_part, MP).reshape(half, feat)
    mine = tie(mine, [(1, 2)])
    got[2, 2] = along_a((1, 2), 1)
    theirs = other_core(mine)
    r_all = jnp.concatenate([jnp.where(core == 0, mine, theirs), jnp.where(core == 0, theirs, mine)], axis=0)

    lower = jnp.linalg.cholesky(gram)
    inv = jax.scipy.linalg.solve_triangular(lower, jnp.eye(rank, dtype=F32), lower=True)
    q_t = jnp.dot(inv, r_all, precision=hi)
    phat = jnp.dot(inv, pbar, precision=hi)

    iy, ix = lax.axis_index("y"), lax.axis_index("x")
    ia, ib = jnp.where(core == 0, iy, ix), jnp.where(core == 0, ix, iy)
    mat, pre_grad = error, jnp.zeros_like(pre_act)
    for da in (0, 1, -1, 2):
        keys = [(da, db) for db in (0, 1, -1, 2)]
        a, b = (ia + da) & 3, (ib + jnp.array([0, 1, -1, 2])) & 3
        where = jnp.where(core == 0, a * nx + b, b * nx + a)
        mat, pre_grad = add_products(where, pre_act, weight, [got[k] for k in keys], mat, pre_grad)

    ph, pw = split(phat, 2)
    qh, ql = split(q_t, 2)
    left = jnp.concatenate([ph, ph, pw], axis=0)
    right = jnp.concatenate([qh, ql, qh], axis=0)
    new_error = (mat - dot(left, right, 0, 0))[None]
    return (pre_grad, new_error, q_t.T)


def solution(mesh):
    sizes = (mesh.shape["replica"] // 2, 2, 4, mesh.shape["mp"] // 4)
    grid = Mesh(mesh.devices.reshape(sizes), ALL)

    def run(*args):
        return shards(sizes, *args)

    return jax.shard_map(
        run,
        mesh=grid,
        in_specs=(
            P(MP, ("z", "core")),
            P(ALL, None),
            P(MP, None),
            P(("z", "core"), MP, None),
            P(),
        ),
        out_specs=(P(MP, ("z", "core")), P(("z", "core"), MP, None), P()),
        check_vma=False,
    )
```

time: 247 us -> 209 us (0.85)
  blocking collectives: 51.8 us -> 18.8 us
  starting transfers between devices: 19.6 us -> 50 us
  waiting for transfers between devices: 95 us -> 70.8 us
  Pallas kernels: 0 us -> 23.2 us
  matrix products: 34.8 us -> 14.6 us
  between operations: 14.5 us -> 1.11 us
    all_gather x2 -> x0, waiting for transfers between devices: 43.7 us -> none  [shards(): lax.all_gather(out_grad[:, lo:up], 'mp', axis=0, tiled=True)]
    ppermute x0 -> x18, starting transfers between devices: none -> 27.7 us  [the longest x15 20.8 us: shift(): return lax.ppermute(x, ALL, perm)]
    pallas_call x0 -> x4, Pallas kernels: none -> 23.2 us  [add_products(): pl.pallas_call(products, out_shape=(jax.ShapeDtypeStruct(mat.shape, F32),...]
    all_to_all x1 -> x0, blocking collectives: 21.9 us -> none  [shards(): r_part = jnp.sum(lax.all_to_all(rows, 'mp', 0, 0, tiled=True), axis=0)]
    all_to_all x1 -> x2, waiting for transfers between devices: 16.9 us -> 38.8 us  [the longest x1 32.2 us: shards(): lax.all_to_all(keep.reshape(mp, half // mp, feat), MP, 0, 0, tiled=True)]
    dot_general x13 -> x9, matrix products: 30.4 us -> 12.6 us  [dot(): lax.dot_general(a, b, (((ca,), (cb,)), ((), ())), preferred_element_type=...]
    all_to_all x1, blocking collectives: 29.8 us -> 18.8 us  [spread(): lax.all_to_all(jnp.broadcast_to(x, (n,) + x.shape), axis, 0, 0, tiled=True)]
    all_to_all x3, waiting for transfers between devices: 34.4 us -> 30.5 us  [spread(): lax.all_to_all(jnp.broadcast_to(x, (n,) + x.shape), axis, 0, 0, tiled=True)]
  transfers between devices with their start and end apart: 6 -> 23, of which waited for: 5 -> 7; matrix products, arithmetic and copies ran while one was open for 18% -> 16% of each run, Pallas kernels for 0% -> 9%
where the time goes in v2:
time: 209 us; the launch traced here: 208 us
  waiting for transfers between devices  70.8 us (34%)
  starting transfers between devices  50 us (24%)
  Pallas kernels  23.2 us (11%)
  blocking collectives  18.8 us (9%)
  local copies, waits for them, and re-layouts  17.3 us (8%)
  matrix products  14.6 us (7%)
  other arithmetic  11.9 us (6%)
    all_to_all x1, waiting for transfers between devices, shards(): lax.all_to_all(keep.reshape(mp, half // mp, feat), MP, 0, 0, tiled=True)  32.2 us
    all_to_all x3, waiting for transfers between devices, spread(): lax.all_to_all(jnp.broadcast_to(x, (n,) + x.shape), axis, 0, 0, tiled=True)  30.5 us
    pallas_call x4, Pallas kernels, add_products(): pl.pallas_call(products, out_shape=(jax.ShapeDtypeStruct(mat.shape, F32),...  23.2 us
    ppermute x15, starting transfers between devices, shift(): return lax.ppermute(x, ALL, perm)  20.8 us
    all_to_all x1, blocking collectives, spread(): lax.all_to_all(jnp.broadcast_to(x, (n,) + x.shape), axis, 0, 0, tiled=True)  18.8 us
    all_to_all x3, starting transfers between devices, spread(): lax.all_to_all(jnp.broadcast_to(x, (n,) + x.shape), axis, 0, 0, tiled=True)  15.2 us
    unnamed x33, local copies, waits for them, and re-layouts  12.8 us
    dot_general x9, matrix products, dot(): lax.dot_general(a, b, (((ca,), (cb,)), ((), ())), preferred_element_type=...  12.6 us
  transfers between devices with their start and end apart: 23, of which 7 were waited for; matrix products, arithmetic and copies ran while one was open for 16% of the time, Pallas kernels for 9%

profile of v2, /device:TPU:1, one launch (start us, length us, event | category | flops | bytes accessed | tf_op | source)
XLA Modules:
  0.0 207.8 jit_solution(18112357197310224844)
XLA Ops:
  0.6 3.6 %collective-permute-start = (bf16[4800,128]{1,0:T(8,128)(2,1)}, bf16[4800,128]{1,0:T(8,128)(2,1)}, u32[]{:S(2)}, u32[]{:S(2)}) collective-permute-start(bf16[4800,128]{1,0:T(8,128)(2,1)} %bitcast.59), channel_id=1, source_target_pairs={{1,0},{2,1},{3,2},{0,3},{5,4},{6,5},{7,6},{4,7},{9,8},{10,9},{11,1... | collective-permute-start | bytes 3686408 | tf_op jit(solution)/shard_map/ppermute | solution.py:59
  4.3 2.5 %collective-permute-start.2 = (bf16[4800,128]{1,0:T(8,128)(2,1)}, bf16[4800,128]{1,0:T(8,128)(2,1)}, u32[]{:S(2)}, u32[]{:S(2)}) collective-permute-start(bf16[4800,128]{1,0:T(8,128)(2,1)} %bitcast.61), channel_id=1, source_target_pairs={{4,0},{5,1},{6,2},{7,3},{8,4},{9,5},{10,6},{11,7},{12,8},{13,9},{1... | collective-permute-start | bytes 3686408 | tf_op jit(solution)/shard_map/ppermute | solution.py:59
  6.8 1.2 reduce-precision_convert_fusion.3
  8.0 1.7 fusion.69
  10.4 6.4 %all-to-all-start = ((f32[16,32,128]{2,1,0:T(8,128)}), f32[16,32,128]{2,1,0:T(8,128)S(1)}, u32[]{:S(2)}, u32[]{:S(2)}) async-start(f32[16,32,128]{2,1,0:T(8,128)} %broadcast_in_dim.23), calls=%async_computation | async-start | bytes 524288 | tf_op jit(solution)/shard_map/all_to_all | solution.py:44
  16.9 2.5 %fusion.37 = f32[96,150]{0,1:T(8,128)S(1)} fusion(bf16[4800,32]{0,1:T(8,128)(2,1)S(1)} %get-tuple-element.69, bf16[4800,32]{0,1:T(8,128)(2,1)S(1)} %get-tuple-element.70, bf16[4800,32]{0,1:T(8,128)(2,1)S(1)} %get-tuple-element.68, f32[1,150,4800]{2,0,1:T(1,128)} %param.12), kind=kOutput, calls=%fused_computation.68 | convolution fusion | flops 143884800 | bytes 3859200 | tf_op jit(solution)/shard_map/dot_general | solution.py:34
  20.2 20.4 %all-to-all-done = f32[16,32,128]{2,1,0:T(8,128)S(1)} async-done(((f32[16,32,128]{2,1,0:T(8,128)}), f32[16,32,128]{2,1,0:T(8,128)S(1)}, u32[]{:S(2)}, u32[]{:S(2)}) %all-to-all-start) | async-done | bytes 262176 | tf_op jit(solution)/shard_map/all_to_all | solution.py:44
  41.6 18.8 %all_to_all.30 = f32[8,32,150]{2,1,0:T(8,128)S(1)} all-to-all(f32[8,32,150]{2,1,0:T(8,128)S(1)} %broadcast_in_dim.24), channel_id=1, replica_groups=mesh['z'=8,'core'=2,'y'=4,'x'=4] {'z'}, dimensions={0} | all-to-all | bytes 307200 | tf_op jit(solution)/shard_map/all_to_all | solution.py:44
  60.4 2.1 %collective-permute-start.4 = (f32[32,150]{1,0:T(8,128)S(1)}, f32[32,150]{1,0:T(8,128)S(1)}, u32[]{:S(2)}, u32[]{:S(2)}) collective-permute-start(f32[32,150]{1,0:T(8,128)S(1)} %reduce_sum.38), channel_id=1, source_target_pairs={{0,16},{16,0},{1,17},{17,1},{2,18},{18,2},{3,19},{19,3},{4,20},{20... | collective-permute-start | bytes 57608 | tf_op jit(solution)/shard_map/ppermute | solution.py:48
  62.5 0.8 collective-permute-start.6
  64.2 1.0 copy-done.10
  65.2 1.8 fusion.24
  67.2 0.7 pad_maximum_fusion.1
  67.9 3.5 %all-to-all-start.2 = ((f32[16,40,128]{2,1,0:T(8,128)}), f32[16,40,128]{2,1,0:T(8,128)S(1)}, u32[]{:S(2)}, u32[]{:S(2)}) async-start(f32[16,40,128]{2,1,0:T(8,128)} %pad_maximum_fusion.1), calls=%async_computation.2 | async-start | bytes 655360 | tf_op jit(solution)/shard_map/all_to_all | solution.py:148
  71.5 3.7 %fusion.35 = f32[96,4800]{1,0:T(8,128)} fusion(bf16[32,150]{1,0:T(8,128)(2,1)S(1)} %get-tuple-element.77, bf16[32,150]{1,0:T(8,128)(2,1)S(1)} %get-tuple-element.76, bf16[32,150]{1,0:T(8,128)(2,1)S(1)} %get-tuple-element.62, f32[1,150,4800]{2,0,1:T(1,128)} %param.12), kind=kOutput, calls=%fused_computation.67 | convolution fusion | flops 141206400 | bytes 4752000 | tf_op jit(solution)/shard_map/dot_general | solution.py:34
  75.1 6.5 %all-to-all-done.2 = f32[16,40,128]{2,1,0:T(8,128)S(1)} async-done(((f32[16,40,128]{2,1,0:T(8,128)}), f32[16,40,128]{2,1,0:T(8,128)S(1)}, u32[]{:S(2)}, u32[]{:S(2)}) %all-to-all-start.2) | async-done | bytes 327712 | tf_op jit(solution)/shard_map/all_to_all | solution.py:148
  82.3 0.9 copy-done.11
  83.2 1.8 fusion.19
  85.0 1.8 collective-permute-start.5
  86.9 2.0 collective-permute-start.8
  88.9 2.7 %collective-permute-start.10 = (bf16[4800,128]{1,0:T(8,128)(2,1)}, bf16[4800,128]{1,0:T(8,128)(2,1)}, u32[]{:S(2)}, u32[]{:S(2)}) collective-permute-start(bf16[4800,128]{1,0:T(8,128)(2,1)} %collective-permute-done.1.b2), channel_id=1, source_target_pairs={{4,0},{5,1},{6,2},{7,3},{8,4},{9,5},{10,6},{11,7},{12,8},{13,9},{1... | collective-permute-start | bytes 3686408 | tf_op jit(solution)/shard_map/ppermute | solution.py:59
  91.6 2.7 %collective-permute-start.7 = (bf16[4800,128]{1,0:T(8,128)(2,1)}, bf16[4800,128]{1,0:T(8,128)(2,1)}, u32[]{:S(2)}, u32[]{:S(2)}) collective-permute-start(bf16[4800,128]{1,0:T(8,128)(2,1)} %collective-permute-done.2.b0), channel_id=1, source_target_pairs={{4,0},{5,1},{6,2},{7,3},{8,4},{9,5},{10,6},{11,7},{12,8},{13,9},{1... | collective-permute-start | bytes 3686408 | tf_op jit(solution)/shard_map/ppermute | solution.py:59
  94.3 1.0 copy.52
  95.4 3.5 %all-to-all-start.3 = ((f32[16,1,4800]{2,1,0:T(1,128)}), f32[16,1,4800]{2,1,0:T(1,128)S(1)}, u32[]{:S(2)}, u32[]{:S(2)}) async-start(f32[16,1,4800]{2,1,0:T(1,128)} %copy.52), calls=%async_computation.3 | async-start | bytes 622592 | tf_op jit(solution)/shard_map/all_to_all | solution.py:156
  98.9 2.0 copy.91
  101.0 32.2 %all-to-all-done.3 = f32[16,1,4800]{2,1,0:T(1,128)S(1)} async-done(((f32[16,1,4800]{2,1,0:T(1,128)}), f32[16,1,4800]{2,1,0:T(1,128)S(1)}, u32[]{:S(2)}, u32[]{:S(2)}) %all-to-all-start.3) | async-done | bytes 307232 | tf_op jit(solution)/shard_map/all_to_all | solution.py:156
  133.5 3.4 %collective-permute-start.14 = (bf16[4800,128]{1,0:T(8,128)(2,1)}, bf16[4800,128]{1,0:T(8,128)(2,1)}, u32[]{:S(2)}, u32[]{:S(2)}) collective-permute-start(bf16[4800,128]{1,0:T(8,128)(2,1)} %copy-done.7), channel_id=1, source_target_pairs={{4,0},{5,1},{6,2},{7,3},{8,4},{9,5},{10,6},{11,7},{12,8},{13,9},{1... | collective-permute-start | bytes 3686408 | tf_op jit(solution)/shard_map/ppermute | solution.py:59
  138.3 3.4 %all-to-all-start.4 = ((f32[8,1,4800]{2,1,0:T(1,128)}), f32[8,1,4800]{2,1,0:T(1,128)S(1)}, u32[]{:S(2)}, u32[]{:S(2)}) async-start(f32[8,1,4800]{2,1,0:T(1,128)} %broadcast_in_dim.26), calls=%async_computation.4 | async-start | bytes 311296 | tf_op jit(solution)/shard_map/all_to_all | solution.py:44
  141.8 2.9 %cholesky.17 = f32[32,32]{1,0:T(8,128)S(1)} custom-call(f32[32,32]{1,0:T(8,128)S(1)} %fusion.61), custom_call_target="Cholesky" | custom-call | tf_op jit(solution)/shard_map/jit(cholesky)/cholesky | solution.py:170
  144.7 6.0 %all-to-all-done.4 = f32[8,1,4800]{2,1,0:T(1,128)S(1)} async-done(((f32[8,1,4800]{2,1,0:T(1,128)}), f32[8,1,4800]{2,1,0:T(1,128)S(1)}, u32[]{:S(2)}, u32[]{:S(2)}) %all-to-all-start.4) | async-done | bytes 153632 | tf_op jit(solution)/shard_map/all_to_all | solution.py:44
  150.8 0.9 broadcast_in_dim.27
  151.7 5.3 %all-to-all-start.5 = ((f32[16,1,4800]{2,1,0:T(1,128)}), f32[16,1,4800]{2,1,0:T(1,128)S(1)}, u32[]{:S(2)}, u32[]{:S(2)}) async-start(f32[16,1,4800]{2,1,0:T(1,128)} %broadcast_in_dim.27), calls=%async_computation.5 | async-start | bytes 622592 | tf_op jit(solution)/shard_map/all_to_all | solution.py:44
  158.4 2.4 %custom-call.7 = f32[1,32,32]{1,2,0:T(8,128)S(1)} custom-call(f32[1,32,32]{2,1,0:T(8,128)S(1)} %fusion.56), custom_call_target="InvertDiagBlocksLowerTriangular" | custom-call | tf_op jit(solution)/shard_map/jit(_solve_triangular)/triangular_solve | solution.py:171
  160.8 4.1 %all-to-all-done.5 = f32[16,1,4800]{2,1,0:T(1,128)S(1)} async-done(((f32[16,1,4800]{2,1,0:T(1,128)}), f32[16,1,4800]{2,1,0:T(1,128)S(1)}, u32[]{:S(2)}, u32[]{:S(2)}) %all-to-all-start.5) | async-done | bytes 307232 | tf_op jit(solution)/shard_map/all_to_all | solution.py:44
  165.0 2.9 %collective-permute-start.17 = (f32[16,4800]{1,0:T(8,128)S(1)}, f32[16,4800]{1,0:T(8,128)S(1)}, u32[]{:S(2)}, u32[]{:S(2)}) collective-permute-start(f32[16,4800]{1,0:T(8,128)S(1)} %bitcast.64), channel_id=1, source_target_pairs={{0,16},{16,0},{1,17},{17,1},{2,18},{18,2},{3,19},{19,3},{4,20},{20... | collective-permute-start | bytes 921608 | tf_op jit(solution)/shard_map/ppermute | solution.py:48
  168.7 1.1 collective-permute-start.13
  169.8 0.9 broadcast_in_dim.28.grad_in
  170.7 1.4 copy-done
  172.1 1.1 copy-done.2
  173.1 1.3 copy-done.8
  174.4 5.6 %shard_map.112 = (f32[150,4800]{1,0:T(8,128)S(1)}, bf16[150,2048]{1,0:T(8,128)(2,1)}) custom-call(s32[4]{0:T(128)S(1)} %get-tuple-element.89.where, bf16[150,2048]{1,0:T(8,128)(2,1)S(1)} %copy-done.2, bf16[150,4800]{1,0:T(8,128)(2,1)S(1)} %copy-done, bf16[4800,128]{1,0:T(8,128)(2,1)S(1)} %bitcast.63, ...), custom_call_target="tpu_custom_call", output_to_operand_aliasing={{0}: (7, {}), {1}: (8, {})} | custom-call | tf_op jit(solution)/shard_map/pallas_call | solution.py:84
  180.0 1.6 collective-permute-start.15
  181.6 6.4 %shard_map.113 = (f32[150,4800]{1,0:T(8,128)S(1)}, bf16[150,2048]{1,0:T(8,128)(2,1)}) custom-call(s32[4]{0:T(128)S(1)} %get-tuple-element.91.where, bf16[150,2048]{1,0:T(8,128)(2,1)S(1)} %copy-done.2, bf16[150,4800]{1,0:T(8,128)(2,1)S(1)} %copy-done, bf16[4800,128]{1,0:T(8,128)(2,1)} %collective-permute-done.2.b0, ...), custom_call_target="tpu_custom_call", output_to_operand_aliasing={{0}: (7, {}), {1}: (8, {})} | custom-call | tf_op jit(solution)/shard_map/pallas_call | solution.py:84
  188.0 6.0 %shard_map.114 = (f32[150,4800]{1,0:T(8,128)S(1)}, bf16[150,2048]{1,0:T(8,128)(2,1)}) custom-call(s32[4]{0:T(128)S(1)} %get-tuple-element.90.where, bf16[150,2048]{1,0:T(8,128)(2,1)S(1)} %copy-done.2, bf16[150,4800]{1,0:T(8,128)(2,1)S(1)} %copy-done, bf16[4800,128]{1,0:T(8,128)(2,1)S(1)} %copy-done.6, ...), custom_call_target="tpu_custom_call", output_to_operand_aliasing={{0}: (7, {}), {1}: (8, {})} | custom-call | tf_op jit(solution)/shard_map/pallas_call | solution.py:84
  194.1 1.5 fusion.17
  196.1 1.4 collective-permute-done.15.b3
  197.6 5.2 %shard_map.115 = (f32[150,4800]{1,0:T(8,128)S(1)}, bf16[150,2048]{1,0:T(8,128)(2,1)}) custom-call(s32[4]{0:T(128)S(1)} %get-tuple-element.92.where, bf16[150,2048]{1,0:T(8,128)(2,1)S(1)} %copy-done.2, bf16[150,4800]{1,0:T(8,128)(2,1)S(1)} %copy-done, bf16[4800,128]{1,0:T(8,128)(2,1)} %collective-permute-done.7.b0, ...), custom_call_target="tpu_custom_call", output_to_operand_aliasing={{0}: (7, {}), {1}: (8, {})} | custom-call | tf_op jit(solution)/shard_map/pallas_call | solution.py:84
  203.2 4.6 %copy.59 = f32[1,150,4800]{2,0,1:T(1,128)} copy(f32[1,150,4800]{2,1,0:T(8,128)S(1)} %subtract_bitcast_fusion) | data formatting | bytes 5760000
  (90 shorter events, 9.1 us)
Async XLA Ops:
  0.6 40.8 %collective-permute-start = (bf16[4800,128]{1,0:T(8,128)(2,1)}, bf16[4800,128]{1,0:T(8,128)(2,1)}, u32[]{:S(2)}, u32[]{:S(2)}) collective-permute-start(bf16[4800,128]{1,0:T(8,128)(2,1)} %bitcast.59), channel_id=1, source_target_pairs={{1,0},{2,1},{3,2},{0,3},{5,4},{6,5},{7,6},{4,7},{9,8},{10,9},{11,1... | collective-permute-start | bytes 3686408 | tf_op jit(solution)/shard_map/ppermute | solution.py:59
  4.3 37.2 %collective-permute-start.1 = (bf16[4800,128]{1,0:T(8,128)(2,1)}, bf16[4800,128]{1,0:T(8,128)(2,1)}, u32[]{:S(2)}, u32[]{:S(2)}) collective-permute-start(bf16[4800,128]{1,0:T(8,128)(2,1)} %bitcast.60), channel_id=1, source_target_pairs={{3,0},{0,1},{1,2},{2,3},{7,4},{4,5},{5,6},{6,7},{11,8},{8,9},{9,10... | collective-permute-start | bytes 3686408 | tf_op jit(solution)/shard_map/ppermute | solution.py:59
  4.3 37.2 %collective-permute-start.2 = (bf16[4800,128]{1,0:T(8,128)(2,1)}, bf16[4800,128]{1,0:T(8,128)(2,1)}, u32[]{:S(2)}, u32[]{:S(2)}) collective-permute-start(bf16[4800,128]{1,0:T(8,128)(2,1)} %bitcast.61), channel_id=1, source_target_pairs={{4,0},{5,1},{6,2},{7,3},{8,4},{9,5},{10,6},{11,7},{12,8},{13,9},{1... | collective-permute-start | bytes 3686408 | tf_op jit(solution)/shard_map/ppermute | solution.py:59
  6.8 34.7 %collective-permute-start.3 = (bf16[4800,128]{1,0:T(8,128)(2,1)}, bf16[4800,128]{1,0:T(8,128)(2,1)S(1)}, u32[]{:S(2)}, u32[]{:S(2)}) collective-permute-start(bf16[4800,128]{1,0:T(8,128)(2,1)} %bitcast.62), channel_id=1, source_target_pairs={{12,0},{13,1},{14,2},{15,3},{0,4},{1,5},{2,6},{3,7},{4,8},{5,9},{6... | collective-permute-start | bytes 3686408 | tf_op jit(solution)/shard_map/ppermute | solution.py:59
  10.4 30.1 %all-to-all-start = ((f32[16,32,128]{2,1,0:T(8,128)}), f32[16,32,128]{2,1,0:T(8,128)S(1)}, u32[]{:S(2)}, u32[]{:S(2)}) async-start(f32[16,32,128]{2,1,0:T(8,128)} %broadcast_in_dim.23), calls=%async_computation | async-start | bytes 524288 | tf_op jit(solution)/shard_map/all_to_all | solution.py:44
  16.9 2.7 %copy-start.9 = (f32[1,150,4800]{2,0,1:T(1,128)S(1)}, f32[1,150,4800]{2,0,1:T(1,128)}, u32[]{:S(2)}) copy-start(f32[1,150,4800]{2,0,1:T(1,128)} %param.12) | copy-start | bytes 8640004
  19.6 21.1 %copy-start.1 = (bf16[150,2048]{1,0:T(8,128)(2,1)S(1)}, bf16[150,2048]{1,0:T(8,128)(2,1)}, u32[]{:S(2)}) copy-start(bf16[150,2048]{1,0:T(8,128)(2,1)} %pre_ref.7) | copy-start | bytes 1843204
  41.5 22.8 %copy-start.5 = (bf16[4800,128]{1,0:T(8,128)(2,1)}, bf16[4800,128]{1,0:T(8,128)(2,1)S(1)}, u32[]{:S(2)}) copy-start(bf16[4800,128]{1,0:T(8,128)(2,1)S(1)} %collective-permute-done.3.b0) | copy-start | bytes 3686404
  60.4 3.0 %collective-permute-start.4 = (f32[32,150]{1,0:T(8,128)S(1)}, f32[32,150]{1,0:T(8,128)S(1)}, u32[]{:S(2)}, u32[]{:S(2)}) collective-permute-start(f32[32,150]{1,0:T(8,128)S(1)} %reduce_sum.38), channel_id=1, source_target_pairs={{0,16},{16,0},{1,17},{17,1},{2,18},{18,2},{3,19},{19,3},{4,20},{20... | collective-permute-start | bytes 57608 | tf_op jit(solution)/shard_map/ppermute | solution.py:48
  62.5 29.1 %collective-permute-start.6 = (bf16[4800,128]{1,0:T(8,128)(2,1)}, bf16[4800,128]{1,0:T(8,128)(2,1)S(1)}, u32[]{:S(2)}, u32[]{:S(2)}) collective-permute-start(bf16[4800,128]{1,0:T(8,128)(2,1)} %collective-permute-done.b1), channel_id=1, source_target_pairs={{1,0},{2,1},{3,2},{0,3},{5,4},{6,5},{7,6},{4,7},{9,8},{10,9},{11,1... | collective-permute-start | bytes 3686408 | tf_op jit(solution)/shard_map/ppermute | solution.py:59
  63.4 1.8 copy-start.10
  67.9 13.8 %all-to-all-start.2 = ((f32[16,40,128]{2,1,0:T(8,128)}), f32[16,40,128]{2,1,0:T(8,128)S(1)}, u32[]{:S(2)}, u32[]{:S(2)}) async-start(f32[16,40,128]{2,1,0:T(8,128)} %pad_maximum_fusion.1), calls=%async_computation.2 | async-start | bytes 655360 | tf_op jit(solution)/shard_map/all_to_all | solution.py:148
  71.5 10.3 %copy-start.3 = (bf16[128,4800]{0,1:T(8,128)(2,1)S(1)}, bf16[128,4800]{0,1:T(8,128)(2,1)}, u32[]{:S(2)}) copy-start(bf16[128,4800]{0,1:T(8,128)(2,1)} %param.10) | copy-start | bytes 3686404
  81.7 1.5 copy-start.11
  85.0 6.6 %collective-permute-start.5 = (f32[16,4800]{1,0:T(8,128)S(1)}, f32[16,4800]{1,0:T(8,128)S(1)}, u32[]{:S(2)}, u32[]{:S(2)}) collective-permute-start(f32[16,4800]{1,0:T(8,128)S(1)} %slice_select_fusion), channel_id=1, source_target_pairs={{0,16},{16,0},{1,17},{17,1},{2,18},{18,2},{3,19},{19,3},{4,20},{20... | collective-permute-start | bytes 921608 | tf_op jit(solution)/shard_map/ppermute | solution.py:48
  86.9 46.6 %collective-permute-start.8 = (bf16[4800,128]{1,0:T(8,128)(2,1)}, bf16[4800,128]{1,0:T(8,128)(2,1)}, u32[]{:S(2)}, u32[]{:S(2)}) collective-permute-start(bf16[4800,128]{1,0:T(8,128)(2,1)} %collective-permute-done.b1), channel_id=1, source_target_pairs={{4,0},{5,1},{6,2},{7,3},{8,4},{9,5},{10,6},{11,7},{12,8},{13,9},{1... | collective-permute-start | bytes 3686408 | tf_op jit(solution)/shard_map/ppermute | solution.py:59
  88.9 44.6 %collective-permute-start.9 = (bf16[4800,128]{1,0:T(8,128)(2,1)}, bf16[4800,128]{1,0:T(8,128)(2,1)}, u32[]{:S(2)}, u32[]{:S(2)}) collective-permute-start(bf16[4800,128]{1,0:T(8,128)(2,1)} %collective-permute-done.b1), channel_id=1, source_target_pairs={{12,0},{13,1},{14,2},{15,3},{0,4},{1,5},{2,6},{3,7},{4,8},{5,9},{6... | collective-permute-start | bytes 3686408 | tf_op jit(solution)/shard_map/ppermute | solution.py:59
  88.9 44.6 %collective-permute-start.10 = (bf16[4800,128]{1,0:T(8,128)(2,1)}, bf16[4800,128]{1,0:T(8,128)(2,1)}, u32[]{:S(2)}, u32[]{:S(2)}) collective-permute-start(bf16[4800,128]{1,0:T(8,128)(2,1)} %collective-permute-done.1.b2), channel_id=1, source_target_pairs={{4,0},{5,1},{6,2},{7,3},{8,4},{9,5},{10,6},{11,7},{12,8},{13,9},{1... | collective-permute-start | bytes 3686408 | tf_op jit(solution)/shard_map/ppermute | solution.py:59
  91.6 41.9 %collective-permute-start.11 = (bf16[4800,128]{1,0:T(8,128)(2,1)}, bf16[4800,128]{1,0:T(8,128)(2,1)}, u32[]{:S(2)}, u32[]{:S(2)}) collective-permute-start(bf16[4800,128]{1,0:T(8,128)(2,1)} %collective-permute-done.1.b2), channel_id=1, source_target_pairs={{12,0},{13,1},{14,2},{15,3},{0,4},{1,5},{2,6},{3,7},{4,8},{5,9},{6... | collective-permute-start | bytes 3686408 | tf_op jit(solution)/shard_map/ppermute | solution.py:59
  91.6 7.3 %copy-start.7 = (bf16[4800,128]{1,0:T(8,128)(2,1)}, bf16[4800,128]{1,0:T(8,128)(2,1)S(1)}, u32[]{:S(2)}) copy-start(bf16[4800,128]{1,0:T(8,128)(2,1)S(1)} %collective-permute-done.6.b3) | copy-start | bytes 3686404
  91.6 41.9 %collective-permute-start.7 = (bf16[4800,128]{1,0:T(8,128)(2,1)}, bf16[4800,128]{1,0:T(8,128)(2,1)}, u32[]{:S(2)}, u32[]{:S(2)}) collective-permute-start(bf16[4800,128]{1,0:T(8,128)(2,1)} %collective-permute-done.2.b0), channel_id=1, source_target_pairs={{4,0},{5,1},{6,2},{7,3},{8,4},{9,5},{10,6},{11,7},{12,8},{13,9},{1... | collective-permute-start | bytes 3686408 | tf_op jit(solution)/shard_map/ppermute | solution.py:59
  95.4 37.9 %all-to-all-start.3 = ((f32[16,1,4800]{2,1,0:T(1,128)}), f32[16,1,4800]{2,1,0:T(1,128)S(1)}, u32[]{:S(2)}, u32[]{:S(2)}) async-start(f32[16,1,4800]{2,1,0:T(1,128)} %copy.52), calls=%async_computation.3 | async-start | bytes 622592 | tf_op jit(solution)/shard_map/all_to_all | solution.py:156
  98.9 2.1 copy-start.12
  133.5 31.4 %collective-permute-start.14 = (bf16[4800,128]{1,0:T(8,128)(2,1)}, bf16[4800,128]{1,0:T(8,128)(2,1)}, u32[]{:S(2)}, u32[]{:S(2)}) collective-permute-start(bf16[4800,128]{1,0:T(8,128)(2,1)} %copy-done.7), channel_id=1, source_target_pairs={{4,0},{5,1},{6,2},{7,3},{8,4},{9,5},{10,6},{11,7},{12,8},{13,9},{1... | collective-permute-start | bytes 3686408 | tf_op jit(solution)/shard_map/ppermute | solution.py:59
  137.5 50.5 %collective-permute-start.16 = (bf16[4800,128]{1,0:T(8,128)(2,1)}, bf16[4800,128]{1,0:T(8,128)(2,1)}, u32[]{:S(2)}, u32[]{:S(2)}) collective-permute-start(bf16[4800,128]{1,0:T(8,128)(2,1)} %copy-done.7), channel_id=1, source_target_pairs={{12,0},{13,1},{14,2},{15,3},{0,4},{1,5},{2,6},{3,7},{4,8},{5,9},{6... | collective-permute-start | bytes 3686408 | tf_op jit(solution)/shard_map/ppermute | solution.py:59
  138.3 12.4 %all-to-all-start.4 = ((f32[8,1,4800]{2,1,0:T(1,128)}), f32[8,1,4800]{2,1,0:T(1,128)S(1)}, u32[]{:S(2)}, u32[]{:S(2)}) async-start(f32[8,1,4800]{2,1,0:T(1,128)} %broadcast_in_dim.26), calls=%async_computation.4 | async-start | bytes 311296 | tf_op jit(solution)/shard_map/all_to_all | solution.py:44
  151.7 13.2 %all-to-all-start.5 = ((f32[16,1,4800]{2,1,0:T(1,128)}), f32[16,1,4800]{2,1,0:T(1,128)S(1)}, u32[]{:S(2)}, u32[]{:S(2)}) async-start(f32[16,1,4800]{2,1,0:T(1,128)} %broadcast_in_dim.27), calls=%async_computation.5 | async-start | bytes 622592 | tf_op jit(solution)/shard_map/all_to_all | solution.py:44
  164.9 5.8 %copy-start.4 = (bf16[128,4800]{0,1:T(8,128)(2,1)S(1)}, bf16[128,4800]{0,1:T(8,128)(2,1)}, u32[]{:S(2)}) copy-start(bf16[128,4800]{0,1:T(8,128)(2,1)} %param.10) | copy-start | bytes 3686404
  165.0 29.0 %collective-permute-start.17 = (f32[16,4800]{1,0:T(8,128)S(1)}, f32[16,4800]{1,0:T(8,128)S(1)}, u32[]{:S(2)}, u32[]{:S(2)}) collective-permute-start(f32[16,4800]{1,0:T(8,128)S(1)} %bitcast.64), channel_id=1, source_target_pairs={{0,16},{16,0},{1,17},{17,1},{2,18},{18,2},{3,19},{19,3},{4,20},{20... | collective-permute-start | bytes 921608 | tf_op jit(solution)/shard_map/ppermute | solution.py:48
  168.3 27.9 %collective-permute-start.12 = (bf16[4800,128]{1,0:T(8,128)(2,1)}, bf16[4800,128]{1,0:T(8,128)(2,1)S(1)}, u32[]{:S(2)}, u32[]{:S(2)}) collective-permute-start(bf16[4800,128]{1,0:T(8,128)(2,1)} %collective-permute-done.8.b1), channel_id=1, source_target_pairs={{4,0},{5,1},{6,2},{7,3},{8,4},{9,5},{10,6},{11,7},{12,8},{13,9},{1... | collective-permute-start | bytes 3686408 | tf_op jit(solution)/shard_map/ppermute | solution.py:59
  168.7 27.4 %collective-permute-start.13 = (bf16[4800,128]{1,0:T(8,128)(2,1)}, bf16[4800,128]{1,0:T(8,128)(2,1)S(1)}, u32[]{:S(2)}, u32[]{:S(2)}) collective-permute-start(bf16[4800,128]{1,0:T(8,128)(2,1)} %collective-permute-done.11.b2), channel_id=1, source_target_pairs={{12,0},{13,1},{14,2},{15,3},{0,4},{1,5},{2,6},{3,7},{4,8},{5,9},{6... | collective-permute-start | bytes 3686408 | tf_op jit(solution)/shard_map/ppermute | solution.py:59
  170.7 1.4 copy-start
  172.1 1.1 copy-start.2
  173.1 1.3 copy-start.8
  180.0 17.6 %collective-permute-start.15 = (bf16[4800,128]{1,0:T(8,128)(2,1)}, bf16[4800,128]{1,0:T(8,128)(2,1)S(1)}, u32[]{:S(2)}, u32[]{:S(2)}) collective-permute-start(bf16[4800,128]{1,0:T(8,128)(2,1)} %collective-permute-done.14.b3), channel_id=1, source_target_pairs={{4,0},{5,1},{6,2},{7,3},{8,4},{9,5},{10,6},{11,7},{12,8},{13,9},{1... | collective-permute-start | bytes 3686408 | tf_op jit(solution)/shard_map/ppermute | solution.py:59
  181.6 6.4 %copy-start.6 = (bf16[4800,128]{1,0:T(8,128)(2,1)S(1)}, bf16[4800,128]{1,0:T(8,128)(2,1)}, u32[]{:S(2)}) copy-start(bf16[4800,128]{1,0:T(8,128)(2,1)} %copy-done.5) | copy-start | bytes 3686404

commit v3 on v2

--- a/solution.py
+++ b/solution.py
@@ -48,22 +48,16 @@
     return lax.ppermute(x, "core", [(0, 1), (1, 0)])
 
 
-def shift(x, sizes, along_b, step):
-    nz, nc, ny, nx = sizes
-    at = lambda z, c, y, w: ((z * nc + c) * ny + y % ny) * nx + w % nx
-    perm = []
-    for z, c, y, w in np.ndindex(*sizes):
-        along_x = along_b == (c == 0)
-        src = at(z, c, y, w + step) if along_x else at(z, c, y + step, w)
-        perm.append((src, at(z, c, y, w)))
-    return lax.ppermute(x, ALL, perm)
-
-
-def products(where, pre_ref, weight_ref, b0, b1, b2, b3, mat_in, grad_in, mat_ref, grad_ref):
+def shift(x, axis, step):
+    n = lax.axis_size(axis)
+    return lax.ppermute(x, axis, [((i + step) % n, i) for i in range(n)])
+
+
+def products(where, pre_ref, weight_ref, *refs):
+    *blocks, mat_in, grad_in, mat_ref, grad_ref = refs
     grad_ref[...] = grad_in[...]
-    own = b0.shape[1]
-    blocks = (b0, b1, b2, b3)
-    spots = [pl.ds(pl.multiple_of(where[i] * own, own), own) for i in range(4)]
+    own = blocks[0].shape[1]
+    spots = [pl.ds(pl.multiple_of(where[i] * own, own), own) for i in range(len(blocks))]
     pre = jnp.concatenate([pre_ref[:, s] for s in spots], axis=1).astype(F32)
     act, pull = jax.vjp(jax.nn.gelu, pre)
     act = act.astype(BF16)
@@ -81,12 +75,13 @@
 
 def add_products(where, pre_act, weight, blocks, mat, pre_grad):
     vmem = pl.BlockSpec(memory_space=pltpu.VMEM)
+    n = len(blocks)
     return pl.pallas_call(
         products,
         out_shape=(jax.ShapeDtypeStruct(mat.shape, F32), jax.ShapeDtypeStruct(pre_grad.shape, BF16)),
-        in_specs=[pl.BlockSpec(memory_space=pltpu.SMEM)] + [vmem] * 8,
+        in_specs=[pl.BlockSpec(memory_space=pltpu.SMEM)] + [vmem] * (n + 4),
         out_specs=(vmem, vmem),
-        input_output_aliases={7: 0, 8: 1},
+        input_output_aliases={n + 3: 0, n + 4: 1},
         compiler_params=pltpu.CompilerParams(vmem_limit_bytes=40 * 2**20),
     )(where, pre_act, weight, *blocks, mat, pre_grad)
 
@@ -104,34 +99,40 @@
     core = lax.axis_index("core")
 
     got = {(0, 0): out_grad.T}
-    along_a = lambda k, step: shift(got[k], sizes, False, step)
-    along_b = lambda k, step: shift(got[k], sizes, True, step)
-
-    def tie(value, keys):
-        out = lax.optimization_barrier([value] + [got[k] for k in keys])
-        got.update(zip(keys, out[1:]))
+    iy, ix = lax.axis_index("y"), lax.axis_index("x")
+    state = [error, jnp.zeros_like(pre_act)]
+
+    def fetch(*moves):
+        new = {}
+        for key, axis, step in moves:
+            dy, dx = (key[0] + step, key[1]) if axis == "y" else (key[0], key[1] + step)
+            new[dy % ny, dx % nx] = shift(got[key[0] % ny, key[1] % nx], axis, step)
+        got.update(new)
+        return list(new)
+
+    def tie(value, keys=(), with_state=False):
+        out = lax.optimization_barrier([value, [got[k] for k in keys], state if with_state else []])
+        got.update(zip(keys, out[1]))
+        if with_state:
+            state[:] = out[2]
         return out[0]
 
-    for step in (1, -1):
-        got[0, step] = along_b((0, 0), step)
-        got[step, 0] = along_a((0, 0), step)
+    def use(keys):
+        where = jnp.stack([((iy + dy) & (ny - 1)) * nx + ((ix + dx) & (nx - 1)) for dy, dx in keys])
+        state[:] = add_products(where, pre_act, weight, [got[k] for k in keys], *state)
 
     act = gelu16(pre_act)
     q3 = jnp.concatenate(split(q_init, 3), axis=1)
     y = fold(dot(q3, out_grad, 0, 1), 3)
-    y_all = spread(y, MP).transpose(1, 0, 2).reshape(rank, toks)
+    y_all = tie(spread(y, MP), [(0, 0)])
+    one = fetch(((0, 0), "x", 1), ((0, 0), "x", -1), ((0, 0), "y", 1), ((0, 0), "y", -1))
+    y_all = y_all.transpose(1, 0, 2).reshape(rank, toks)
     y3 = jnp.concatenate(split(y_all, 3), axis=0)
     e2 = split(error, 2)
     p_err = sum(fold(dot(q3, e, 0, 1), 3) for e in e2)
     p_local = fold(dot(y3, act, 1, 1), 3) + p_err
-    p_local = tie(p_local, [(0, 1), (0, -1), (1, 0), (-1, 0)])
-    got[0, 2] = along_b((0, 1), 1)
-    got[2, 0] = along_a((1, 0), 1)
-    for db in (1, -1):
-        for da in (1, -1):
-            got[da, db] = along_a((0, db), da)
     pbar = jnp.sum(spread(p_local, "z"), axis=0)
-    pbar = (pbar + other_core(pbar)) / groups
+    pbar = tie((pbar + other_core(pbar)) / groups, one)
 
     l3 = jnp.concatenate(split(pbar, 3), axis=0)
     z_part = fold(dot(l3, act, 1, 0), 3)
@@ -145,7 +146,10 @@
         ],
         axis=1,
     )
-    took = jnp.sum(lax.all_to_all(sent, MP, 0, 0, tiled=True), axis=0)
+    took = tie(lax.all_to_all(sent, MP, 0, 0, tiled=True), one)
+    two = fetch(((0, 1), "y", 1), ((0, -1), "y", -1), ((1, 0), "x", -1), ((-1, 0), "x", 1))
+    use([(0, 0)] + one)
+    took = jnp.sum(took, axis=0)
     z = took[:rank]
     gram = jnp.concatenate(jnp.split(took[rank:], side, axis=1), axis=0)
 
@@ -153,17 +157,16 @@
     r_local = fold(dot(z3, out_grad, 1, 0), 3) + sum(fold(dot(l3, e, 1, 0), 3) for e in e2)
     low, high = r_local[:half], r_local[half:]
     keep = jnp.where(core == 0, low, high) + other_core(jnp.where(core == 0, high, low))
-    r_part = lax.all_to_all(keep.reshape(mp, half // mp, feat), MP, 0, 0, tiled=True)
-    r_part = jnp.sum(r_part, axis=0)
-    r_part = tie(r_part, [(0, 2), (2, 0), (1, 1), (-1, 1), (1, -1), (-1, -1)])
-    got[1, 2] = along_a((0, 2), 1)
-    got[-1, 2] = along_a((0, 2), -1)
-    got[2, 1] = along_a((1, 1), 1)
-    got[2, -1] = along_a((-1, -1), -1)
-    r_part = jnp.sum(spread(r_part, "z"), axis=0) / groups
-    mine = spread(r_part, MP).reshape(half, feat)
-    mine = tie(mine, [(1, 2)])
-    got[2, 2] = along_a((1, 2), 1)
+    r_part = lax.all_to_all(keep.reshape(nz, half // nz, feat), "z", 0, 0, tiled=True)
+    r_part = tie(jnp.sum(r_part, axis=0), two, True)
+    r_part = tie(spread(r_part, MP), two)
+    three = fetch(((0, 1), "x", 1), ((1, 0), "y", 1), ((1, -1), "x", -1), ((-1, 1), "y", -1))
+    use(two)
+    r_part = jnp.sum(r_part, axis=0) / groups
+    mine = tie(spread(r_part, "z"), three, True).reshape(half, feat)
+    four = fetch(((-1, 1), "x", 1), ((1, 2), "y", 1), ((-1, -1), "y", -1))
+    use(three)
+    use(four)
     theirs = other_core(mine)
     r_all = jnp.concatenate([jnp.where(core == 0, mine, theirs), jnp.where(core == 0, theirs, mine)], axis=0)
 
@@ -172,15 +175,7 @@
     q_t = jnp.dot(inv, r_all, precision=hi)
     phat = jnp.dot(inv, pbar, precision=hi)
 
-    iy, ix = lax.axis_index("y"), lax.axis_index("x")
-    ia, ib = jnp.where(core == 0, iy, ix), jnp.where(core == 0, ix, iy)
-    mat, pre_grad = error, jnp.zeros_like(pre_act)
-    for da in (0, 1, -1, 2):
-        keys = [(da, db) for db in (0, 1, -1, 2)]
-        a, b = (ia + da) & 3, (ib + jnp.array([0, 1, -1, 2])) & 3
-        where = jnp.where(core == 0, a * nx + b, b * nx + a)
-        mat, pre_grad = add_products(where, pre_act, weight, [got[k] for k in keys], mat, pre_grad)
-
+    mat, pre_grad = state
     ph, pw = split(phat, 2)
     qh, ql = split(q_t, 2)
     left = jnp.concatenate([ph, ph, pw], axis=0)

time: 209 us -> 196 us (0.938)
  waiting for transfers between devices: 70.8 us -> 37.8 us
  starting transfers between devices: 50 us -> 64.2 us
  local copies, waits for them, and re-layouts: 17.3 us -> 23.2 us
    all_to_all x2, waiting for transfers between devices: 38.8 us -> 4.3 us  [the longest x1 4.29 us: shards(): took = tie(lax.all_to_all(sent, MP, 0, 0, tiled=True), one)]
    ppermute x15, waiting for transfers between devices: 1.49 us -> 23.1 us  [shift(): return lax.ppermute(x, axis, [((i + step) % n, i) for i in range(n)])]
    all_to_all x3, waiting for transfers between devices: 30.5 us -> 9.55 us  [spread(): lax.all_to_all(jnp.broadcast_to(x, (n,) + x.shape), axis, 0, 0, tiled=True)]
    ppermute x3, starting transfers between devices: 6.88 us -> 14.7 us  [other_core(): return lax.ppermute(x, 'core', [(0, 1), (1, 0)])]
    all_to_all x3, starting transfers between devices: 15.2 us -> 21 us  [spread(): lax.all_to_all(jnp.broadcast_to(x, (n,) + x.shape), axis, 0, 0, tiled=True)]
    unnamed x33 -> x46, local copies, waits for them, and re-layouts: 12.8 us -> 17.7 us
    all_to_all x2, starting transfers between devices: 7.08 us -> 11.7 us  [the longest x1 8.18 us: shards(): lax.all_to_all(keep.reshape(nz, half // nz, feat), 'z', 0, 0, tiled=True)]
    ppermute x15, starting transfers between devices: 20.8 us -> 16.7 us  [shift(): return lax.ppermute(x, axis, [((i + step) % n, i) for i in range(n)])]
  transfers between devices with their start and end apart: 23 -> 23, of which waited for: 7 -> 12; matrix products, arithmetic and copies ran while one was open for 16% -> 12% of each run, Pallas kernels for 9% -> 10%
where the time goes in v3:
time: 196 us; the launch traced here: 195 us
  starting transfers between devices  64.2 us (33%)
  waiting for transfers between devices  37.8 us (19%)
  Pallas kernels  24.3 us (12%)
  local copies, waits for them, and re-layouts  23.2 us (12%)
  blocking collectives  17.4 us (9%)
  matrix products  13.9 us (7%)
  other arithmetic  13.1 us (7%)
    pallas_call x4, Pallas kernels, add_products(): pl.pallas_call(products, out_shape=(jax.ShapeDtypeStruct(mat.shape, F32),...  24.3 us
    ppermute x15, waiting for transfers between devices, shift(): return lax.ppermute(x, axis, [((i + step) % n, i) for i in range(n)])  23.1 us
    all_to_all x3, starting transfers between devices, spread(): lax.all_to_all(jnp.broadcast_to(x, (n,) + x.shape), axis, 0, 0, tiled=True)  21 us
    unnamed x46, local copies, waits for them, and re-layouts  17.7 us
    all_to_all x1, blocking collectives, spread(): lax.all_to_all(jnp.broadcast_to(x, (n,) + x.shape), axis, 0, 0, tiled=True)  17.4 us
    ppermute x15, starting transfers between devices, shift(): return lax.ppermute(x, axis, [((i + step) % n, i) for i in range(n)])  16.7 us
    ppermute x3, starting transfers between devices, other_core(): return lax.ppermute(x, 'core', [(0, 1), (1, 0)])  14.7 us
    dot_general x9, matrix products, dot(): lax.dot_general(a, b, (((ca,), (cb,)), ((), ())), preferred_element_type=...  11.9 us
  transfers between devices with their start and end apart: 23, of which 12 were waited for; matrix products, arithmetic and copies ran while one was open for 12% of the time, Pallas kernels for 10%

profile of v3, /device:TPU:1, one launch (start us, length us, event | category | flops | bytes accessed | tf_op | source)
XLA Modules:
  0.0 195.0 jit_solution(13681396694898060590)
XLA Ops:
  0.6 1.2 reduce-precision_convert_fusion.3
  2.6 1.9 fusion.69
  5.2 7.6 %all-to-all-start = ((f32[16,32,128]{2,1,0:T(8,128)}), f32[16,32,128]{2,1,0:T(8,128)S(1)}, u32[]{:S(2)}, u32[]{:S(2)}) async-start(f32[16,32,128]{2,1,0:T(8,128)} %broadcast_in_dim.23), calls=%async_computation | async-start | bytes 524288 | tf_op jit(solution)/shard_map/all_to_all | solution.py:44
  12.9 1.9 fusion.37
  15.7 4.6 %all-to-all-done = f32[16,32,128]{2,1,0:T(8,128)S(1)} async-done(((f32[16,32,128]{2,1,0:T(8,128)}), f32[16,32,128]{2,1,0:T(8,128)S(1)}, u32[]{:S(2)}, u32[]{:S(2)}) %all-to-all-start) | async-done | bytes 262176 | tf_op jit(solution)/shard_map/all_to_all | solution.py:44
  24.2 17.4 %all_to_all.30 = f32[8,32,150]{2,1,0:T(8,128)S(1)} all-to-all(f32[8,32,150]{2,1,0:T(8,128)S(1)} %broadcast_in_dim.24), channel_id=1, replica_groups=mesh['z'=8,'core'=2,'y'=4,'x'=4] {'z'}, dimensions={0} | all-to-all | bytes 307200 | tf_op jit(solution)/shard_map/all_to_all | solution.py:44
  41.7 4.6 %collective-permute-start = (f32[32,150]{1,0:T(8,128)S(1)}, f32[32,150]{1,0:T(8,128)S(1)}, u32[]{:S(2)}, u32[]{:S(2)}) collective-permute-start(f32[32,150]{1,0:T(8,128)S(1)} %reduce_sum.36), channel_id=1, source_target_pairs={{0,16},{16,0},{1,17},{17,1},{2,18},{18,2},{3,19},{19,3},{4,20},{20... | collective-permute-start | bytes 57608 | tf_op jit(solution)/shard_map/ppermute | solution.py:48
  47.2 1.5 collective-permute-done.2.refs_2_
  48.7 1.2 collective-permute-done.4.refs_4_
  50.7 1.7 fusion.24
  53.3 3.5 %all-to-all-start.2 = ((f32[16,40,128]{2,1,0:T(8,128)}), f32[16,40,128]{2,1,0:T(8,128)S(1)}, u32[]{:S(2)}, u32[]{:S(2)}) async-start(f32[16,40,128]{2,1,0:T(8,128)} %pad_maximum_fusion.1), calls=%async_computation.2 | async-start | bytes 655360 | tf_op jit(solution)/shard_map/all_to_all | solution.py:149
  56.9 3.6 %fusion.35 = f32[96,4800]{1,0:T(8,128)} fusion(bf16[32,150]{1,0:T(8,128)(2,1)S(1)} %get-tuple-element.106, bf16[32,150]{1,0:T(8,128)(2,1)S(1)} %get-tuple-element.107, bf16[32,150]{1,0:T(8,128)(2,1)S(1)} %get-tuple-element.105, f32[1,150,4800]{2,0,1:T(1,128)} %param.8), kind=kOutput, calls=%fused_computation.66 | convolution fusion | flops 141206400 | bytes 4752000 | tf_op jit(solution)/shard_map/dot_general | solution.py:34
  60.4 4.3 %all-to-all-done.2 = f32[16,40,128]{2,1,0:T(8,128)S(1)} async-done(((f32[16,40,128]{2,1,0:T(8,128)}), f32[16,40,128]{2,1,0:T(8,128)S(1)}, u32[]{:S(2)}, u32[]{:S(2)}) %all-to-all-start.2) | async-done | bytes 327712 | tf_op jit(solution)/shard_map/all_to_all | solution.py:149
  65.3 0.9 copy-done.12
  66.3 1.7 fusion.19
  68.0 4.8 %collective-permute-start.5 = (f32[16,4800]{1,0:T(8,128)S(1)}, f32[16,4800]{1,0:T(8,128)S(1)}, u32[]{:S(2)}, u32[]{:S(2)}) collective-permute-start(f32[16,4800]{1,0:T(8,128)S(1)} %slice_select_fusion), channel_id=1, source_target_pairs={{0,16},{16,0},{1,17},{17,1},{2,18},{18,2},{3,19},{19,3},{4,20},{20... | collective-permute-start | bytes 921608 | tf_op jit(solution)/shard_map/ppermute | solution.py:48
  74.6 2.4 %collective-permute-start.9 = (bf16[4800,128]{1,0:T(8,128)(2,1)}, bf16[4800,128]{1,0:T(8,128)(2,1)}, u32[]{:S(2)}, u32[]{:S(2)}) collective-permute-start(bf16[4800,128]{1,0:T(8,128)(2,1)} %collective-permute-done.4.refs_4_), channel_id=1, source_target_pairs={{1,0},{2,1},{3,2},{0,3},{5,4},{6,5},{7,6},{4,7},{9,8},{10,9},{11,1... | collective-permute-start | bytes 3686408 | tf_op jit(solution)/shard_map/ppermute | solution.py:53
  77.9 8.2 %all-to-all-start.3 = ((f32[8,2,4800]{2,1,0:T(2,128)}), f32[8,2,4800]{2,1,0:T(2,128)S(1)}, u32[]{:S(2)}, u32[]{:S(2)}) async-start(f32[8,2,4800]{2,1,0:T(2,128)} %reshape.30), calls=%async_computation.3 | async-start | bytes 622592 | tf_op jit(solution)/shard_map/all_to_all | solution.py:160
  86.1 2.0 %copy.70 = f32[1,150,4800]{2,1,0:T(8,128)S(1)} copy(f32[1,150,4800]{2,0,1:T(1,128)} %param.8) | data formatting | bytes 5760000
  89.2 1.4 copy-done
  90.5 1.1 copy-done.4
  91.6 1.3 copy-done.8
  92.9 7.3 %shard_map.76 = (f32[150,4800]{1,0:T(8,128)S(1)}, bf16[150,2048]{1,0:T(8,128)(2,1)}) custom-call(s32[5]{0:T(128)S(1)} %stack.69.where, bf16[150,2048]{1,0:T(8,128)(2,1)S(1)} %copy-done.4, bf16[150,4800]{1,0:T(8,128)(2,1)S(1)} %copy-done, bf16[4800,128]{1,0:T(8,128)(2,1)S(1)} %bitcast.74, ...), custom_call_target="tpu_custom_call", output_to_operand_aliasing={{0}: (8, {}), {1}: (9, {})} | custom-call | tf_op jit(solution)/shard_map/pallas_call | solution.py:79
  100.3 1.5 collective-permute-done.6.refs_0_
  101.7 1.4 collective-permute-done.7.refs_1_
  103.8 1.0 broadcast_in_dim.27
  104.8 5.3 %all-to-all-start.4 = ((f32[16,2,4800]{2,1,0:T(2,128)}), f32[16,2,4800]{2,1,0:T(2,128)}, u32[]{:S(2)}, u32[]{:S(2)}) async-start(f32[16,2,4800]{2,1,0:T(2,128)} %broadcast_in_dim.27), calls=%async_computation.4 | async-start | bytes 1245184 | tf_op jit(solution)/shard_map/all_to_all | solution.py:44
  110.3 2.5 %collective-permute-start.11 = (bf16[4800,128]{1,0:T(8,128)(2,1)}, bf16[4800,128]{1,0:T(8,128)(2,1)}, u32[]{:S(2)}, u32[]{:S(2)}) collective-permute-start(bf16[4800,128]{1,0:T(8,128)(2,1)} %collective-permute-done.1.refs_1_), channel_id=1, source_target_pairs={{1,0},{2,1},{3,2},{0,3},{5,4},{6,5},{7,6},{4,7},{9,8},{10,9},{11,1... | collective-permute-start | bytes 3686408 | tf_op jit(solution)/shard_map/ppermute | solution.py:53
  112.8 2.4 %collective-permute-start.12 = (bf16[4800,128]{1,0:T(8,128)(2,1)}, bf16[4800,128]{1,0:T(8,128)(2,1)}, u32[]{:S(2)}, u32[]{:S(2)}) collective-permute-start(bf16[4800,128]{1,0:T(8,128)(2,1)} %collective-permute-done.3.refs_3_), channel_id=1, source_target_pairs={{4,0},{8,4},{12,8},{0,12},{5,1},{9,5},{13,9},{1,13},{6,2},{10,6},{... | collective-permute-start | bytes 3686408 | tf_op jit(solution)/shard_map/ppermute | solution.py:53
  115.7 4.9 %all-to-all-done.4 = f32[16,2,4800]{2,1,0:T(2,128)} async-done(((f32[16,2,4800]{2,1,0:T(2,128)}), f32[16,2,4800]{2,1,0:T(2,128)}, u32[]{:S(2)}, u32[]{:S(2)}) %all-to-all-start.4) | async-done | bytes 614432 | tf_op jit(solution)/shard_map/all_to_all | solution.py:44
  121.0 1.3 reduce_sum.39
  123.1 8.2 %all-to-all-start.5 = ((f32[8,2,4800]{2,1,0:T(2,128)}), f32[8,2,4800]{2,1,0:T(2,128)S(1)}, u32[]{:S(2)}, u32[]{:S(2)}) async-start(f32[8,2,4800]{2,1,0:T(2,128)} %broadcast_in_dim.28), calls=%async_computation.5 | async-start | bytes 622592 | tf_op jit(solution)/shard_map/all_to_all | solution.py:44
  131.4 2.9 %cholesky.17 = f32[32,32]{1,0:T(8,128)S(1)} custom-call(f32[32,32]{1,0:T(8,128)S(1)} %fusion.61), custom_call_target="Cholesky" | custom-call | tf_op jit(solution)/shard_map/jit(cholesky)/cholesky | solution.py:173
  135.6 2.4 %custom-call.7 = f32[1,32,32]{1,2,0:T(8,128)S(1)} custom-call(f32[1,32,32]{2,1,0:T(8,128)S(1)} %fusion.56), custom_call_target="InvertDiagBlocksLowerTriangular" | custom-call | tf_op jit(solution)/shard_map/jit(_solve_triangular)/triangular_solve | solution.py:174
  138.1 1.4 copy-done.1
  139.5 1.1 copy-done.5
  140.6 6.3 %shard_map.77 = (f32[150,4800]{1,0:T(8,128)S(1)}, bf16[150,2048]{1,0:T(8,128)(2,1)}) custom-call(s32[4]{0:T(128)S(1)} %pad_add_fusion.1.where, bf16[150,2048]{1,0:T(8,128)(2,1)S(1)} %copy-done.5, bf16[150,4800]{1,0:T(8,128)(2,1)S(1)} %copy-done.1, bf16[4800,128]{1,0:T(8,128)(2,1)} %collective-permute-done.6.refs_0_, ...), custom_call_target="tpu_custom_call", output_to_operand_aliasing={{0}: (7, {}), {1}: (8, {})} | custom-call | tf_op jit(solution)/shard_map/pallas_call | solution.py:79
  148.6 5.3 %collective-permute-start.17 = (f32[16,4800]{1,0:T(8,128)}, f32[16,4800]{1,0:T(8,128)S(1)}, u32[]{:S(2)}, u32[]{:S(2)}) collective-permute-start(f32[16,4800]{1,0:T(8,128)} %reshape.31), channel_id=1, source_target_pairs={{0,16},{16,0},{1,17},{17,1},{2,18},{18,2},{3,19},{19,3},{4,20},{20... | collective-permute-start | bytes 921608 | tf_op jit(solution)/shard_map/ppermute | solution.py:48
  154.3 1.6 collective-permute-start.10
  155.9 2.7 %collective-permute-start.15 = (bf16[4800,128]{1,0:T(8,128)(2,1)}, bf16[4800,128]{1,0:T(8,128)(2,1)S(1)}, u32[]{:S(2)}, u32[]{:S(2)}) collective-permute-start(bf16[4800,128]{1,0:T(8,128)(2,1)} %collective-permute-done.13.refs_2_), channel_id=1, source_target_pairs={{4,0},{8,4},{12,8},{0,12},{5,1},{9,5},{13,9},{1,13},{6,2},{10,6},{... | collective-permute-start | bytes 3686408 | tf_op jit(solution)/shard_map/ppermute | solution.py:53
  158.6 1.4 copy-done.2
  159.9 1.1 copy-done.6
  161.0 6.4 %shard_map.78 = (f32[150,4800]{1,0:T(8,128)S(1)}, bf16[150,2048]{1,0:T(8,128)(2,1)}) custom-call(s32[4]{0:T(128)S(1)} %pad_add_fusion.2.where, bf16[150,2048]{1,0:T(8,128)(2,1)S(1)} %copy-done.6, bf16[150,4800]{1,0:T(8,128)(2,1)S(1)} %copy-done.2, bf16[4800,128]{1,0:T(8,128)(2,1)} %collective-permute-done.11.refs_0_, ...), custom_call_target="tpu_custom_call", output_to_operand_aliasing={{0}: (7, {}), {1}: (8, {})} | custom-call | tf_op jit(solution)/shard_map/pallas_call | solution.py:79
  167.4 1.5 fusion.17
  169.5 13.9 %collective-permute-done.10.refs_0_ = bf16[4800,128]{1,0:T(8,128)(2,1)S(1)} collective-permute-done((bf16[4800,128]{1,0:T(8,128)(2,1)}, bf16[4800,128]{1,0:T(8,128)(2,1)S(1)}, u32[]{:S(2)}, u32[]{:S(2)}) %collective-permute-start.10) | collective-permute-done | bytes 1228832 | tf_op jit(solution)/shard_map/ppermute | solution.py:53
  183.4 2.2 %collective-permute-done.16.refs_2_ = bf16[4800,128]{1,0:T(8,128)(2,1)S(1)} collective-permute-done((bf16[4800,128]{1,0:T(8,128)(2,1)}, bf16[4800,128]{1,0:T(8,128)(2,1)S(1)}, u32[]{:S(2)}, u32[]{:S(2)}) %collective-permute-start.16) | collective-permute-done | bytes 1228832 | tf_op jit(solution)/shard_map/ppermute | solution.py:53
  185.6 4.4 %shard_map.79 = (f32[150,4800]{1,0:T(8,128)S(1)}, bf16[150,2048]{1,0:T(8,128)(2,1)}) custom-call(s32[3]{0:T(128)S(1)} %pad_add_fusion.where, bf16[150,2048]{1,0:T(8,128)(2,1)S(1)} %copy-done.6, bf16[150,4800]{1,0:T(8,128)(2,1)S(1)} %copy-done.2, bf16[4800,128]{1,0:T(8,128)(2,1)S(1)} %collective-permute-done.10.refs_0_, ...), custom_call_target="tpu_custom_call", output_to_operand_aliasing={{0}: (6, {}), {1}: (7, {})} | custom-call | tf_op jit(solution)/shard_map/pallas_call | solution.py:79
  190.4 4.6 %copy.41 = f32[1,150,4800]{2,0,1:T(1,128)} copy(f32[1,150,4800]{2,1,0:T(8,128)S(1)} %subtract_bitcast_fusion) | data formatting | bytes 5760000
  (105 shorter events, 20.4 us)
Async XLA Ops:
  1.8 0.7 copy-start.14
  1.8 2.6 %copy-start.16 = (bf16[4800,32]{0,1:T(8,128)(2,1)}, bf16[4800,32]{0,1:T(8,128)(2,1)S(1)}, u32[]{:S(2)}) copy-start(bf16[4800,32]{0,1:T(8,128)(2,1)S(1)} %get-tuple-element.98) | copy-start | bytes 921604
  1.9 2.6 %copy-start.18 = (bf16[4800,32]{0,1:T(8,128)(2,1)}, bf16[4800,32]{0,1:T(8,128)(2,1)S(1)}, u32[]{:S(2)}) copy-start(bf16[4800,32]{0,1:T(8,128)(2,1)S(1)} %get-tuple-element.99) | copy-start | bytes 921604
  2.6 10.2 %copy-start.9 = (f32[1,150,4800]{2,0,1:T(1,128)S(1)}, f32[1,150,4800]{2,0,1:T(1,128)}, u32[]{:S(2)}) copy-start(f32[1,150,4800]{2,0,1:T(1,128)} %param.8) | copy-start | bytes 8640004
  5.2 15.1 %all-to-all-start = ((f32[16,32,128]{2,1,0:T(8,128)}), f32[16,32,128]{2,1,0:T(8,128)S(1)}, u32[]{:S(2)}, u32[]{:S(2)}) async-start(f32[16,32,128]{2,1,0:T(8,128)} %broadcast_in_dim.23), calls=%async_computation | async-start | bytes 524288 | tf_op jit(solution)/shard_map/all_to_all | solution.py:44
  12.8 2.1 %copy-start.10 = (f32[1,150,4800]{2,0,1:T(1,128)S(1)}, f32[1,150,4800]{2,0,1:T(1,128)}, u32[]{:S(2)}) copy-start(f32[1,150,4800]{2,0,1:T(1,128)} %param.8) | copy-start | bytes 8640004
  12.8 2.1 %copy-start.15 = (bf16[4800,32]{0,1:T(8,128)(2,1)S(1)}, bf16[4800,32]{0,1:T(8,128)(2,1)}, u32[]{:S(2)}) copy-start(bf16[4800,32]{0,1:T(8,128)(2,1)} %copy-done.14) | copy-start | bytes 921604
  12.8 2.2 %copy-start.17 = (bf16[4800,32]{0,1:T(8,128)(2,1)S(1)}, bf16[4800,32]{0,1:T(8,128)(2,1)}, u32[]{:S(2)}) copy-start(bf16[4800,32]{0,1:T(8,128)(2,1)} %copy-done.16) | copy-start | bytes 921604
  12.8 2.3 %copy-start.19 = (bf16[4800,32]{0,1:T(8,128)(2,1)S(1)}, bf16[4800,32]{0,1:T(8,128)(2,1)}, u32[]{:S(2)}) copy-start(bf16[4800,32]{0,1:T(8,128)(2,1)} %copy-done.18) | copy-start | bytes 921604
  15.1 5.2 %copy-start.7 = (bf16[128,4800]{0,1:T(8,128)(2,1)S(1)}, bf16[128,4800]{0,1:T(8,128)(2,1)}, u32[]{:S(2)}) copy-start(bf16[128,4800]{0,1:T(8,128)(2,1)} %param.6) | copy-start | bytes 3686404
  15.1 8.2 %copy-start.3 = (bf16[150,2048]{1,0:T(8,128)(2,1)S(1)}, bf16[150,2048]{1,0:T(8,128)(2,1)}, u32[]{:S(2)}) copy-start(bf16[150,2048]{1,0:T(8,128)(2,1)} %pre_ref.7) | copy-start | bytes 1843204
  20.3 26.9 %collective-permute-start.1 = (bf16[4800,128]{1,0:T(8,128)(2,1)S(1)}, bf16[4800,128]{1,0:T(8,128)(2,1)}, u32[]{:S(2)}, u32[]{:S(2)}) collective-permute-start(bf16[4800,128]{1,0:T(8,128)(2,1)S(1)} %bitcast.70), channel_id=1, source_target_pairs={{1,0},{2,1},{3,2},{0,3},{5,4},{6,5},{7,6},{4,7},{9,8},{10,9},{11,1... | collective-permute-start | bytes 3686408 | tf_op jit(solution)/shard_map/ppermute | solution.py:53
  21.0 27.7 %collective-permute-start.2 = (bf16[4800,128]{1,0:T(8,128)(2,1)S(1)}, bf16[4800,128]{1,0:T(8,128)(2,1)}, u32[]{:S(2)}, u32[]{:S(2)}) collective-permute-start(bf16[4800,128]{1,0:T(8,128)(2,1)S(1)} %bitcast.71), channel_id=1, source_target_pairs={{3,0},{0,1},{1,2},{2,3},{7,4},{4,5},{5,6},{6,7},{11,8},{8,9},{9,10... | collective-permute-start | bytes 3686408 | tf_op jit(solution)/shard_map/ppermute | solution.py:53
  21.8 26.9 %collective-permute-start.3 = (bf16[4800,128]{1,0:T(8,128)(2,1)S(1)}, bf16[4800,128]{1,0:T(8,128)(2,1)}, u32[]{:S(2)}, u32[]{:S(2)}) collective-permute-start(bf16[4800,128]{1,0:T(8,128)(2,1)S(1)} %bitcast.72), channel_id=1, source_target_pairs={{4,0},{8,4},{12,8},{0,12},{5,1},{9,5},{13,9},{1,13},{6,2},{10,6},{... | collective-permute-start | bytes 3686408 | tf_op jit(solution)/shard_map/ppermute | solution.py:53
  22.7 27.2 %collective-permute-start.4 = (bf16[4800,128]{1,0:T(8,128)(2,1)S(1)}, bf16[4800,128]{1,0:T(8,128)(2,1)}, u32[]{:S(2)}, u32[]{:S(2)}) collective-permute-start(bf16[4800,128]{1,0:T(8,128)(2,1)S(1)} %bitcast.73), channel_id=1, source_target_pairs={{12,0},{0,4},{4,8},{8,12},{13,1},{1,5},{5,9},{9,13},{14,2},{2,6},{... | collective-permute-start | bytes 3686408 | tf_op jit(solution)/shard_map/ppermute | solution.py:53
  41.7 5.5 %collective-permute-start = (f32[32,150]{1,0:T(8,128)S(1)}, f32[32,150]{1,0:T(8,128)S(1)}, u32[]{:S(2)}, u32[]{:S(2)}) collective-permute-start(f32[32,150]{1,0:T(8,128)S(1)} %reduce_sum.36), channel_id=1, source_target_pairs={{0,16},{16,0},{1,17},{17,1},{2,18},{18,2},{3,19},{19,3},{4,20},{20... | collective-permute-start | bytes 57608 | tf_op jit(solution)/shard_map/ppermute | solution.py:48
  47.2 3.5 %copy-start.11 = (f32[1,150,4800]{2,0,1:T(1,128)S(1)}, f32[1,150,4800]{2,0,1:T(1,128)}, u32[]{:S(2)}) copy-start(f32[1,150,4800]{2,0,1:T(1,128)} %param.8) | copy-start | bytes 8640004
  53.3 11.4 %all-to-all-start.2 = ((f32[16,40,128]{2,1,0:T(8,128)}), f32[16,40,128]{2,1,0:T(8,128)S(1)}, u32[]{:S(2)}, u32[]{:S(2)}) async-start(f32[16,40,128]{2,1,0:T(8,128)} %pad_maximum_fusion.1), calls=%async_computation.2 | async-start | bytes 655360 | tf_op jit(solution)/shard_map/all_to_all | solution.py:149
  64.8 1.5 copy-start.12
  68.0 9.0 %collective-permute-start.5 = (f32[16,4800]{1,0:T(8,128)S(1)}, f32[16,4800]{1,0:T(8,128)S(1)}, u32[]{:S(2)}, u32[]{:S(2)}) collective-permute-start(f32[16,4800]{1,0:T(8,128)S(1)} %slice_select_fusion), channel_id=1, source_target_pairs={{0,16},{16,0},{1,17},{17,1},{2,18},{18,2},{3,19},{19,3},{4,20},{20... | collective-permute-start | bytes 921608 | tf_op jit(solution)/shard_map/ppermute | solution.py:48
  72.8 28.9 %collective-permute-start.6 = (bf16[4800,128]{1,0:T(8,128)(2,1)}, bf16[4800,128]{1,0:T(8,128)(2,1)}, u32[]{:S(2)}, u32[]{:S(2)}) collective-permute-start(bf16[4800,128]{1,0:T(8,128)(2,1)} %collective-permute-done.1.refs_1_), channel_id=1, source_target_pairs={{4,0},{8,4},{12,8},{0,12},{5,1},{9,5},{13,9},{1,13},{6,2},{10,6},{... | collective-permute-start | bytes 3686408 | tf_op jit(solution)/shard_map/ppermute | solution.py:53
  73.4 29.8 %collective-permute-start.7 = (bf16[4800,128]{1,0:T(8,128)(2,1)}, bf16[4800,128]{1,0:T(8,128)(2,1)}, u32[]{:S(2)}, u32[]{:S(2)}) collective-permute-start(bf16[4800,128]{1,0:T(8,128)(2,1)} %collective-permute-done.2.refs_2_), channel_id=1, source_target_pairs={{12,0},{0,4},{4,8},{8,12},{13,1},{1,5},{5,9},{9,13},{14,2},{2,6},{... | collective-permute-start | bytes 3686408 | tf_op jit(solution)/shard_map/ppermute | solution.py:53
  74.3 29.5 %collective-permute-start.8 = (bf16[4800,128]{1,0:T(8,128)(2,1)}, bf16[4800,128]{1,0:T(8,128)(2,1)}, u32[]{:S(2)}, u32[]{:S(2)}) collective-permute-start(bf16[4800,128]{1,0:T(8,128)(2,1)} %collective-permute-done.3.refs_3_), channel_id=1, source_target_pairs={{3,0},{0,1},{1,2},{2,3},{7,4},{4,5},{5,6},{6,7},{11,8},{8,9},{9,10... | collective-permute-start | bytes 3686408 | tf_op jit(solution)/shard_map/ppermute | solution.py:53
  74.6 29.2 %collective-permute-start.9 = (bf16[4800,128]{1,0:T(8,128)(2,1)}, bf16[4800,128]{1,0:T(8,128)(2,1)}, u32[]{:S(2)}, u32[]{:S(2)}) collective-permute-start(bf16[4800,128]{1,0:T(8,128)(2,1)} %collective-permute-done.4.refs_4_), channel_id=1, source_target_pairs={{1,0},{2,1},{3,2},{0,3},{5,4},{6,5},{7,6},{4,7},{9,8},{10,9},{11,1... | collective-permute-start | bytes 3686408 | tf_op jit(solution)/shard_map/ppermute | solution.py:53
  77.9 22.2 %all-to-all-start.3 = ((f32[8,2,4800]{2,1,0:T(2,128)}), f32[8,2,4800]{2,1,0:T(2,128)S(1)}, u32[]{:S(2)}, u32[]{:S(2)}) async-start(f32[8,2,4800]{2,1,0:T(2,128)} %reshape.30), calls=%async_computation.3 | async-start | bytes 622592 | tf_op jit(solution)/shard_map/all_to_all | solution.py:160
  89.2 1.4 copy-start
  90.5 1.1 copy-start.4
  91.6 1.3 copy-start.8
  104.8 15.9 %all-to-all-start.4 = ((f32[16,2,4800]{2,1,0:T(2,128)}), f32[16,2,4800]{2,1,0:T(2,128)}, u32[]{:S(2)}, u32[]{:S(2)}) async-start(f32[16,2,4800]{2,1,0:T(2,128)} %broadcast_in_dim.27), calls=%async_computation.4 | async-start | bytes 1245184 | tf_op jit(solution)/shard_map/all_to_all | solution.py:44
  110.3 36.6 %collective-permute-start.11 = (bf16[4800,128]{1,0:T(8,128)(2,1)}, bf16[4800,128]{1,0:T(8,128)(2,1)}, u32[]{:S(2)}, u32[]{:S(2)}) collective-permute-start(bf16[4800,128]{1,0:T(8,128)(2,1)} %collective-permute-done.1.refs_1_), channel_id=1, source_target_pairs={{1,0},{2,1},{3,2},{0,3},{5,4},{6,5},{7,6},{4,7},{9,8},{10,9},{11,1... | collective-permute-start | bytes 3686408 | tf_op jit(solution)/shard_map/ppermute | solution.py:53
  112.8 34.1 %collective-permute-start.12 = (bf16[4800,128]{1,0:T(8,128)(2,1)}, bf16[4800,128]{1,0:T(8,128)(2,1)}, u32[]{:S(2)}, u32[]{:S(2)}) collective-permute-start(bf16[4800,128]{1,0:T(8,128)(2,1)} %collective-permute-done.3.refs_3_), channel_id=1, source_target_pairs={{4,0},{8,4},{12,8},{0,12},{5,1},{9,5},{13,9},{1,13},{6,2},{10,6},{... | collective-permute-start | bytes 3686408 | tf_op jit(solution)/shard_map/ppermute | solution.py:53
  120.6 27.0 %collective-permute-start.13 = (bf16[4800,128]{1,0:T(8,128)(2,1)}, bf16[4800,128]{1,0:T(8,128)(2,1)}, u32[]{:S(2)}, u32[]{:S(2)}) collective-permute-start(bf16[4800,128]{1,0:T(8,128)(2,1)} %collective-permute-done.8.refs_2_), channel_id=1, source_target_pairs={{3,0},{0,1},{1,2},{2,3},{7,4},{4,5},{5,6},{6,7},{11,8},{8,9},{9,10... | collective-permute-start | bytes 3686408 | tf_op jit(solution)/shard_map/ppermute | solution.py:53
  121.0 26.7 %collective-permute-start.14 = (bf16[4800,128]{1,0:T(8,128)(2,1)}, bf16[4800,128]{1,0:T(8,128)(2,1)}, u32[]{:S(2)}, u32[]{:S(2)}) collective-permute-start(bf16[4800,128]{1,0:T(8,128)(2,1)} %collective-permute-done.9.refs_3_), channel_id=1, source_target_pairs={{12,0},{0,4},{4,8},{8,12},{13,1},{1,5},{5,9},{9,13},{14,2},{2,6},{... | collective-permute-start | bytes 3686408 | tf_op jit(solution)/shard_map/ppermute | solution.py:53
  123.1 23.8 %all-to-all-start.5 = ((f32[8,2,4800]{2,1,0:T(2,128)}), f32[8,2,4800]{2,1,0:T(2,128)S(1)}, u32[]{:S(2)}, u32[]{:S(2)}) async-start(f32[8,2,4800]{2,1,0:T(2,128)} %broadcast_in_dim.28), calls=%async_computation.5 | async-start | bytes 622592 | tf_op jit(solution)/shard_map/all_to_all | solution.py:44
  138.1 1.4 copy-start.1
  139.5 1.1 copy-start.5
  148.6 18.8 %collective-permute-start.17 = (f32[16,4800]{1,0:T(8,128)}, f32[16,4800]{1,0:T(8,128)S(1)}, u32[]{:S(2)}, u32[]{:S(2)}) collective-permute-start(f32[16,4800]{1,0:T(8,128)} %reshape.31), channel_id=1, source_target_pairs={{0,16},{16,0},{1,17},{17,1},{2,18},{18,2},{3,19},{19,3},{4,20},{20... | collective-permute-start | bytes 921608 | tf_op jit(solution)/shard_map/ppermute | solution.py:48
  154.3 29.2 %collective-permute-start.10 = (bf16[4800,128]{1,0:T(8,128)(2,1)}, bf16[4800,128]{1,0:T(8,128)(2,1)S(1)}, u32[]{:S(2)}, u32[]{:S(2)}) collective-permute-start(bf16[4800,128]{1,0:T(8,128)(2,1)} %collective-permute-done.9.refs_3_), channel_id=1, source_target_pairs={{1,0},{2,1},{3,2},{0,3},{5,4},{6,5},{7,6},{4,7},{9,8},{10,9},{11,1... | collective-permute-start | bytes 3686408 | tf_op jit(solution)/shard_map/ppermute | solution.py:53
  155.9 29.8 %collective-permute-start.16 = (bf16[4800,128]{1,0:T(8,128)(2,1)}, bf16[4800,128]{1,0:T(8,128)(2,1)S(1)}, u32[]{:S(2)}, u32[]{:S(2)}) collective-permute-start(bf16[4800,128]{1,0:T(8,128)(2,1)} %collective-permute-done.7.refs_1_), channel_id=1, source_target_pairs={{12,0},{0,4},{4,8},{8,12},{13,1},{1,5},{5,9},{9,13},{14,2},{2,6},{... | collective-permute-start | bytes 3686408 | tf_op jit(solution)/shard_map/ppermute | solution.py:53
  155.9 29.8 %collective-permute-start.15 = (bf16[4800,128]{1,0:T(8,128)(2,1)}, bf16[4800,128]{1,0:T(8,128)(2,1)S(1)}, u32[]{:S(2)}, u32[]{:S(2)}) collective-permute-start(bf16[4800,128]{1,0:T(8,128)(2,1)} %collective-permute-done.13.refs_2_), channel_id=1, source_target_pairs={{4,0},{8,4},{12,8},{0,12},{5,1},{9,5},{13,9},{1,13},{6,2},{10,6},{... | collective-permute-start | bytes 3686408 | tf_op jit(solution)/shard_map/ppermute | solution.py:53
  158.6 1.4 copy-start.2
  159.9 1.1 copy-start.6
  161.0 6.4 %copy-start.13 = (f32[16,4800]{1,0:T(8,128)S(1)}, f32[16,4800]{1,0:T(8,128)}, u32[]{:S(2)}) copy-start(f32[16,4800]{1,0:T(8,128)} %reshape.31) | copy-start | bytes 921604

commit v4 on v3

v4 whole, which is shorter than its diff:
```python
import functools

import jax
import jax.numpy as jnp
from jax import lax
from jax.experimental import pallas as pl
from jax.experimental.pallas import tpu as pltpu
from jax.sharding import Mesh, PartitionSpec as P

F32 = jnp.float32
BF16 = jnp.bfloat16
MP = ("y", "x")
ALL = ("z", "core", "y", "x")


def gelu_back(pre, grad):
    _, pull = jax.vjp(jax.nn.gelu, pre)
    return pull(grad)[0]


def gelu16(pre):
    return jax.nn.gelu(pre.astype(F32)).astype(BF16)


def split(x, parts):
    out = []
    for _ in range(parts):
        top = lax.reduce_precision(x, 8, 7)
        out.append(top.astype(BF16))
        x = x - top
    return out


def dot(a, b, ca, cb):
    return lax.dot_general(a, b, (((ca,), (cb,)), ((), ())), preferred_element_type=F32)


def fold(x, parts, axis=0):
    n = x.shape[axis] // parts
    return sum(lax.slice_in_dim(x, i * n, (i + 1) * n, axis=axis) for i in range(parts))


def spread(x, axis):
    n = lax.axis_size(axis)
    return lax.all_to_all(jnp.broadcast_to(x, (n,) + x.shape), axis, 0, 0, tiled=True)


def other_core(x):
    return lax.ppermute(x, "core", [(0, 1), (1, 0)])


def shift(x, axis, step):
    n = lax.axis_size(axis)
    return lax.ppermute(x, axis, [((i + step) % n, i) for i in range(n)])


def partner(x):
    return lax.ppermute(x, "x", [(i, i ^ 1) for i in range(lax.axis_size("x"))])


def peer(x):
    n = lax.axis_size("x")
    return lax.ppermute(x, "x", [(i, n - 1 - i) for i in range(n)])


def products(n, first, last, where, pre_a, pre_b, w_a, w_b, *refs):
    refs = list(refs)
    blocks = [[refs.pop(0) for _ in range(k)] for k in n]
    total = None if first else refs.pop(0)
    keep_ref, send_ref, *outs = refs
    own = blocks[0][0].shape[1]
    rows, feat = w_a.shape
    spots = [pl.ds(pl.multiple_of(where[i] * own, own), own) for i in range(len(blocks))]
    pre = [jnp.concatenate([p[:, s] for s in spots], axis=1) for p in (pre_a, pre_b)]
    act = gelu16(jnp.concatenate(pre, axis=0))
    back = jnp.zeros(act.shape, F32)
    edges, at = [], 0
    for ref in blocks[0]:
        edges.append(at)
        at += ref.shape[0]
    for k, edge in enumerate(edges):
        size = blocks[0][k].shape[0]
        for lo in range(0, size, 512):
            here = slice(lo, min(size, lo + 512))
            part = slice(edge + here.start, edge + here.stop)
            piece = jnp.concatenate([b[k][here, :] for b in blocks], axis=1)
            left = jnp.concatenate([w_a[:, part], w_b[:, part]], axis=0)
            back = back + dot(left, piece, 1, 0)
            more = dot(act, piece, 1, 1)
            if total is not None:
                more = more + total[:, part]
            if last:
                outs[0][:, part] = more[:rows]
                outs[1][:, part] = more[rows:].astype(BF16)
            else:
                outs[0][:, part] = more
    keep_ref[...] = back[:rows]
    send_ref[...] = back[rows:].astype(BF16)


def add_products(where, pre, weight, blocks, total, last=False):
    vmem = pl.BlockSpec(memory_space=pltpu.VMEM)
    rows, feat = weight[0].shape
    toks = sum(b[0].shape[1] for b in blocks)
    flat = [x for b in blocks for x in b] + ([] if total is None else [total])
    shape = jax.ShapeDtypeStruct
    out = [shape((rows, toks), F32), shape((rows, toks), BF16)]
    if last:
        out += [shape((rows, feat), F32), shape((rows, feat), BF16)]
    else:
        out += [shape((2 * rows, feat), F32)]
    return pl.pallas_call(
        functools.partial(products, [len(b) for b in blocks], total is None, last),
        out_shape=out,
        in_specs=[pl.BlockSpec(memory_space=pltpu.SMEM)] + [vmem] * (4 + len(flat)),
        out_specs=[vmem] * len(out),
        compiler_params=pltpu.CompilerParams(vmem_limit_bytes=40 * 2**20),
    )(where, *pre, *weight, *flat)


def grads(counts, own, where, pre_ref, *refs):
    *halves, out_ref = refs
    k = 0
    for n, keep, came in zip(counts, halves[::2], halves[1::2]):
        for i in range(n):
            s = pl.ds(pl.multiple_of(where[k] * own, own), own)
            back = keep[:, i * own:(i + 1) * own] + came[:, i * own:(i + 1) * own].astype(F32)
            out = gelu_back(pre_ref[:, s].astype(F32), back).astype(BF16)
            out_ref[:, s] = out[:out_ref.shape[0]]
            k += 1


def pre_grads(where, pre, rows, own, halves):
    vmem = pl.BlockSpec(memory_space=pltpu.VMEM)
    counts = [a.shape[1] // own for a, _ in halves]
    return pl.pallas_call(
        functools.partial(grads, counts, own),
        out_shape=jax.ShapeDtypeStruct((rows, pre.shape[1]), BF16),
        in_specs=[pl.BlockSpec(memory_space=pltpu.SMEM)] + [vmem] * (1 + 2 * len(halves)),
        out_specs=vmem,
        compiler_params=pltpu.CompilerParams(vmem_limit_bytes=40 * 2**20),
    )(where, pre, *[x for pair in halves for x in pair])


def finish(side, own_ref, came_ref, error_ref, left_ref, right_ref, out_ref):
    rows, feat = error_ref.shape
    width = own_ref.shape[1]
    start = feat - width
    first = side[0] == 0
    left = left_ref[...]
    for base, top, turn in ((0, start, True), (start, feat, False)):
        for lo in range(base, top, 512):
            part = slice(lo, min(top, lo + 512))
            at = slice(part.start - base, part.stop - base)
            mine, came = own_ref[:, at], came_ref[:, at].astype(F32)
            grad = jnp.where(first, mine, came) if turn else jnp.where(first, came, mine)
            out_ref[:, part] = grad[:rows] + error_ref[:, part] - dot(left, right_ref[:, part], 1, 0)


def new_errors(side, own, came, error, left, right):
    vmem = pl.BlockSpec(memory_space=pltpu.VMEM)
    return pl.pallas_call(
        finish,
        out_shape=jax.ShapeDtypeStruct(error.shape, F32),
        in_specs=[pl.BlockSpec(memory_space=pltpu.SMEM)] + [vmem] * 5,
        out_specs=vmem,
        compiler_params=pltpu.CompilerParams(vmem_limit_bytes=40 * 2**20),
    )(side, own, came, error, left, right)


def tie(*values):
    return lax.optimization_barrier(values)


def shards(sizes, pre_act, out_grad, weight, error, q_init):
    hi = lax.Precision.HIGHEST
    nz, nc, ny, nx = sizes
    groups = nz * nc
    mp = ny * nx
    rank = q_init.shape[1]
    half = rank // 2
    hid, toks = pre_act.shape
    own, feat = out_grad.shape
    error = error[0]
    core = lax.axis_index("core")

    iy, ix = lax.axis_index("y"), lax.axis_index("x")

    side = (ix ^ (ix >> 1)) & 1
    start = feat // 256 * 128
    width = feat - start
    rows = -(-hid // 16) * 16
    og = out_grad.T
    og_give = jnp.where(side == 0, og[start:], og[:width])
    og_mine = jnp.where(side == 0, og[:width], og[start:])
    og_came = partner(og_give)
    below = jnp.where((ix & 1) == 0, og_mine, og_came)
    above = jnp.where((ix & 1) == 0, og_came, og_mine)
    block = jnp.concatenate([below, above], axis=1)
    pair = 2 * own
    pre_pad = jnp.pad(pre_act, ((0, rows - hid), (0, 0)))
    w_pad = jnp.pad(weight, ((0, rows - hid), (0, 0)))
    w_first, w_last = w_pad[:, :width], w_pad[:, start:]
    w_last = jnp.where(jnp.arange(width) < width - start, jnp.zeros_like(w_last), w_last)
    w_mine = jnp.where(side == 0, w_first, w_last)
    w_give = jnp.where(side == 0, w_last, w_first)

    def spot(keys):
        return jnp.stack([((iy + dy) & (ny - 1)) * (nx // 2) + ((ix >> 1) ^ j) for j, dy in keys])

    act = gelu16(pre_act)
    q3 = jnp.concatenate(split(q_init, 3), axis=1)
    y = fold(dot(q3, out_grad, 0, 1), 3)
    y_all, block, pre_pad, w_give = tie(spread(y, MP), block, pre_pad, w_give)
    up, down, over = shift(block, "y", 1), shift(block, "y", -1), peer(block)
    pre_two = (pre_pad, partner(pre_pad))
    w_two = (w_mine, partner(w_give))
    y_all = y_all.transpose(1, 0, 2).reshape(rank, toks)
    y3 = jnp.concatenate(split(y_all, 3), axis=0)
    e2 = split(error, 2)
    p_err = sum(fold(dot(q3, e, 0, 1), 3) for e in e2)
    p_local = fold(dot(y3, act, 1, 1), 3) + p_err
    pbar = jnp.sum(spread(p_local, "z"), axis=0)
    pbar, up, down, over = tie((pbar + other_core(pbar)) / groups, up, down, over)

    l3 = jnp.concatenate(split(pbar, 3), axis=0)
    z_part = fold(dot(l3, act, 1, 0), 3)
    gram_part = jnp.dot(pbar, pbar.T, precision=hi)
    quarter = 128 // rank
    flat = jnp.concatenate(jnp.split(gram_part, quarter, axis=0), axis=1)
    sent = jnp.concatenate(
        [
            z_part.reshape(rank, mp, own).transpose(1, 0, 2),
            jnp.broadcast_to(flat, (mp,) + flat.shape),
        ],
        axis=1,
    )
    took, up, down, over = tie(lax.all_to_all(sent, MP, 0, 0, tiled=True), up, down, over)
    far, over_up, over_down = shift(up, "y", 1), peer(up), shift(over, "y", -1)
    keys = [[(0, 0), (0, 1), (0, -1), (1, 0)], [(0, 2), (1, 1), (1, -1)], [(1, 2)]]
    places = [spot(k) for k in keys]
    keep_1, send_1, total = add_products(places[0], pre_two, w_two, [[block], [up], [down], [over]], None)
    took = jnp.sum(took, axis=0)
    z = took[:rank]
    gram = jnp.concatenate(jnp.split(took[rank:], quarter, axis=1), axis=0)

    z3 = jnp.concatenate(split(z, 3), axis=0)
    r_local = fold(dot(z3, out_grad, 1, 0), 3) + sum(fold(dot(l3, e, 1, 0), 3) for e in e2)
    low, high = r_local[:half], r_local[half:]
    keep = jnp.where(core == 0, low, high) + other_core(jnp.where(core == 0, high, low))
    r_part = lax.all_to_all(keep.reshape(nz, half // nz, feat), "z", 0, 0, tiled=True)
    r_part, far, over_up, over_down, total = tie(jnp.sum(r_part, axis=0), far, over_up, over_down, total)
    came_1 = partner(send_1)
    r_part, far, over_up, over_down = tie(spread(r_part, MP), far, over_up, over_down)
    cut = (width // 3 + 64) // 128 * 128
    last = [
        peer(far[:cut]),
        shift(over_up[cut:2 * cut], "y", 1),
        shift(over_down[2 * cut:], "y", -1),
    ]
    keep_2, send_2, total = add_products(places[1], pre_two, w_two, [[far], [over_up], [over_down]], total)
    r_part = jnp.sum(r_part, axis=0) / groups
    mine, total, *last = tie(spread(r_part, "z"), total, *last)
    mine = mine.reshape(half, feat)
    came_2 = partner(send_2)
    keep_3, send_3, grad_mine, grad_give = add_products(places[2], pre_two, w_two, [last], total, True)
    grad_came = partner(grad_give)
    came_3 = partner(send_3)
    halves = [(keep_1, came_1), (keep_2, came_2), (keep_3, came_3)]
    pre_grad = pre_grads(jnp.concatenate(places), pre_pad, hid, pair, halves)
    theirs = other_core(mine)
    r_all = jnp.concatenate([jnp.where(core == 0, mine, theirs), jnp.where(core == 0, theirs, mine)], axis=0)

    lower = jnp.linalg.cholesky(gram)
    inv = jax.scipy.linalg.solve_triangular(lower, jnp.eye(rank, dtype=F32), lower=True)
    q_t = jnp.dot(inv, r_all, precision=hi)
    phat = jnp.dot(inv, pbar, precision=hi)

    ph, pw = split(phat, 2)
    qh, ql = split(q_t, 2)
    left = jnp.concatenate([ph, ph, pw], axis=0).T
    right = jnp.concatenate([qh, ql, qh], axis=0)
    new_error = new_errors(side.reshape(1), grad_mine, grad_came, error, left, right)[None]
    return (pre_grad, new_error, q_t.T)


def solution(mesh):
    sizes = (mesh.shape["replica"] // 2, 2, 4, mesh.shape["mp"] // 4)
    grid = Mesh(mesh.devices.reshape(sizes), ALL)

    def run(*args):
        return shards(sizes, *args)

    return jax.shard_map(
        run,
        mesh=grid,
        in_specs=(
            P(MP, ("z", "core")),
            P(ALL, None),
            P(MP, None),
            P(("z", "core"), MP, None),
            P(),
        ),
        out_specs=(P(MP, ("z", "core")), P(("z", "core"), MP, None), P()),
        check_vma=False,
    )
```

time: 196 us -> 213 us (1.087)
  waiting for transfers between devices: 37.8 us -> 54.6 us
  starting transfers between devices: 64.2 us -> 53.7 us
  local copies, waits for them, and re-layouts: 23.2 us -> 31.1 us
  other arithmetic: 13.1 us -> 19.8 us
  Pallas kernels: 24.3 us -> 18.1 us
  matrix products: 13.9 us -> 16.1 us
    ppermute x0 -> x10, waiting for transfers between devices: none -> 33.6 us  [the longest x7 32.8 us: partner(): return lax.ppermute(x, 'x', [(i, i ^ 1) for i in range(lax.axis_size('x'))])]
    ppermute x15 -> x6, waiting for transfers between devices: 23.1 us -> 3.8 us  [shift(): return lax.ppermute(x, axis, [((i + step) % n, i) for i in range(n)])]
    ppermute x15 -> x6, starting transfers between devices: 16.7 us -> 4.4 us  [shift(): return lax.ppermute(x, axis, [((i + step) % n, i) for i in range(n)])]
    ppermute x0 -> x10, starting transfers between devices: none -> 6.9 us  [the longest x7 6.62 us: partner(): return lax.ppermute(x, 'x', [(i, i ^ 1) for i in range(lax.axis_size('x'))])]
    select_n x0 -> x3, other arithmetic: none -> 6.86 us  [the longest x1 3.36 us: shards(): w_mine = jnp.where(side == 0, w_first, w_last)]
    pallas_call x4 -> x5, Pallas kernels: 24.3 us -> 18.1 us  [the longest x3 14.3 us: add_products(): pl.pallas_call(functools.partial(products, [len(b) for b in blocks], tota...]
    slice x0 -> x3, local copies, waits for them, and re-layouts: none -> 5.4 us  [the longest x1 1.81 us: shards(): far[:cut]]
    ppermute x3, starting transfers between devices: 14.7 us -> 11.8 us  [other_core(): return lax.ppermute(x, 'core', [(0, 1), (1, 0)])]
  transfers between devices with their start and end apart: 23 -> 24, of which waited for: 12 -> 11; matrix products, arithmetic and copies ran while one was open for 12% -> 19% of each run, Pallas kernels for 10% -> 8%
where the time goes in v4:
time: 213 us; the launch traced here: 212 us
  waiting for transfers between devices  54.6 us (26%)
  starting transfers between devices  53.7 us (25%)
  local copies, waits for them, and re-layouts  31.1 us (15%)
  other arithmetic  19.8 us (9%)
  Pallas kernels  18.1 us (8%)
  blocking collectives  17.4 us (8%)
  matrix products  16.1 us (8%)
    ppermute x7, waiting for transfers between devices, partner(): return lax.ppermute(x, 'x', [(i, i ^ 1) for i in range(lax.axis_size('x'))])  32.8 us
    unnamed x44, local copies, waits for them, and re-layouts  19.1 us
    all_to_all x3, starting transfers between devices, spread(): lax.all_to_all(jnp.broadcast_to(x, (n,) + x.shape), axis, 0, 0, tiled=True)  18.9 us
    all_to_all x1, blocking collectives, spread(): lax.all_to_all(jnp.broadcast_to(x, (n,) + x.shape), axis, 0, 0, tiled=True)  17.4 us
    pallas_call x3, Pallas kernels, add_products(): pl.pallas_call(functools.partial(products, [len(b) for b in blocks], tota...  14.3 us
    dot_general x8, matrix products, dot(): lax.dot_general(a, b, (((ca,), (cb,)), ((), ())), preferred_element_type=...  14.1 us
    all_to_all x3, waiting for transfers between devices, spread(): lax.all_to_all(jnp.broadcast_to(x, (n,) + x.shape), axis, 0, 0, tiled=True)  12 us
    ppermute x3, starting transfers between devices, other_core(): return lax.ppermute(x, 'core', [(0, 1), (1, 0)])  11.8 us
  transfers between devices with their start and end apart: 24, of which 11 were waited for; matrix products, arithmetic and copies ran while one was open for 19% of the time, Pallas kernels for 8%

profile of v4, /device:TPU:1, one launch (start us, length us, event | category | flops | bytes accessed | tf_op | source)
XLA Modules:
  0.0 212.0 jit_solution(16992495631397388345)
XLA Ops:
  0.7 2.3 %broadcast_select_fusion.2 = bf16[2496,128]{1,0:T(8,128)(2,1)} fusion(pred[]{:T(512)S(6)} %eq.7, bf16[4800,128]{1,0:T(8,128)(2,1)} %bitcast.65), kind=kLoop, calls=%fused_computation.29 | loop fusion | flops 319488 | bytes 1916929 | tf_op jit(solution)/shard_map/jit(_where)/select_n | solution.py:194
  3.0 2.0 collective-permute-start
  6.4 6.5 %all-to-all-start = ((f32[16,32,128]{2,1,0:T(8,128)}), f32[16,32,128]{2,1,0:T(8,128)S(1)}, u32[]{:S(2)}, u32[]{:S(2)}) async-start(f32[16,32,128]{2,1,0:T(8,128)} %broadcast_in_dim.27), calls=%async_computation | async-start | bytes 524288 | tf_op jit(solution)/shard_map/all_to_all | solution.py:45
  12.9 2.5 %fusion.20 = f32[96,150]{0,1:T(8,128)S(1)} fusion(bf16[4800,32]{0,1:T(8,128)(2,1)S(1)} %get-tuple-element.99, bf16[4800,32]{0,1:T(8,128)(2,1)S(1)} %get-tuple-element.100, bf16[4800,32]{0,1:T(8,128)(2,1)S(1)} %get-tuple-element.98, f32[1,150,4800]{2,0,1:T(1,128)} %param.8), kind=kOutput, calls=%fused_computation.50 | convolution fusion | flops 142444800 | bytes 3859200 | tf_op jit(solution)/shard_map/dot_general | solution.py:35
  15.6 1.7 fusion.32
  17.4 3.4 %broadcast_select_fusion = (bf16[160,2496]{1,0:T(8,128)(2,1)S(1)}, bf16[160,2496]{1,0:T(8,128)(2,1)}) fusion(pred[]{:T(512)S(6)} %eq.7, bf16[150,4800]{1,0:T(8,128)(2,1)} %param.7, pred[2496]{0:T(1024)(128)(4,1)S(1)} %iota_compare_fusion.3), kind=kLoop, calls=%fused_computation.27 | loop fusion | flops 1597440 | bytes 3039937 | tf_op jit(solution)/shard_map/jit(_where)/select_n | solution.py:205
  22.1 4.6 %all-to-all-done = f32[16,32,128]{2,1,0:T(8,128)S(1)} async-done(((f32[16,32,128]{2,1,0:T(8,128)}), f32[16,32,128]{2,1,0:T(8,128)S(1)}, u32[]{:S(2)}, u32[]{:S(2)}) %all-to-all-start) | async-done | bytes 262176 | tf_op jit(solution)/shard_map/all_to_all | solution.py:45
  28.2 1.7 fusion.21
  30.2 17.4 %all_to_all.30 = f32[8,32,150]{2,1,0:T(8,128)S(1)} all-to-all(f32[8,32,150]{2,1,0:T(8,128)S(1)} %broadcast_in_dim.30), channel_id=1, replica_groups=mesh['z'=8,'core'=2,'y'=4,'x'=4] {'z'}, dimensions={0} | all-to-all | bytes 307200 | tf_op jit(solution)/shard_map/all_to_all | solution.py:45
  47.6 3.9 %collective-permute-start.3 = (f32[32,150]{1,0:T(8,128)S(1)}, f32[32,150]{1,0:T(8,128)S(1)}, u32[]{:S(2)}, u32[]{:S(2)}) collective-permute-start(f32[32,150]{1,0:T(8,128)S(1)} %reduce_sum.36), channel_id=1, source_target_pairs={{0,16},{16,0},{1,17},{17,1},{2,18},{18,2},{3,19},{19,3},{4,20},{20... | collective-permute-start | bytes 57608 | tf_op jit(solution)/shard_map/ppermute | solution.py:49
  52.4 2.4 %collective-permute-done.4.refs_1_ = bf16[2496,256]{1,0:T(8,128)(2,1)} collective-permute-done((bf16[2496,256]{1,0:T(8,128)(2,1)S(1)}, bf16[2496,256]{1,0:T(8,128)(2,1)}, u32[]{:S(2)}, u32[]{:S(2)}) %collective-permute-start.4) | collective-permute-done | bytes 1277984 | tf_op jit(solution)/shard_map/ppermute | solution.py:54
  54.8 1.4 collective-permute-done.5.refs_2_
  57.2 1.9 fusion.53
  59.2 1.8 fusion.19
  61.8 3.5 %all-to-all-start.2 = ((f32[16,40,128]{2,1,0:T(8,128)}), f32[16,40,128]{2,1,0:T(8,128)S(1)}, u32[]{:S(2)}, u32[]{:S(2)}) async-start(f32[16,40,128]{2,1,0:T(8,128)} %pad_maximum_fusion.3), calls=%async_computation.2 | async-start | bytes 655360 | tf_op jit(solution)/shard_map/all_to_all | solution.py:238
  65.4 3.7 %fusion.30 = f32[96,4800]{1,0:T(8,128)} fusion(bf16[32,150]{1,0:T(8,128)(2,1)S(1)} %get-tuple-element.107, bf16[32,150]{1,0:T(8,128)(2,1)S(1)} %get-tuple-element.108, bf16[32,150]{1,0:T(8,128)(2,1)S(1)} %get-tuple-element.106, f32[1,150,4800]{2,0,1:T(1,128)} %param.8), kind=kOutput, calls=%fused_computation.70 | convolution fusion | flops 141206400 | bytes 4752000 | tf_op jit(solution)/shard_map/dot_general | solution.py:35
  69.0 4.4 %all-to-all-done.2 = f32[16,40,128]{2,1,0:T(8,128)S(1)} async-done(((f32[16,40,128]{2,1,0:T(8,128)}), f32[16,40,128]{2,1,0:T(8,128)S(1)}, u32[]{:S(2)}, u32[]{:S(2)}) %all-to-all-start.2) | async-done | bytes 327712 | tf_op jit(solution)/shard_map/all_to_all | solution.py:238
  74.9 1.8 fusion.14
  76.8 4.1 %collective-permute-start.8 = (f32[16,4800]{1,0:T(8,128)S(1)}, f32[16,4800]{1,0:T(8,128)S(1)}, u32[]{:S(2)}, u32[]{:S(2)}) collective-permute-start(f32[16,4800]{1,0:T(8,128)S(1)} %slice_select_fusion), channel_id=1, source_target_pairs={{0,16},{16,0},{1,17},{17,1},{2,18},{18,2},{3,19},{19,3},{4,20},{20... | collective-permute-start | bytes 921608 | tf_op jit(solution)/shard_map/ppermute | solution.py:49
  85.0 8.2 %all-to-all-start.3 = ((f32[8,2,4800]{2,1,0:T(2,128)}), f32[8,2,4800]{2,1,0:T(2,128)S(1)}, u32[]{:S(2)}, u32[]{:S(2)}) async-start(f32[8,2,4800]{2,1,0:T(2,128)} %reshape.33), calls=%async_computation.3 | async-start | bytes 622592 | tf_op jit(solution)/shard_map/all_to_all | solution.py:251
  93.2 3.7 %copy.83 = f32[1,150,4800]{2,1,0:T(8,128)} copy(f32[1,150,4800]{2,0,1:T(1,128)} %param.8) | data formatting | bytes 5760000
  97.2 17.6 %collective-permute-done.2.w_b = bf16[160,2496]{1,0:T(8,128)(2,1)S(1)} collective-permute-done((bf16[160,2496]{1,0:T(8,128)(2,1)}, bf16[160,2496]{1,0:T(8,128)(2,1)S(1)}, u32[]{:S(2)}, u32[]{:S(2)}) %collective-permute-start.2) | collective-permute-done | bytes 798752 | tf_op jit(solution)/shard_map/ppermute | solution.py:58
  114.8 1.3 copy-done.2
  116.1 6.2 %shard_map.76 = (f32[160,1024]{1,0:T(8,128)S(1)}, bf16[160,1024]{1,0:T(8,128)(2,1)}, f32[320,2496]{1,0:T(8,128)S(1)}) custom-call(s32[4]{0:T(128)S(1)} %pad_add_fusion.where, bf16[160,2048]{1,0:T(8,128)(2,1)S(1)} %pad.8.pre_a.pre_ref, bf16[160,2048]{1,0:T(8,128)(2,1)S(1)} %collective-permute-done.1.pre_b, bf16[160,2496]{1,0:T(8,128)(2,1)S(1)} %get-tuple-element.92.w_a, ...), custom_call_target="tpu_custom_call" | custom-call | tf_op jit(solution)/shard_map/pallas_call | solution.py:112
  122.3 1.7 copy-done.3
  125.9 4.3 %all-to-all-start.4 = ((f32[16,2,4800]{2,1,0:T(2,128)}), f32[16,2,4800]{2,1,0:T(2,128)}, u32[]{:S(2)}, u32[]{:S(2)}) async-start(f32[16,2,4800]{2,1,0:T(2,128)} %broadcast_in_dim.32), calls=%async_computation.4 | async-start | bytes 1245184 | tf_op jit(solution)/shard_map/all_to_all | solution.py:45
  130.8 2.9 %cholesky.17 = f32[32,32]{1,0:T(8,128)S(1)} custom-call(f32[32,32]{1,0:T(8,128)S(1)} %fusion.49), custom_call_target="Cholesky" | custom-call | tf_op jit(solution)/shard_map/jit(cholesky)/cholesky | solution.py:274
  134.5 7.4 %all-to-all-done.4 = f32[16,2,4800]{2,1,0:T(2,128)} async-done(((f32[16,2,4800]{2,1,0:T(2,128)}), f32[16,2,4800]{2,1,0:T(2,128)}, u32[]{:S(2)}, u32[]{:S(2)}) %all-to-all-start.4) | async-done | bytes 614432 | tf_op jit(solution)/shard_map/all_to_all | solution.py:45
  141.8 1.8 slice.152
  143.7 1.8 slice.153
  145.5 1.5 collective-permute-start.14
  146.9 1.3 reduce_sum.39
  149.0 8.2 %all-to-all-start.5 = ((f32[8,2,4800]{2,1,0:T(2,128)}), f32[8,2,4800]{2,1,0:T(2,128)}, u32[]{:S(2)}, u32[]{:S(2)}) async-start(f32[8,2,4800]{2,1,0:T(2,128)} %broadcast_in_dim.33), calls=%async_computation.5 | async-start | bytes 622592 | tf_op jit(solution)/shard_map/all_to_all | solution.py:45
  157.9 2.4 %custom-call.7 = f32[1,32,32]{1,2,0:T(8,128)S(1)} custom-call(f32[1,32,32]{2,1,0:T(8,128)S(1)} %fusion.44), custom_call_target="InvertDiagBlocksLowerTriangular" | custom-call | tf_op jit(solution)/shard_map/jit(_solve_triangular)/triangular_solve | solution.py:275
  160.4 1.8 slice.154
  164.4 1.9 copy-done.4
  166.3 5.6 %shard_map.77 = (f32[160,768]{1,0:T(8,128)S(1)}, bf16[160,768]{1,0:T(8,128)(2,1)}, f32[320,2496]{1,0:T(8,128)S(1)}) custom-call(s32[3]{0:T(128)S(1)} %pad_add_fusion.1.where, bf16[160,2048]{1,0:T(8,128)(2,1)S(1)} %pad.8.pre_a.pre_ref, bf16[160,2048]{1,0:T(8,128)(2,1)S(1)} %collective-permute-done.1.pre_b, bf16[160,2496]{1,0:T(8,128)(2,1)S(1)} %get-tuple-element.92.w_a, ...), custom_call_target="tpu_custom_call" | custom-call | tf_op jit(solution)/shard_map/pallas_call | solution.py:112
  172.0 1.7 copy-done.5
  174.1 1.9 reshape.35
  176.0 3.8 %collective-permute-start.18 = (f32[16,4800]{1,0:T(8,128)}, f32[16,4800]{1,0:T(8,128)S(1)}, u32[]{:S(2)}, u32[]{:S(2)}) collective-permute-start(f32[16,4800]{1,0:T(8,128)} %reshape.35), channel_id=1, source_target_pairs={{0,16},{16,0},{1,17},{17,1},{2,18},{18,2},{3,19},{19,3},{4,20},{20... | collective-permute-start | bytes 921608 | tf_op jit(solution)/shard_map/ppermute | solution.py:49
  180.7 1.9 copy-done.6
  182.6 2.5 %shard_map.78 = (f32[160,256]{1,0:T(8,128)S(1)}, bf16[160,256]{1,0:T(8,128)(2,1)S(1)}, f32[160,2496]{1,0:T(8,128)S(1)}, bf16[160,2496]{1,0:T(8,128)(2,1)S(1)}) custom-call(s32[1]{0:T(128)} %bitcast.7.where, bf16[160,2048]{1,0:T(8,128)(2,1)S(1)} %pad.8.pre_a.pre_ref, bf16[160,2048]{1,0:T(8,128)(2,1)S(1)} %collective-permute-done.1.pre_b, ...), custom_call_target="tpu_custom_call" | custom-call | tf_op jit(solution)/shard_map/pallas_call | solution.py:112
  185.3 1.5 collective-permute-start.17
  186.8 2.4 %collective-permute-done.16.refs_5_ = bf16[160,256]{1,0:T(8,128)(2,1)S(1)} collective-permute-done((bf16[160,256]{1,0:T(8,128)(2,1)S(1)}, bf16[160,256]{1,0:T(8,128)(2,1)S(1)}, u32[]{:S(2)}, u32[]{:S(2)}) %collective-permute-start.16) | collective-permute-done | bytes 81952 | tf_op jit(solution)/shard_map/ppermute | solution.py:58
  189.2 3.2 %shard_map.79 = bf16[150,2048]{1,0:T(8,128)(2,1)} custom-call(s32[8]{0:T(128)S(1)} %concatenate.37.where, bf16[160,2048]{1,0:T(8,128)(2,1)S(1)} %pad.8.pre_a.pre_ref, f32[160,1024]{1,0:T(8,128)S(1)} %copy-done.8, bf16[160,1024]{1,0:T(8,128)(2,1)} %collective-permute-done.7.refs_1_, f32[160,768]{1,0:T(8,128)S(1)} %get-tuple-element.62.refs_2_, ...), custom_call_target="tpu_custom_call" | custom-call | tf_op jit(solution)/shard_map/pallas_call | solution.py:136
  192.5 1.5 fusion.12
  194.1 12.7 %collective-permute-done.17.came_ref = bf16[160,2496]{1,0:T(8,128)(2,1)S(1)} collective-permute-done((bf16[160,2496]{1,0:T(8,128)(2,1)S(1)}, bf16[160,2496]{1,0:T(8,128)(2,1)S(1)}, u32[]{:S(2)}, u32[]{:S(2)}) %collective-permute-start.17) | collective-permute-done | bytes 798752 | tf_op jit(solution)/shard_map/ppermute | solution.py:58
  207.4 4.6 %copy.54 = f32[1,150,4800]{2,0,1:T(1,128)} copy(f32[1,150,4800]{2,1,0:T(8,128)S(1)} %bitcast.64) | data formatting | bytes 5760000
  (116 shorter events, 23.0 us)
Async XLA Ops:
  0.6 4.4 %copy-start.15 = (f32[4800,32]{0,1:T(8,128)S(1)}, f32[4800,32]{0,1:T(8,128)}, u32[]{:S(2)}) copy-start(f32[4800,32]{0,1:T(8,128)} %param.9) | copy-start | bytes 1843204
  0.7 4.5 %copy-start.11 = (bf16[128,4800]{0,1:T(8,128)(2,1)S(1)}, bf16[128,4800]{0,1:T(8,128)(2,1)}, u32[]{:S(2)}) copy-start(bf16[128,4800]{0,1:T(8,128)(2,1)} %param.6) | copy-start | bytes 3686404
  3.0 17.7 %collective-permute-start = (bf16[2496,128]{1,0:T(8,128)(2,1)}, bf16[2496,128]{1,0:T(8,128)(2,1)}, u32[]{:S(2)}, u32[]{:S(2)}) collective-permute-start(bf16[2496,128]{1,0:T(8,128)(2,1)} %broadcast_select_fusion.2), channel_id=1, source_target_pairs={{0,1},{1,0},{2,3},{3,2},{4,5},{5,4},{6,7},{7,6},{8,9},{9,8},{10,11... | collective-permute-start | bytes 1916936 | tf_op jit(solution)/shard_map/ppermute | solution.py:58
  5.1 7.7 %copy-start.17 = (bf16[4800,32]{0,1:T(8,128)(2,1)}, bf16[4800,32]{0,1:T(8,128)(2,1)S(1)}, u32[]{:S(2)}) copy-start(bf16[4800,32]{0,1:T(8,128)(2,1)S(1)} %get-tuple-element.99) | copy-start | bytes 921604
  5.1 7.7 %copy-start.18 = (bf16[4800,32]{0,1:T(8,128)(2,1)}, bf16[4800,32]{0,1:T(8,128)(2,1)S(1)}, u32[]{:S(2)}) copy-start(bf16[4800,32]{0,1:T(8,128)(2,1)S(1)} %get-tuple-element.100) | copy-start | bytes 921604
  6.4 20.4 %all-to-all-start = ((f32[16,32,128]{2,1,0:T(8,128)}), f32[16,32,128]{2,1,0:T(8,128)S(1)}, u32[]{:S(2)}, u32[]{:S(2)}) async-start(f32[16,32,128]{2,1,0:T(8,128)} %broadcast_in_dim.27), calls=%async_computation | async-start | bytes 524288 | tf_op jit(solution)/shard_map/all_to_all | solution.py:45
  12.9 2.7 %copy-start.9 = (f32[1,150,4800]{2,0,1:T(1,128)S(1)}, f32[1,150,4800]{2,0,1:T(1,128)}, u32[]{:S(2)}) copy-start(f32[1,150,4800]{2,0,1:T(1,128)} %param.8) | copy-start | bytes 8640004
  15.6 1.7 copy-start.16
  22.1 7.8 %copy-start.1 = (bf16[2496,256]{1,0:T(8,128)(2,1)}, bf16[2496,256]{1,0:T(8,128)(2,1)S(1)}, u32[]{:S(2)}) copy-start(bf16[2496,256]{1,0:T(8,128)(2,1)S(1)} %pad_maximum_fusion.refs_0_) | copy-start | bytes 3833860
  26.7 28.1 %collective-permute-start.4 = (bf16[2496,256]{1,0:T(8,128)(2,1)S(1)}, bf16[2496,256]{1,0:T(8,128)(2,1)}, u32[]{:S(2)}, u32[]{:S(2)}) collective-permute-start(bf16[2496,256]{1,0:T(8,128)(2,1)S(1)} %pad_maximum_fusion.refs_0_), channel_id=1, source_target_pairs={{4,0},{8,4},{12,8},{0,12},{5,1},{9,5},{13,9},{1,13},{6,2},{10,6},{... | collective-permute-start | bytes 3833864 | tf_op jit(solution)/shard_map/ppermute | solution.py:54
  27.2 29.1 %collective-permute-start.5 = (bf16[2496,256]{1,0:T(8,128)(2,1)S(1)}, bf16[2496,256]{1,0:T(8,128)(2,1)}, u32[]{:S(2)}, u32[]{:S(2)}) collective-permute-start(bf16[2496,256]{1,0:T(8,128)(2,1)S(1)} %pad_maximum_fusion.refs_0_), channel_id=1, source_target_pairs={{12,0},{0,4},{4,8},{8,12},{13,1},{1,5},{5,9},{9,13},{14,2},{2,6},{... | collective-permute-start | bytes 3833864 | tf_op jit(solution)/shard_map/ppermute | solution.py:54
  28.2 28.8 %collective-permute-start.6 = (bf16[2496,256]{1,0:T(8,128)(2,1)S(1)}, bf16[2496,256]{1,0:T(8,128)(2,1)}, u32[]{:S(2)}, u32[]{:S(2)}) collective-permute-start(bf16[2496,256]{1,0:T(8,128)(2,1)S(1)} %pad_maximum_fusion.refs_0_), channel_id=1, source_target_pairs={{0,3},{1,2},{2,1},{3,0},{4,7},{5,6},{6,5},{7,4},{8,11},{9,10},{10,... | collective-permute-start | bytes 3833864 | tf_op jit(solution)/shard_map/ppermute | solution.py:63
  47.6 4.8 %collective-permute-start.3 = (f32[32,150]{1,0:T(8,128)S(1)}, f32[32,150]{1,0:T(8,128)S(1)}, u32[]{:S(2)}, u32[]{:S(2)}) collective-permute-start(f32[32,150]{1,0:T(8,128)S(1)} %reduce_sum.36), channel_id=1, source_target_pairs={{0,16},{16,0},{1,17},{17,1},{2,18},{18,2},{3,19},{19,3},{4,20},{20... | collective-permute-start | bytes 57608 | tf_op jit(solution)/shard_map/ppermute | solution.py:49
  57.1 2.0 copy-start.10
  61.8 11.6 %all-to-all-start.2 = ((f32[16,40,128]{2,1,0:T(8,128)}), f32[16,40,128]{2,1,0:T(8,128)S(1)}, u32[]{:S(2)}, u32[]{:S(2)}) async-start(f32[16,40,128]{2,1,0:T(8,128)} %pad_maximum_fusion.3), calls=%async_computation.2 | async-start | bytes 655360 | tf_op jit(solution)/shard_map/all_to_all | solution.py:238
  65.4 8.1 %copy-start.12 = (bf16[128,4800]{0,1:T(8,128)(2,1)S(1)}, bf16[128,4800]{0,1:T(8,128)(2,1)}, u32[]{:S(2)}) copy-start(bf16[128,4800]{0,1:T(8,128)(2,1)} %param.6) | copy-start | bytes 3686404
  73.4 1.5 copy-start.13
  76.8 6.7 %collective-permute-start.8 = (f32[16,4800]{1,0:T(8,128)S(1)}, f32[16,4800]{1,0:T(8,128)S(1)}, u32[]{:S(2)}, u32[]{:S(2)}) collective-permute-start(f32[16,4800]{1,0:T(8,128)S(1)} %slice_select_fusion), channel_id=1, source_target_pairs={{0,16},{16,0},{1,17},{17,1},{2,18},{18,2},{3,19},{19,3},{4,20},{20... | collective-permute-start | bytes 921608 | tf_op jit(solution)/shard_map/ppermute | solution.py:49
  80.8 16.4 %collective-permute-start.1 = (bf16[160,2048]{1,0:T(8,128)(2,1)S(1)}, bf16[160,2048]{1,0:T(8,128)(2,1)S(1)}, u32[]{:S(2)}, u32[]{:S(2)}) collective-permute-start(bf16[160,2048]{1,0:T(8,128)(2,1)S(1)} %pad.8.pre_a.pre_ref), channel_id=1, source_target_pairs={{0,1},{1,0},{2,3},{3,2},{4,5},{5,4},{6,7},{7,6},{8,9},{9,8},{10,11... | collective-permute-start | bytes 1966088 | tf_op jit(solution)/shard_map/ppermute | solution.py:58
  81.1 33.6 %collective-permute-start.2 = (bf16[160,2496]{1,0:T(8,128)(2,1)}, bf16[160,2496]{1,0:T(8,128)(2,1)S(1)}, u32[]{:S(2)}, u32[]{:S(2)}) collective-permute-start(bf16[160,2496]{1,0:T(8,128)(2,1)} %get-tuple-element.40), channel_id=1, source_target_pairs={{0,1},{1,0},{2,3},{3,2},{4,5},{5,4},{6,7},{7,6},{8,9},{9,8},{10,11... | collective-permute-start | bytes 2396168 | tf_op jit(solution)/shard_map/ppermute | solution.py:58
  82.3 42.6 %collective-permute-start.10 = (bf16[2496,256]{1,0:T(8,128)(2,1)}, bf16[2496,256]{1,0:T(8,128)(2,1)}, u32[]{:S(2)}, u32[]{:S(2)}) collective-permute-start(bf16[2496,256]{1,0:T(8,128)(2,1)} %collective-permute-done.4.refs_1_), channel_id=1, source_target_pairs={{0,3},{1,2},{2,1},{3,0},{4,7},{5,6},{6,5},{7,4},{8,11},{9,10},{10,... | collective-permute-start | bytes 3833864 | tf_op jit(solution)/shard_map/ppermute | solution.py:63
  82.6 42.3 %collective-permute-start.9 = (bf16[2496,256]{1,0:T(8,128)(2,1)}, bf16[2496,256]{1,0:T(8,128)(2,1)}, u32[]{:S(2)}, u32[]{:S(2)}) collective-permute-start(bf16[2496,256]{1,0:T(8,128)(2,1)} %collective-permute-done.4.refs_1_), channel_id=1, source_target_pairs={{4,0},{8,4},{12,8},{0,12},{5,1},{9,5},{13,9},{1,13},{6,2},{10,6},{... | collective-permute-start | bytes 3833864 | tf_op jit(solution)/shard_map/ppermute | solution.py:54
  83.5 41.4 %collective-permute-start.11 = (bf16[2496,256]{1,0:T(8,128)(2,1)}, bf16[2496,256]{1,0:T(8,128)(2,1)}, u32[]{:S(2)}, u32[]{:S(2)}) collective-permute-start(bf16[2496,256]{1,0:T(8,128)(2,1)} %collective-permute-done.6.refs_3_), channel_id=1, source_target_pairs={{12,0},{0,4},{4,8},{8,12},{13,1},{1,5},{5,9},{9,13},{14,2},{2,6},{... | collective-permute-start | bytes 3833864 | tf_op jit(solution)/shard_map/ppermute | solution.py:54
  85.0 39.8 %all-to-all-start.3 = ((f32[8,2,4800]{2,1,0:T(2,128)}), f32[8,2,4800]{2,1,0:T(2,128)S(1)}, u32[]{:S(2)}, u32[]{:S(2)}) async-start(f32[8,2,4800]{2,1,0:T(2,128)} %reshape.33), calls=%async_computation.3 | async-start | bytes 622592 | tf_op jit(solution)/shard_map/all_to_all | solution.py:251
  114.8 1.3 copy-start.2
  122.3 1.7 copy-start.3
  123.9 0.8 copy-start.7
  125.9 15.9 %all-to-all-start.4 = ((f32[16,2,4800]{2,1,0:T(2,128)}), f32[16,2,4800]{2,1,0:T(2,128)}, u32[]{:S(2)}, u32[]{:S(2)}) async-start(f32[16,2,4800]{2,1,0:T(2,128)} %broadcast_in_dim.32), calls=%async_computation.4 | async-start | bytes 1245184 | tf_op jit(solution)/shard_map/all_to_all | solution.py:45
  143.7 30.4 %collective-permute-start.13 = (bf16[896,256]{1,0:T(8,128)(2,1)}, bf16[896,256]{1,0:T(8,128)(2,1)}, u32[]{:S(2)}, u32[]{:S(2)}) collective-permute-start(bf16[896,256]{1,0:T(8,128)(2,1)} %slice.152), channel_id=1, source_target_pairs={{0,3},{1,2},{2,1},{3,0},{4,7},{5,6},{6,5},{7,4},{8,11},{9,10},{10,... | collective-permute-start | bytes 1376264 | tf_op jit(solution)/shard_map/ppermute | solution.py:63
  145.5 28.6 %collective-permute-start.14 = (bf16[896,256]{1,0:T(8,128)(2,1)}, bf16[896,256]{1,0:T(8,128)(2,1)}, u32[]{:S(2)}, u32[]{:S(2)}) collective-permute-start(bf16[896,256]{1,0:T(8,128)(2,1)} %slice.153), channel_id=1, source_target_pairs={{4,0},{8,4},{12,8},{0,12},{5,1},{9,5},{13,9},{1,13},{6,2},{10,6},{... | collective-permute-start | bytes 1376264 | tf_op jit(solution)/shard_map/ppermute | solution.py:54
  149.0 25.0 %all-to-all-start.5 = ((f32[8,2,4800]{2,1,0:T(2,128)}), f32[8,2,4800]{2,1,0:T(2,128)}, u32[]{:S(2)}, u32[]{:S(2)}) async-start(f32[8,2,4800]{2,1,0:T(2,128)} %broadcast_in_dim.33), calls=%async_computation.5 | async-start | bytes 622592 | tf_op jit(solution)/shard_map/all_to_all | solution.py:45
  162.1 11.9 %collective-permute-start.15 = (bf16[704,256]{1,0:T(8,128)(2,1)}, bf16[704,256]{1,0:T(8,128)(2,1)}, u32[]{:S(2)}, u32[]{:S(2)}) collective-permute-start(bf16[704,256]{1,0:T(8,128)(2,1)} %slice.154), channel_id=1, source_target_pairs={{12,0},{0,4},{4,8},{8,12},{13,1},{1,5},{5,9},{9,13},{14,2},{2,6},{... | collective-permute-start | bytes 1081352 | tf_op jit(solution)/shard_map/ppermute | solution.py:54
  163.3 23.5 %collective-permute-start.7 = (bf16[160,1024]{1,0:T(8,128)(2,1)}, bf16[160,1024]{1,0:T(8,128)(2,1)}, u32[]{:S(2)}, u32[]{:S(2)}) collective-permute-start(bf16[160,1024]{1,0:T(8,128)(2,1)} %get-tuple-element.51), channel_id=1, source_target_pairs={{0,1},{1,0},{2,3},{3,2},{4,5},{5,4},{6,7},{7,6},{8,9},{9,8},{10,11... | collective-permute-start | bytes 983048 | tf_op jit(solution)/shard_map/ppermute | solution.py:58
  164.4 1.9 copy-start.4
  172.0 1.7 copy-start.5
  173.6 13.2 %collective-permute-start.12 = (bf16[160,768]{1,0:T(8,128)(2,1)}, bf16[160,768]{1,0:T(8,128)(2,1)}, u32[]{:S(2)}, u32[]{:S(2)}) collective-permute-start(bf16[160,768]{1,0:T(8,128)(2,1)} %get-tuple-element.63), channel_id=1, source_target_pairs={{0,1},{1,0},{2,3},{3,2},{4,5},{5,4},{6,7},{7,6},{8,9},{9,8},{10,11... | collective-permute-start | bytes 737288 | tf_op jit(solution)/shard_map/ppermute | solution.py:58
  176.0 16.5 %collective-permute-start.18 = (f32[16,4800]{1,0:T(8,128)}, f32[16,4800]{1,0:T(8,128)S(1)}, u32[]{:S(2)}, u32[]{:S(2)}) collective-permute-start(f32[16,4800]{1,0:T(8,128)} %reshape.35), channel_id=1, source_target_pairs={{0,16},{16,0},{1,17},{17,1},{2,18},{18,2},{3,19},{19,3},{4,20},{20... | collective-permute-start | bytes 921608 | tf_op jit(solution)/shard_map/ppermute | solution.py:49
  180.7 1.9 copy-start.6
  182.6 6.6 %copy-start.8 = (f32[160,1024]{1,0:T(8,128)S(1)}, f32[160,1024]{1,0:T(8,128)}, u32[]{:S(2)}) copy-start(f32[160,1024]{1,0:T(8,128)} %copy-done.7) | copy-start | bytes 1966084
  185.0 4.2 %collective-permute-start.16 = (bf16[160,256]{1,0:T(8,128)(2,1)S(1)}, bf16[160,256]{1,0:T(8,128)(2,1)S(1)}, u32[]{:S(2)}, u32[]{:S(2)}) collective-permute-start(bf16[160,256]{1,0:T(8,128)(2,1)S(1)} %get-tuple-element.71), channel_id=1, source_target_pairs={{0,1},{1,0},{2,3},{3,2},{4,5},{5,4},{6,7},{7,6},{8,9},{9,8},{10,11... | collective-permute-start | bytes 245768 | tf_op jit(solution)/shard_map/ppermute | solution.py:58
  185.3 7.2 %copy-start.14 = (f32[16,4800]{1,0:T(8,128)S(1)}, f32[16,4800]{1,0:T(8,128)}, u32[]{:S(2)}) copy-start(f32[16,4800]{1,0:T(8,128)} %reshape.35) | copy-start | bytes 921604
  185.3 21.5 %collective-permute-start.17 = (bf16[160,2496]{1,0:T(8,128)(2,1)S(1)}, bf16[160,2496]{1,0:T(8,128)(2,1)S(1)}, u32[]{:S(2)}, u32[]{:S(2)}) collective-permute-start(bf16[160,2496]{1,0:T(8,128)(2,1)S(1)} %get-tuple-element.73), channel_id=1, source_target_pairs={{0,1},{1,0},{2,3},{3,2},{4,5},{5,4},{6,7},{7,6},{8,9},{9,8},{10,11... | collective-permute-start | bytes 2396168 | tf_op jit(solution)/shard_map/ppermute | solution.py:58
  192.5 14.3 %copy-start = (f32[1,150,4800]{2,1,0:T(8,128)S(1)}, f32[1,150,4800]{2,1,0:T(8,128)}, u32[]{:S(2)}) copy-start(f32[1,150,4800]{2,1,0:T(8,128)} %copy.83) | copy-start | bytes 8640004

commit v5 on v4

--- a/solution.py
+++ b/solution.py
@@ -124,7 +124,8 @@
     for n, keep, came in zip(counts, halves[::2], halves[1::2]):
         for i in range(n):
             s = pl.ds(pl.multiple_of(where[k] * own, own), own)
-            back = keep[:, i * own:(i + 1) * own] + came[:, i * own:(i + 1) * own].astype(F32)
+            j = i ^ 1
+            back = keep[:, i * own:(i + 1) * own] + came[:, j * own:(j + 1) * own].astype(F32)
             out = gelu_back(pre_ref[:, s].astype(F32), back).astype(BF16)
             out_ref[:, s] = out[:out_ref.shape[0]]
             k += 1
@@ -193,11 +194,6 @@
     og = out_grad.T
     og_give = jnp.where(side == 0, og[start:], og[:width])
     og_mine = jnp.where(side == 0, og[:width], og[start:])
-    og_came = partner(og_give)
-    below = jnp.where((ix & 1) == 0, og_mine, og_came)
-    above = jnp.where((ix & 1) == 0, og_came, og_mine)
-    block = jnp.concatenate([below, above], axis=1)
-    pair = 2 * own
     pre_pad = jnp.pad(pre_act, ((0, rows - hid), (0, 0)))
     w_pad = jnp.pad(weight, ((0, rows - hid), (0, 0)))
     w_first, w_last = w_pad[:, :width], w_pad[:, start:]
@@ -206,13 +202,27 @@
     w_give = jnp.where(side == 0, w_last, w_first)
 
     def spot(keys):
-        return jnp.stack([((iy + dy) & (ny - 1)) * (nx // 2) + ((ix >> 1) ^ j) for j, dy in keys])
+        out = []
+        for j, dy in keys:
+            at = (nx - 1 - ix) if j else ix
+            row = ((iy + dy) & (ny - 1)) * nx
+            out += [row + at, row + (at ^ 1)]
+        return jnp.stack(out)
+
+    def around(x):
+        return shift(x, "y", 1), shift(x, "y", -1), peer(x)
+
+    def beyond(up, down, over):
+        return shift(up, "y", 1), peer(up), shift(over, "y", -1)
+
+    a0, b0 = og_mine, partner(og_give)
+    a1 = around(a0)
 
     act = gelu16(pre_act)
     q3 = jnp.concatenate(split(q_init, 3), axis=1)
     y = fold(dot(q3, out_grad, 0, 1), 3)
-    y_all, block, pre_pad, w_give = tie(spread(y, MP), block, pre_pad, w_give)
-    up, down, over = shift(block, "y", 1), shift(block, "y", -1), peer(block)
+    y_all, a0, b0, a1, pre_pad, w_give = tie(spread(y, MP), a0, b0, a1, pre_pad, w_give)
+    b1 = around(b0)
     pre_two = (pre_pad, partner(pre_pad))
     w_two = (w_mine, partner(w_give))
     y_all = y_all.transpose(1, 0, 2).reshape(rank, toks)
@@ -220,8 +230,10 @@
     e2 = split(error, 2)
     p_err = sum(fold(dot(q3, e, 0, 1), 3) for e in e2)
     p_local = fold(dot(y3, act, 1, 1), 3) + p_err
-    pbar = jnp.sum(spread(p_local, "z"), axis=0)
-    pbar, up, down, over = tie((pbar + other_core(pbar)) / groups, up, down, over)
+    p_local, b1, pre_two = tie(spread(p_local, "z"), b1, pre_two)
+    a2, b2 = beyond(*a1), beyond(*b1)
+    pbar = jnp.sum(p_local, axis=0)
+    pbar = (pbar + other_core(pbar)) / groups
 
     l3 = jnp.concatenate(split(pbar, 3), axis=0)
     z_part = fold(dot(l3, act, 1, 0), 3)
@@ -235,11 +247,13 @@
         ],
         axis=1,
     )
-    took, up, down, over = tie(lax.all_to_all(sent, MP, 0, 0, tiled=True), up, down, over)
-    far, over_up, over_down = shift(up, "y", 1), peer(up), shift(over, "y", -1)
+    sent, a2, w_two = tie(sent, a2, w_two)
+    a3 = peer(a2[0])
     keys = [[(0, 0), (0, 1), (0, -1), (1, 0)], [(0, 2), (1, 1), (1, -1)], [(1, 2)]]
     places = [spot(k) for k in keys]
-    keep_1, send_1, total = add_products(places[0], pre_two, w_two, [[block], [up], [down], [over]], None)
+    turns = [[x] for both in zip((a0,) + a1, (b0,) + b1) for x in both]
+    keep_1, send_1, total = add_products(places[0], pre_two, w_two, turns, None)
+    took = lax.all_to_all(sent, MP, 0, 0, tiled=True)
     took = jnp.sum(took, axis=0)
     z = took[:rank]
     gram = jnp.concatenate(jnp.split(took[rank:], quarter, axis=1), axis=0)
@@ -249,25 +263,22 @@
     low, high = r_local[:half], r_local[half:]
     keep = jnp.where(core == 0, low, high) + other_core(jnp.where(core == 0, high, low))
     r_part = lax.all_to_all(keep.reshape(nz, half // nz, feat), "z", 0, 0, tiled=True)
-    r_part, far, over_up, over_down, total = tie(jnp.sum(r_part, axis=0), far, over_up, over_down, total)
+    r_part, b2, a3, total = tie(r_part, b2, a3, total)
+    b3 = shift(b2[1], "y", 1)
     came_1 = partner(send_1)
-    r_part, far, over_up, over_down = tie(spread(r_part, MP), far, over_up, over_down)
-    cut = (width // 3 + 64) // 128 * 128
-    last = [
-        peer(far[:cut]),
-        shift(over_up[cut:2 * cut], "y", 1),
-        shift(over_down[2 * cut:], "y", -1),
-    ]
-    keep_2, send_2, total = add_products(places[1], pre_two, w_two, [[far], [over_up], [over_down]], total)
-    r_part = jnp.sum(r_part, axis=0) / groups
-    mine, total, *last = tie(spread(r_part, "z"), total, *last)
-    mine = mine.reshape(half, feat)
+    turns = [[x] for both in zip(a2, b2) for x in both]
+    keep_2, send_2, total = add_products(places[1], pre_two, w_two, turns, total)
+    r_part = jnp.sum(r_part, axis=0)
+    r_part, b3, total = tie(spread(r_part, MP), b3, total)
     came_2 = partner(send_2)
-    keep_3, send_3, grad_mine, grad_give = add_products(places[2], pre_two, w_two, [last], total, True)
+    keep_3, send_3, grad_mine, grad_give = add_products(places[2], pre_two, w_two, [[a3], [b3]], total, True)
+    r_part, grad_give, send_3 = tie(jnp.sum(r_part, axis=0) / groups, grad_give, send_3)
     grad_came = partner(grad_give)
     came_3 = partner(send_3)
+    mine, grad_came = tie(spread(r_part, "z"), grad_came)
+    mine = mine.reshape(half, feat)
     halves = [(keep_1, came_1), (keep_2, came_2), (keep_3, came_3)]
-    pre_grad = pre_grads(jnp.concatenate(places), pre_pad, hid, pair, halves)
+    pre_grad = pre_grads(jnp.concatenate(places), pre_pad, hid, own, halves)
     theirs = other_core(mine)
     r_all = jnp.concatenate([jnp.where(core == 0, mine, theirs), jnp.where(core == 0, theirs, mine)], axis=0)
 

time: 213 us -> 212 us (level)
  waiting for transfers between devices: 54.6 us -> 43.6 us
  starting transfers between devices: 53.7 us -> 60.6 us
  local copies, waits for them, and re-layouts: 31.1 us -> 35.7 us
    ppermute x7, waiting for transfers between devices: 32.8 us -> 7.42 us  [partner(): return lax.ppermute(x, 'x', [(i, i ^ 1) for i in range(lax.axis_size('x'))])]
    ppermute x3 -> x5, waiting for transfers between devices: 0.73 us -> 18.8 us  [peer(): return lax.ppermute(x, 'x', [(i, n - 1 - i) for i in range(n)])]
    unnamed x44 -> x72, local copies, waits for them, and re-layouts: 19.1 us -> 29.3 us
    ppermute x3 -> x5, starting transfers between devices: 0.28 us -> 8.48 us  [peer(): return lax.ppermute(x, 'x', [(i, n - 1 - i) for i in range(n)])]
    all_to_all x3, starting transfers between devices: 18.9 us -> 12.9 us  [spread(): lax.all_to_all(jnp.broadcast_to(x, (n,) + x.shape), axis, 0, 0, tiled=True)]
    ppermute x6 -> x9, starting transfers between devices: 4.4 us -> 10.1 us  [shift(): return lax.ppermute(x, axis, [((i + step) % n, i) for i in range(n)])]
    slice x3 -> x0, local copies, waits for them, and re-layouts: 5.4 us -> none  [the longest x1 1.81 us: shards(): far[:cut]]
    all_to_all x1, starting transfers between devices: 8.18 us -> 3.43 us  [shards(): lax.all_to_all(keep.reshape(nz, half // nz, feat), 'z', 0, 0, tiled=True)]
  transfers between devices with their start and end apart: 24 -> 29, of which waited for: 11 -> 9; matrix products, arithmetic and copies ran while one was open for 19% -> 17% of each run, Pallas kernels for 8% -> 8%
where the time goes in v5:
time: 212 us; the launch traced here: 210 us
  starting transfers between devices  60.6 us (29%)
  waiting for transfers between devices  43.6 us (21%)
  local copies, waits for them, and re-layouts  35.7 us (17%)
  other arithmetic  19.6 us (9%)
  blocking collectives  17.4 us (8%)
  Pallas kernels  17.3 us (8%)
  matrix products  15.1 us (7%)
    unnamed x72, local copies, waits for them, and re-layouts  29.3 us
    ppermute x5, waiting for transfers between devices, peer(): return lax.ppermute(x, 'x', [(i, n - 1 - i) for i in range(n)])  18.8 us
    all_to_all x1, blocking collectives, spread(): lax.all_to_all(jnp.broadcast_to(x, (n,) + x.shape), axis, 0, 0, tiled=True)  17.4 us
    pallas_call x3, Pallas kernels, add_products(): pl.pallas_call(functools.partial(products, [len(b) for b in blocks], tota...  13.8 us
    ppermute x3, starting transfers between devices, other_core(): return lax.ppermute(x, 'core', [(0, 1), (1, 0)])  13.4 us
    all_to_all x3, starting transfers between devices, spread(): lax.all_to_all(jnp.broadcast_to(x, (n,) + x.shape), axis, 0, 0, tiled=True)  12.9 us
    dot_general x8, matrix products, dot(): lax.dot_general(a, b, (((ca,), (cb,)), ((), ())), preferred_element_type=...  12.3 us
    all_to_all x3, waiting for transfers between devices, spread(): lax.all_to_all(jnp.broadcast_to(x, (n,) + x.shape), axis, 0, 0, tiled=True)  11.6 us
  transfers between devices with their start and end apart: 29, of which 9 were waited for; matrix products, arithmetic and copies ran while one was open for 17% of the time, Pallas kernels for 8%

profile of v5, /device:TPU:1, one launch (start us, length us, event | category | flops | bytes accessed | tf_op | source)
XLA Modules:
  0.0 210.4 jit_solution(12975470355830862266)
XLA Ops:
  0.7 2.4 %broadcast_select_fusion.2 = (bf16[2496,128]{1,0:T(8,128)(2,1)}, bf16[2496,128]{1,0:T(8,128)(2,1)S(1)}) fusion(pred[]{:T(512)S(6)} %eq.4, bf16[4800,128]{1,0:T(8,128)(2,1)} %bitcast.73), kind=kLoop, calls=%fused_computation.28 | loop fusion | flops 638976 | bytes 2555905 | tf_op jit(solution)/shard_map/jit(_where)/select_n | solution.py:195
  3.0 3.6 %collective-permute-start.1 = (bf16[2496,128]{1,0:T(8,128)(2,1)S(1)}, bf16[2496,128]{1,0:T(8,128)(2,1)}, u32[]{:S(2)}, u32[]{:S(2)}) collective-permute-start(bf16[2496,128]{1,0:T(8,128)(2,1)S(1)} %get-tuple-element.58.refs_0_), channel_id=1, source_target_pairs={{4,0},{8,4},{12,8},{0,12},{5,1},{9,5},{13,9},{1,13},{6,2},{10,6},{... | collective-permute-start | bytes 1916936 | tf_op jit(solution)/shard_map/ppermute | solution.py:54
  6.6 2.5 %collective-permute-start.3 = (bf16[2496,128]{1,0:T(8,128)(2,1)S(1)}, bf16[2496,128]{1,0:T(8,128)(2,1)}, u32[]{:S(2)}, u32[]{:S(2)}) collective-permute-start(bf16[2496,128]{1,0:T(8,128)(2,1)S(1)} %get-tuple-element.58.refs_0_), channel_id=1, source_target_pairs={{0,3},{1,2},{2,1},{3,0},{4,7},{5,6},{6,5},{7,4},{8,11},{9,10},{10,... | collective-permute-start | bytes 1916936 | tf_op jit(solution)/shard_map/ppermute | solution.py:63
  10.8 5.2 %all-to-all-start = ((f32[16,32,128]{2,1,0:T(8,128)}), f32[16,32,128]{2,1,0:T(8,128)S(1)}, u32[]{:S(2)}, u32[]{:S(2)}) async-start(f32[16,32,128]{2,1,0:T(8,128)} %broadcast_in_dim.27), calls=%async_computation | async-start | bytes 524288 | tf_op jit(solution)/shard_map/all_to_all | solution.py:45
  16.1 3.4 %broadcast_select_fusion = (bf16[160,2496]{1,0:T(8,128)(2,1)S(1)}, bf16[160,2496]{1,0:T(8,128)(2,1)}) fusion(pred[]{:T(512)S(6)} %eq.4, bf16[150,4800]{1,0:T(8,128)(2,1)} %param.7, pred[2496]{0:T(1024)(128)(4,1)S(1)} %iota_compare_fusion.3), kind=kLoop, calls=%fused_computation.26 | loop fusion | flops 1597440 | bytes 3039937 | tf_op jit(solution)/shard_map/jit(_where)/select_n | solution.py:201
  20.7 7.9 %all-to-all-done = f32[16,32,128]{2,1,0:T(8,128)S(1)} async-done(((f32[16,32,128]{2,1,0:T(8,128)}), f32[16,32,128]{2,1,0:T(8,128)S(1)}, u32[]{:S(2)}, u32[]{:S(2)}) %all-to-all-start) | async-done | bytes 262176 | tf_op jit(solution)/shard_map/all_to_all | solution.py:45
  30.9 1.5 collective-permute-start.6
  32.5 1.7 fusion.21
  34.5 17.4 %all_to_all.30 = f32[8,32,150]{2,1,0:T(8,128)S(1)} all-to-all(f32[8,32,150]{2,1,0:T(8,128)S(1)} %broadcast_in_dim.30), channel_id=1, replica_groups=mesh['z'=8,'core'=2,'y'=4,'x'=4] {'z'}, dimensions={0} | all-to-all | bytes 307200 | tf_op jit(solution)/shard_map/all_to_all | solution.py:45
  52.8 4.6 %collective-permute-start.8 = (f32[32,150]{1,0:T(8,128)S(1)}, f32[32,150]{1,0:T(8,128)S(1)}, u32[]{:S(2)}, u32[]{:S(2)}) collective-permute-start(f32[32,150]{1,0:T(8,128)S(1)} %reduce_sum.36), channel_id=1, source_target_pairs={{0,16},{16,0},{1,17},{17,1},{2,18},{18,2},{3,19},{19,3},{4,20},{20... | collective-permute-start | bytes 57608 | tf_op jit(solution)/shard_map/ppermute | solution.py:49
  57.5 1.5 collective-permute-start.10
  58.9 1.4 collective-permute-start.9
  60.4 1.5 collective-permute-start.12
  62.6 1.9 fusion.53
  65.3 1.7 fusion.19
  67.1 7.8 %collective-permute-done.10.refs_2_ = bf16[2496,128]{1,0:T(8,128)(2,1)S(1)} collective-permute-done((bf16[2496,128]{1,0:T(8,128)(2,1)}, bf16[2496,128]{1,0:T(8,128)(2,1)S(1)}, u32[]{:S(2)}, u32[]{:S(2)}) %collective-permute-start.10) | collective-permute-done | bytes 639008 | tf_op jit(solution)/shard_map/ppermute | solution.py:63
  75.7 1.3 collective-permute-done.11.refs_4_
  77.9 1.7 collective-permute-done.12.w_b
  79.6 7.0 %all-to-all-start.2 = ((f32[16,40,128]{2,1,0:T(8,128)}), f32[16,40,128]{2,1,0:T(8,128)S(1)}, u32[]{:S(2)}, u32[]{:S(2)}) async-start(f32[16,40,128]{2,1,0:T(8,128)} %pad_maximum_fusion.2), calls=%async_computation.2 | async-start | bytes 655360 | tf_op jit(solution)/shard_map/all_to_all | solution.py:256
  86.6 3.6 %fusion.30 = f32[96,4800]{1,0:T(8,128)} fusion(bf16[32,150]{1,0:T(8,128)(2,1)S(1)} %get-tuple-element.122, bf16[32,150]{1,0:T(8,128)(2,1)S(1)} %get-tuple-element.121, bf16[32,150]{1,0:T(8,128)(2,1)S(1)} %get-tuple-element.103, f32[1,150,4800]{2,0,1:T(1,128)} %param.8), kind=kOutput, calls=%fused_computation.67 | convolution fusion | flops 141206400 | bytes 4752000 | tf_op jit(solution)/shard_map/dot_general | solution.py:35
  90.1 4.4 %all-to-all-done.2 = f32[16,40,128]{2,1,0:T(8,128)S(1)} async-done(((f32[16,40,128]{2,1,0:T(8,128)}), f32[16,40,128]{2,1,0:T(8,128)S(1)}, u32[]{:S(2)}, u32[]{:S(2)}) %all-to-all-start.2) | async-done | bytes 327712 | tf_op jit(solution)/shard_map/all_to_all | solution.py:256
  94.6 2.0 fusion.38
  96.5 1.8 fusion.14
  98.3 3.3 %collective-permute-start.14 = (f32[16,4800]{1,0:T(8,128)S(1)}, f32[16,4800]{1,0:T(8,128)S(1)}, u32[]{:S(2)}, u32[]{:S(2)}) collective-permute-start(f32[16,4800]{1,0:T(8,128)S(1)} %slice_select_fusion), channel_id=1, source_target_pairs={{0,16},{16,0},{1,17},{17,1},{2,18},{18,2},{3,19},{19,3},{4,20},{20... | collective-permute-start | bytes 921608 | tf_op jit(solution)/shard_map/ppermute | solution.py:49
  103.4 2.4 %collective-permute-start.18 = (bf16[2496,128]{1,0:T(8,128)(2,1)}, bf16[2496,128]{1,0:T(8,128)(2,1)}, u32[]{:S(2)}, u32[]{:S(2)}) collective-permute-start(bf16[2496,128]{1,0:T(8,128)(2,1)} %collective-permute-done.9.refs_0_), channel_id=1, source_target_pairs={{0,3},{1,2},{2,1},{3,0},{4,7},{5,6},{6,5},{7,4},{8,11},{9,10},{10,... | collective-permute-start | bytes 1916936 | tf_op jit(solution)/shard_map/ppermute | solution.py:63
  106.8 3.4 %all-to-all-start.3 = ((f32[8,2,4800]{2,1,0:T(2,128)}), f32[8,2,4800]{2,1,0:T(2,128)S(1)}, u32[]{:S(2)}, u32[]{:S(2)}) async-start(f32[8,2,4800]{2,1,0:T(2,128)} %reshape.33), calls=%async_computation.3 | async-start | bytes 622592 | tf_op jit(solution)/shard_map/all_to_all | solution.py:265
  113.6 6.0 %shard_map.76 = (f32[160,1024]{1,0:T(8,128)S(1)}, bf16[160,1024]{1,0:T(8,128)(2,1)}, f32[320,2496]{1,0:T(8,128)S(1)}) custom-call(s32[8]{0:T(128)S(1)} %stack.73.where, bf16[160,2048]{1,0:T(8,128)(2,1)S(1)} %pad.8.pre_a.pre_ref, bf16[160,2048]{1,0:T(8,128)(2,1)S(1)} %collective-permute-done.7.pre_b, bf16[160,2496]{1,0:T(8,128)(2,1)S(1)} %get-tuple-element.56.w_a, ...), custom_call_target="tpu_custom_call" | custom-call | tf_op jit(solution)/shard_map/pallas_call | solution.py:112
  119.5 1.7 copy-done.1
  122.0 11.0 %collective-permute-done.18.refs_0_ = bf16[2496,128]{1,0:T(8,128)(2,1)} collective-permute-done((bf16[2496,128]{1,0:T(8,128)(2,1)}, bf16[2496,128]{1,0:T(8,128)(2,1)}, u32[]{:S(2)}, u32[]{:S(2)}) %collective-permute-start.18) | collective-permute-done | bytes 639008 | tf_op jit(solution)/shard_map/ppermute | solution.py:63
  134.2 4.3 %all-to-all-start.4 = ((f32[16,2,4800]{2,1,0:T(2,128)}), f32[16,2,4800]{2,1,0:T(2,128)}, u32[]{:S(2)}, u32[]{:S(2)}) async-start(f32[16,2,4800]{2,1,0:T(2,128)} %broadcast_in_dim.32), calls=%async_computation.4 | async-start | bytes 1245184 | tf_op jit(solution)/shard_map/all_to_all | solution.py:45
  138.4 2.5 %collective-permute-start.20 = (bf16[2496,128]{1,0:T(8,128)(2,1)}, bf16[2496,128]{1,0:T(8,128)(2,1)}, u32[]{:S(2)}, u32[]{:S(2)}) collective-permute-start(bf16[2496,128]{1,0:T(8,128)(2,1)} %collective-permute-done.16.refs_3_), channel_id=1, source_target_pairs={{4,0},{8,4},{12,8},{0,12},{5,1},{9,5},{13,9},{1,13},{6,2},{10,6},{... | collective-permute-start | bytes 1916936 | tf_op jit(solution)/shard_map/ppermute | solution.py:54
  141.0 3.6 %copy.71 = f32[1,150,4800]{2,1,0:T(8,128)} copy(f32[1,150,4800]{2,0,1:T(1,128)} %param.8) | data formatting | bytes 5760000
  144.8 1.5 collective-permute-start.13
  146.9 2.9 %cholesky.17 = f32[32,32]{1,0:T(8,128)S(1)} custom-call(f32[32,32]{1,0:T(8,128)S(1)} %fusion.49), custom_call_target="Cholesky" | custom-call | tf_op jit(solution)/shard_map/jit(cholesky)/cholesky | solution.py:285
  149.9 1.9 copy-done.2
  154.0 4.6 %shard_map.77 = (f32[160,768]{1,0:T(8,128)S(1)}, bf16[160,768]{1,0:T(8,128)(2,1)S(1)}, f32[320,2496]{1,0:T(8,128)S(1)}) custom-call(s32[6]{0:T(128)S(1)} %stack.74.where, bf16[160,2048]{1,0:T(8,128)(2,1)S(1)} %pad.8.pre_a.pre_ref, bf16[160,2048]{1,0:T(8,128)(2,1)S(1)} %collective-permute-done.7.pre_b, bf16[160,2496]{1,0:T(8,128)(2,1)S(1)} %get-tuple-element.56.w_a, ...), custom_call_target="tpu_custom_call" | custom-call | tf_op jit(solution)/shard_map/pallas_call | solution.py:112
  158.6 1.7 copy-done.3
  162.2 1.9 copy-done.4
  164.2 3.3 %shard_map.78 = (f32[160,256]{1,0:T(8,128)S(1)}, bf16[160,256]{1,0:T(8,128)(2,1)S(1)}, f32[160,2496]{1,0:T(8,128)S(1)}, bf16[160,2496]{1,0:T(8,128)(2,1)}) custom-call(s32[2]{0:T(128)S(1)} %pad_add_fusion.where, bf16[160,2048]{1,0:T(8,128)(2,1)S(1)} %pad.8.pre_a.pre_ref, bf16[160,2048]{1,0:T(8,128)(2,1)S(1)} %collective-permute-done.7.pre_b, ...), custom_call_target="tpu_custom_call" | custom-call | tf_op jit(solution)/shard_map/pallas_call | solution.py:112
  171.4 3.4 %all-to-all-start.5 = ((f32[8,2,4800]{2,1,0:T(2,128)}), f32[8,2,4800]{2,1,0:T(2,128)S(1)}, u32[]{:S(2)}, u32[]{:S(2)}) async-start(f32[8,2,4800]{2,1,0:T(2,128)} %broadcast_in_dim.33), calls=%async_computation.5 | async-start | bytes 622592 | tf_op jit(solution)/shard_map/all_to_all | solution.py:45
  175.5 2.4 %custom-call.7 = f32[1,32,32]{1,2,0:T(8,128)S(1)} custom-call(f32[1,32,32]{2,1,0:T(8,128)S(1)} %fusion.44), custom_call_target="InvertDiagBlocksLowerTriangular" | custom-call | tf_op jit(solution)/shard_map/jit(_solve_triangular)/triangular_solve | solution.py:286
  181.4 3.7 %all-to-all-done.5 = f32[8,2,4800]{2,1,0:T(2,128)S(1)} async-done(((f32[8,2,4800]{2,1,0:T(2,128)}), f32[8,2,4800]{2,1,0:T(2,128)S(1)}, u32[]{:S(2)}, u32[]{:S(2)}) %all-to-all-start.5) | async-done | bytes 307232 | tf_op jit(solution)/shard_map/all_to_all | solution.py:45
  185.2 2.0 collective-permute-done.22.came_ref
  188.1 5.5 %collective-permute-start.23 = (f32[16,4800]{1,0:T(8,128)}, f32[16,4800]{1,0:T(8,128)S(1)}, u32[]{:S(2)}, u32[]{:S(2)}) collective-permute-start(f32[16,4800]{1,0:T(8,128)} %reshape.35), channel_id=1, source_target_pairs={{0,16},{16,0},{1,17},{17,1},{2,18},{18,2},{3,19},{19,3},{4,20},{20... | collective-permute-start | bytes 921608 | tf_op jit(solution)/shard_map/ppermute | solution.py:49
  195.3 3.7 %collective-permute-done.21.refs_5_ = bf16[160,256]{1,0:T(8,128)(2,1)S(1)} collective-permute-done((bf16[160,256]{1,0:T(8,128)(2,1)S(1)}, bf16[160,256]{1,0:T(8,128)(2,1)S(1)}, u32[]{:S(2)}, u32[]{:S(2)}) %collective-permute-start.21) | collective-permute-done | bytes 81952 | tf_op jit(solution)/shard_map/ppermute | solution.py:58
  199.0 2.9 %shard_map.79 = bf16[150,2048]{1,0:T(8,128)(2,1)} custom-call(s32[16]{0:T(128)S(1)} %concatenate.34.where, bf16[160,2048]{1,0:T(8,128)(2,1)S(1)} %pad.8.pre_a.pre_ref, f32[160,1024]{1,0:T(8,128)S(1)} %copy-done.10, bf16[160,1024]{1,0:T(8,128)(2,1)} %collective-permute-done.13.refs_1_, f32[160,768]{1,0:T(8,128)S(1)} %get-tuple-element.74.refs_2_, ...), custom_call_target="tpu_custom_call" | custom-call | tf_op jit(solution)/shard_map/pallas_call | solution.py:137
  203.1 1.5 fusion.12
  205.9 4.6 %copy.42 = f32[1,150,4800]{2,0,1:T(1,128)} copy(f32[1,150,4800]{2,1,0:T(8,128)S(1)} %bitcast.72) | data formatting | bytes 5760000
  (150 shorter events, 36.1 us)
Async XLA Ops:
  0.6 8.4 %copy-start.27 = (f32[4800,32]{0,1:T(8,128)S(1)}, f32[4800,32]{0,1:T(8,128)}, u32[]{:S(2)}) copy-start(f32[4800,32]{0,1:T(8,128)} %param.9) | copy-start | bytes 1843204
  0.7 8.6 %copy-start.25 = (bf16[128,4800]{0,1:T(8,128)(2,1)S(1)}, bf16[128,4800]{0,1:T(8,128)(2,1)}, u32[]{:S(2)}) copy-start(bf16[128,4800]{0,1:T(8,128)(2,1)} %param.6) | copy-start | bytes 3686404
  3.0 6.6 %copy-start.5 = (bf16[2496,128]{1,0:T(8,128)(2,1)}, bf16[2496,128]{1,0:T(8,128)(2,1)S(1)}, u32[]{:S(2)}) copy-start(bf16[2496,128]{1,0:T(8,128)(2,1)S(1)} %get-tuple-element.58.refs_0_) | copy-start | bytes 1916932
  3.0 25.5 %collective-permute-start.1 = (bf16[2496,128]{1,0:T(8,128)(2,1)S(1)}, bf16[2496,128]{1,0:T(8,128)(2,1)}, u32[]{:S(2)}, u32[]{:S(2)}) collective-permute-start(bf16[2496,128]{1,0:T(8,128)(2,1)S(1)} %get-tuple-element.58.refs_0_), channel_id=1, source_target_pairs={{4,0},{8,4},{12,8},{0,12},{5,1},{9,5},{13,9},{1,13},{6,2},{10,6},{... | collective-permute-start | bytes 1916936 | tf_op jit(solution)/shard_map/ppermute | solution.py:54
  6.6 22.0 %collective-permute-start.2 = (bf16[2496,128]{1,0:T(8,128)(2,1)S(1)}, bf16[2496,128]{1,0:T(8,128)(2,1)S(1)}, u32[]{:S(2)}, u32[]{:S(2)}) collective-permute-start(bf16[2496,128]{1,0:T(8,128)(2,1)S(1)} %get-tuple-element.58.refs_0_), channel_id=1, source_target_pairs={{12,0},{0,4},{4,8},{8,12},{13,1},{1,5},{5,9},{9,13},{14,2},{2,6},{... | collective-permute-start | bytes 1916936 | tf_op jit(solution)/shard_map/ppermute | solution.py:54
  6.6 22.8 %collective-permute-start.3 = (bf16[2496,128]{1,0:T(8,128)(2,1)S(1)}, bf16[2496,128]{1,0:T(8,128)(2,1)}, u32[]{:S(2)}, u32[]{:S(2)}) collective-permute-start(bf16[2496,128]{1,0:T(8,128)(2,1)S(1)} %get-tuple-element.58.refs_0_), channel_id=1, source_target_pairs={{0,3},{1,2},{2,1},{3,0},{4,7},{5,6},{6,5},{7,4},{8,11},{9,10},{10,... | collective-permute-start | bytes 1916936 | tf_op jit(solution)/shard_map/ppermute | solution.py:63
  9.1 20.3 %collective-permute-start = (bf16[2496,128]{1,0:T(8,128)(2,1)}, bf16[2496,128]{1,0:T(8,128)(2,1)}, u32[]{:S(2)}, u32[]{:S(2)}) collective-permute-start(bf16[2496,128]{1,0:T(8,128)(2,1)} %get-tuple-element.107), channel_id=1, source_target_pairs={{0,1},{1,0},{2,3},{3,2},{4,5},{5,4},{6,7},{7,6},{8,9},{9,8},{10,11... | collective-permute-start | bytes 1916936 | tf_op jit(solution)/shard_map/ppermute | solution.py:58
  10.8 17.8 %all-to-all-start = ((f32[16,32,128]{2,1,0:T(8,128)}), f32[16,32,128]{2,1,0:T(8,128)S(1)}, u32[]{:S(2)}, u32[]{:S(2)}) async-start(f32[16,32,128]{2,1,0:T(8,128)} %broadcast_in_dim.27), calls=%async_computation | async-start | bytes 524288 | tf_op jit(solution)/shard_map/all_to_all | solution.py:45
  16.0 3.4 %copy-start.28 = (bf16[150,2048]{1,0:T(8,128)(2,1)S(1)}, bf16[150,2048]{1,0:T(8,128)(2,1)}, u32[]{:S(2)}) copy-start(bf16[150,2048]{1,0:T(8,128)(2,1)} %param.5) | copy-start | bytes 1843204
  16.0 3.5 %copy-start.22 = (f32[1,150,4800]{2,0,1:T(1,128)S(1)}, f32[1,150,4800]{2,0,1:T(1,128)}, u32[]{:S(2)}) copy-start(f32[1,150,4800]{2,0,1:T(1,128)} %param.8) | copy-start | bytes 8640004
  16.0 3.5 %copy-start.30 = (bf16[4800,32]{0,1:T(8,128)(2,1)S(1)}, bf16[4800,32]{0,1:T(8,128)(2,1)}, u32[]{:S(2)}) copy-start(bf16[4800,32]{0,1:T(8,128)(2,1)} %copy-done.29) | copy-start | bytes 921604
  16.1 3.5 %copy-start.32 = (bf16[4800,32]{0,1:T(8,128)(2,1)S(1)}, bf16[4800,32]{0,1:T(8,128)(2,1)}, u32[]{:S(2)}) copy-start(bf16[4800,32]{0,1:T(8,128)(2,1)} %copy-done.31) | copy-start | bytes 921604
  29.4 22.5 %collective-permute-start.4 = (bf16[2496,128]{1,0:T(8,128)(2,1)}, bf16[2496,128]{1,0:T(8,128)(2,1)}, u32[]{:S(2)}, u32[]{:S(2)}) collective-permute-start(bf16[2496,128]{1,0:T(8,128)(2,1)} %collective-permute-done.refs_1_), channel_id=1, source_target_pairs={{4,0},{8,4},{12,8},{0,12},{5,1},{9,5},{13,9},{1,13},{6,2},{10,6},{... | collective-permute-start | bytes 1916936 | tf_op jit(solution)/shard_map/ppermute | solution.py:54
  29.7 22.2 %collective-permute-start.5 = (bf16[2496,128]{1,0:T(8,128)(2,1)}, bf16[2496,128]{1,0:T(8,128)(2,1)S(1)}, u32[]{:S(2)}, u32[]{:S(2)}) collective-permute-start(bf16[2496,128]{1,0:T(8,128)(2,1)} %collective-permute-done.refs_1_), channel_id=1, source_target_pairs={{12,0},{0,4},{4,8},{8,12},{13,1},{1,5},{5,9},{9,13},{14,2},{2,6},{... | collective-permute-start | bytes 1916936 | tf_op jit(solution)/shard_map/ppermute | solution.py:54
  30.9 21.9 %collective-permute-start.6 = (bf16[2496,128]{1,0:T(8,128)(2,1)}, bf16[2496,128]{1,0:T(8,128)(2,1)}, u32[]{:S(2)}, u32[]{:S(2)}) collective-permute-start(bf16[2496,128]{1,0:T(8,128)(2,1)} %collective-permute-done.refs_1_), channel_id=1, source_target_pairs={{0,3},{1,2},{2,1},{3,0},{4,7},{5,6},{6,5},{7,4},{8,11},{9,10},{10,... | collective-permute-start | bytes 1916936 | tf_op jit(solution)/shard_map/ppermute | solution.py:63
  32.4 20.4 %collective-permute-start.7 = (bf16[160,2048]{1,0:T(8,128)(2,1)S(1)}, bf16[160,2048]{1,0:T(8,128)(2,1)S(1)}, u32[]{:S(2)}, u32[]{:S(2)}) collective-permute-start(bf16[160,2048]{1,0:T(8,128)(2,1)S(1)} %pad.8.pre_a.pre_ref), channel_id=1, source_target_pairs={{0,1},{1,0},{2,3},{3,2},{4,5},{5,4},{6,7},{7,6},{8,9},{9,8},{10,11... | collective-permute-start | bytes 1966088 | tf_op jit(solution)/shard_map/ppermute | solution.py:58
  52.8 9.1 %collective-permute-start.8 = (f32[32,150]{1,0:T(8,128)S(1)}, f32[32,150]{1,0:T(8,128)S(1)}, u32[]{:S(2)}, u32[]{:S(2)}) collective-permute-start(f32[32,150]{1,0:T(8,128)S(1)} %reduce_sum.36), channel_id=1, source_target_pairs={{0,16},{16,0},{1,17},{17,1},{2,18},{18,2},{3,19},{19,3},{4,20},{20... | collective-permute-start | bytes 57608 | tf_op jit(solution)/shard_map/ppermute | solution.py:49
  57.5 17.4 %collective-permute-start.10 = (bf16[2496,128]{1,0:T(8,128)(2,1)}, bf16[2496,128]{1,0:T(8,128)(2,1)S(1)}, u32[]{:S(2)}, u32[]{:S(2)}) collective-permute-start(bf16[2496,128]{1,0:T(8,128)(2,1)} %collective-permute-done.1.refs_2_), channel_id=1, source_target_pairs={{0,3},{1,2},{2,1},{3,0},{4,7},{5,6},{6,5},{7,4},{8,11},{9,10},{10,... | collective-permute-start | bytes 1916936 | tf_op jit(solution)/shard_map/ppermute | solution.py:63
  58.9 16.8 %collective-permute-start.9 = (bf16[2496,128]{1,0:T(8,128)(2,1)}, bf16[2496,128]{1,0:T(8,128)(2,1)}, u32[]{:S(2)}, u32[]{:S(2)}) collective-permute-start(bf16[2496,128]{1,0:T(8,128)(2,1)} %collective-permute-done.1.refs_2_), channel_id=1, source_target_pairs={{4,0},{8,4},{12,8},{0,12},{5,1},{9,5},{13,9},{1,13},{6,2},{10,6},{... | collective-permute-start | bytes 1916936 | tf_op jit(solution)/shard_map/ppermute | solution.py:54
  60.3 16.7 %collective-permute-start.11 = (bf16[2496,128]{1,0:T(8,128)(2,1)}, bf16[2496,128]{1,0:T(8,128)(2,1)S(1)}, u32[]{:S(2)}, u32[]{:S(2)}) collective-permute-start(bf16[2496,128]{1,0:T(8,128)(2,1)} %collective-permute-done.3.refs_6_), channel_id=1, source_target_pairs={{12,0},{0,4},{4,8},{8,12},{13,1},{1,5},{5,9},{9,13},{14,2},{2,6},{... | collective-permute-start | bytes 1916936 | tf_op jit(solution)/shard_map/ppermute | solution.py:54
  60.4 19.2 %collective-permute-start.12 = (bf16[160,2496]{1,0:T(8,128)(2,1)}, bf16[160,2496]{1,0:T(8,128)(2,1)S(1)}, u32[]{:S(2)}, u32[]{:S(2)}) collective-permute-start(bf16[160,2496]{1,0:T(8,128)(2,1)} %get-tuple-element.55), channel_id=1, source_target_pairs={{0,1},{1,0},{2,3},{3,2},{4,5},{5,4},{6,7},{7,6},{8,9},{9,8},{10,11... | collective-permute-start | bytes 2396168 | tf_op jit(solution)/shard_map/ppermute | solution.py:58
  62.6 2.8 %copy-start.23 = (f32[1,150,4800]{2,0,1:T(1,128)S(1)}, f32[1,150,4800]{2,0,1:T(1,128)}, u32[]{:S(2)}) copy-start(f32[1,150,4800]{2,0,1:T(1,128)} %param.8) | copy-start | bytes 8640004
  79.6 14.9 %all-to-all-start.2 = ((f32[16,40,128]{2,1,0:T(8,128)}), f32[16,40,128]{2,1,0:T(8,128)S(1)}, u32[]{:S(2)}, u32[]{:S(2)}) async-start(f32[16,40,128]{2,1,0:T(8,128)} %pad_maximum_fusion.2), calls=%async_computation.2 | async-start | bytes 655360 | tf_op jit(solution)/shard_map/all_to_all | solution.py:256
  94.5 2.0 copy-start.24
  98.3 7.5 %collective-permute-start.14 = (f32[16,4800]{1,0:T(8,128)S(1)}, f32[16,4800]{1,0:T(8,128)S(1)}, u32[]{:S(2)}, u32[]{:S(2)}) collective-permute-start(f32[16,4800]{1,0:T(8,128)S(1)} %slice_select_fusion), channel_id=1, source_target_pairs={{0,16},{16,0},{1,17},{17,1},{2,18},{18,2},{3,19},{19,3},{4,20},{20... | collective-permute-start | bytes 921608 | tf_op jit(solution)/shard_map/ppermute | solution.py:49
  101.7 20.4 %collective-permute-start.15 = (bf16[2496,128]{1,0:T(8,128)(2,1)}, bf16[2496,128]{1,0:T(8,128)(2,1)}, u32[]{:S(2)}, u32[]{:S(2)}) collective-permute-start(bf16[2496,128]{1,0:T(8,128)(2,1)} %collective-permute-done.4.refs_3_), channel_id=1, source_target_pairs={{4,0},{8,4},{12,8},{0,12},{5,1},{9,5},{13,9},{1,13},{6,2},{10,6},{... | collective-permute-start | bytes 1916936 | tf_op jit(solution)/shard_map/ppermute | solution.py:54
  102.2 19.8 %collective-permute-start.16 = (bf16[2496,128]{1,0:T(8,128)(2,1)}, bf16[2496,128]{1,0:T(8,128)(2,1)}, u32[]{:S(2)}, u32[]{:S(2)}) collective-permute-start(bf16[2496,128]{1,0:T(8,128)(2,1)} %collective-permute-done.4.refs_3_), channel_id=1, source_target_pairs={{0,3},{1,2},{2,1},{3,0},{4,7},{5,6},{6,5},{7,4},{8,11},{9,10},{10,... | collective-permute-start | bytes 1916936 | tf_op jit(solution)/shard_map/ppermute | solution.py:63
  102.9 19.1 %collective-permute-start.17 = (bf16[2496,128]{1,0:T(8,128)(2,1)}, bf16[2496,128]{1,0:T(8,128)(2,1)}, u32[]{:S(2)}, u32[]{:S(2)}) collective-permute-start(bf16[2496,128]{1,0:T(8,128)(2,1)} %collective-permute-done.6.refs_7_), channel_id=1, source_target_pairs={{12,0},{0,4},{4,8},{8,12},{13,1},{1,5},{5,9},{9,13},{14,2},{2,6},{... | collective-permute-start | bytes 1916936 | tf_op jit(solution)/shard_map/ppermute | solution.py:54
  103.4 29.6 %collective-permute-start.18 = (bf16[2496,128]{1,0:T(8,128)(2,1)}, bf16[2496,128]{1,0:T(8,128)(2,1)}, u32[]{:S(2)}, u32[]{:S(2)}) collective-permute-start(bf16[2496,128]{1,0:T(8,128)(2,1)} %collective-permute-done.9.refs_0_), channel_id=1, source_target_pairs={{0,3},{1,2},{2,1},{3,0},{4,7},{5,6},{6,5},{7,4},{8,11},{9,10},{10,... | collective-permute-start | bytes 1916936 | tf_op jit(solution)/shard_map/ppermute | solution.py:63
  106.8 26.3 %all-to-all-start.3 = ((f32[8,2,4800]{2,1,0:T(2,128)}), f32[8,2,4800]{2,1,0:T(2,128)S(1)}, u32[]{:S(2)}, u32[]{:S(2)}) async-start(f32[8,2,4800]{2,1,0:T(2,128)} %reshape.33), calls=%async_computation.3 | async-start | bytes 622592 | tf_op jit(solution)/shard_map/all_to_all | solution.py:265
  110.3 1.1 copy-start.6
  119.5 1.7 copy-start.1
  134.2 26.7 %all-to-all-start.4 = ((f32[16,2,4800]{2,1,0:T(2,128)}), f32[16,2,4800]{2,1,0:T(2,128)}, u32[]{:S(2)}, u32[]{:S(2)}) async-start(f32[16,2,4800]{2,1,0:T(2,128)} %broadcast_in_dim.32), calls=%async_computation.4 | async-start | bytes 1245184 | tf_op jit(solution)/shard_map/all_to_all | solution.py:45
  138.4 22.5 %collective-permute-start.20 = (bf16[2496,128]{1,0:T(8,128)(2,1)}, bf16[2496,128]{1,0:T(8,128)(2,1)}, u32[]{:S(2)}, u32[]{:S(2)}) collective-permute-start(bf16[2496,128]{1,0:T(8,128)(2,1)} %collective-permute-done.16.refs_3_), channel_id=1, source_target_pairs={{4,0},{8,4},{12,8},{0,12},{5,1},{9,5},{13,9},{1,13},{6,2},{10,6},{... | collective-permute-start | bytes 1916936 | tf_op jit(solution)/shard_map/ppermute | solution.py:54
  144.8 50.5 %collective-permute-start.13 = (bf16[160,1024]{1,0:T(8,128)(2,1)}, bf16[160,1024]{1,0:T(8,128)(2,1)}, u32[]{:S(2)}, u32[]{:S(2)}) collective-permute-start(bf16[160,1024]{1,0:T(8,128)(2,1)} %get-tuple-element.64), channel_id=1, source_target_pairs={{0,1},{1,0},{2,3},{3,2},{4,5},{5,4},{6,7},{7,6},{8,9},{9,8},{10,11... | collective-permute-start | bytes 983048 | tf_op jit(solution)/shard_map/ppermute | solution.py:58
  149.9 1.9 copy-start.2
  158.5 1.7 copy-start.3
  162.2 1.9 copy-start.4
  167.4 1.2 copy-start.7
  169.2 29.8 %copy-start.10 = (f32[160,1024]{1,0:T(8,128)S(1)}, f32[160,1024]{1,0:T(8,128)}, u32[]{:S(2)}) copy-start(f32[160,1024]{1,0:T(8,128)} %copy-done.9) | copy-start | bytes 1966084
  169.2 29.8 %copy-start.20 = (f32[160,256]{1,0:T(8,128)S(1)}, f32[160,256]{1,0:T(8,128)}, u32[]{:S(2)}) copy-start(f32[160,256]{1,0:T(8,128)} %copy-done.19) | copy-start | bytes 491524
  169.2 17.9 %collective-permute-start.22 = (bf16[160,2496]{1,0:T(8,128)(2,1)}, bf16[160,2496]{1,0:T(8,128)(2,1)S(1)}, u32[]{:S(2)}, u32[]{:S(2)}) collective-permute-start(bf16[160,2496]{1,0:T(8,128)(2,1)} %get-tuple-element.88), channel_id=1, source_target_pairs={{0,1},{1,0},{2,3},{3,2},{4,5},{5,4},{6,7},{7,6},{8,9},{9,8},{10,11... | collective-permute-start | bytes 2396168 | tf_op jit(solution)/shard_map/ppermute | solution.py:58
  171.4 13.8 %all-to-all-start.5 = ((f32[8,2,4800]{2,1,0:T(2,128)}), f32[8,2,4800]{2,1,0:T(2,128)S(1)}, u32[]{:S(2)}, u32[]{:S(2)}) async-start(f32[8,2,4800]{2,1,0:T(2,128)} %broadcast_in_dim.33), calls=%async_computation.5 | async-start | bytes 622592 | tf_op jit(solution)/shard_map/all_to_all | solution.py:45
  180.6 14.8 %collective-permute-start.19 = (bf16[160,768]{1,0:T(8,128)(2,1)}, bf16[160,768]{1,0:T(8,128)(2,1)S(1)}, u32[]{:S(2)}, u32[]{:S(2)}) collective-permute-start(bf16[160,768]{1,0:T(8,128)(2,1)} %copy-done.21), channel_id=1, source_target_pairs={{0,1},{1,0},{2,3},{3,2},{4,5},{5,4},{6,7},{7,6},{8,9},{9,8},{10,11... | collective-permute-start | bytes 737288 | tf_op jit(solution)/shard_map/ppermute | solution.py:58
  188.1 13.8 %collective-permute-start.23 = (f32[16,4800]{1,0:T(8,128)}, f32[16,4800]{1,0:T(8,128)S(1)}, u32[]{:S(2)}, u32[]{:S(2)}) collective-permute-start(f32[16,4800]{1,0:T(8,128)} %reshape.35), channel_id=1, source_target_pairs={{0,16},{16,0},{1,17},{17,1},{2,18},{18,2},{3,19},{19,3},{4,20},{20... | collective-permute-start | bytes 921608 | tf_op jit(solution)/shard_map/ppermute | solution.py:49
  194.6 4.4 %collective-permute-start.21 = (bf16[160,256]{1,0:T(8,128)(2,1)S(1)}, bf16[160,256]{1,0:T(8,128)(2,1)S(1)}, u32[]{:S(2)}, u32[]{:S(2)}) collective-permute-start(bf16[160,256]{1,0:T(8,128)(2,1)S(1)} %get-tuple-element.85), channel_id=1, source_target_pairs={{0,1},{1,0},{2,3},{3,2},{4,5},{5,4},{6,7},{7,6},{8,9},{9,8},{10,11... | collective-permute-start | bytes 245768 | tf_op jit(solution)/shard_map/ppermute | solution.py:58
  201.9 2.7 %copy-start.8 = (f32[160,2496]{1,0:T(8,128)S(1)}, f32[160,2496]{1,0:T(8,128)}, u32[]{:S(2)}) copy-start(f32[160,2496]{1,0:T(8,128)} %copy-done.7) | copy-start | bytes 4792324
  203.1 2.2 %copy-start = (f32[1,150,4800]{2,1,0:T(8,128)S(1)}, f32[1,150,4800]{2,1,0:T(8,128)}, u32[]{:S(2)}) copy-start(f32[1,150,4800]{2,1,0:T(8,128)} %copy.71) | copy-start | bytes 8640004
  (14 other events, 12.0 us)

commit v6 on v5

--- a/solution.py
+++ b/solution.py
@@ -114,7 +114,7 @@
         out_shape=out,
         in_specs=[pl.BlockSpec(memory_space=pltpu.SMEM)] + [vmem] * (4 + len(flat)),
         out_specs=[vmem] * len(out),
-        compiler_params=pltpu.CompilerParams(vmem_limit_bytes=40 * 2**20),
+        compiler_params=pltpu.CompilerParams(vmem_limit_bytes=20 * 2**20),
     )(where, *pre, *weight, *flat)
 
 
@@ -139,12 +139,12 @@
         out_shape=jax.ShapeDtypeStruct((rows, pre.shape[1]), BF16),
         in_specs=[pl.BlockSpec(memory_space=pltpu.SMEM)] + [vmem] * (1 + 2 * len(halves)),
         out_specs=vmem,
-        compiler_params=pltpu.CompilerParams(vmem_limit_bytes=40 * 2**20),
+        compiler_params=pltpu.CompilerParams(vmem_limit_bytes=20 * 2**20),
     )(where, pre, *[x for pair in halves for x in pair])
 
 
 def finish(side, own_ref, came_ref, error_ref, left_ref, right_ref, out_ref):
-    rows, feat = error_ref.shape
+    rows, _, feat = error_ref.shape
     width = own_ref.shape[1]
     start = feat - width
     first = side[0] == 0
@@ -155,7 +155,7 @@
             at = slice(part.start - base, part.stop - base)
             mine, came = own_ref[:, at], came_ref[:, at].astype(F32)
             grad = jnp.where(first, mine, came) if turn else jnp.where(first, came, mine)
-            out_ref[:, part] = grad[:rows] + error_ref[:, part] - dot(left, right_ref[:, part], 1, 0)
+            out_ref[:, 0, part] = grad[:rows] + error_ref[:, 0, part] - dot(left, right_ref[:, part], 1, 0)
 
 
 def new_errors(side, own, came, error, left, right):
@@ -165,8 +165,27 @@
         out_shape=jax.ShapeDtypeStruct(error.shape, F32),
         in_specs=[pl.BlockSpec(memory_space=pltpu.SMEM)] + [vmem] * 5,
         out_specs=vmem,
-        compiler_params=pltpu.CompilerParams(vmem_limit_bytes=40 * 2**20),
+        compiler_params=pltpu.CompilerParams(vmem_limit_bytes=20 * 2**20),
     )(side, own, came, error, left, right)
+
+
+def right_rows(z_ref, og_ref, more_ref, out_ref):
+    rank, feat = out_ref.shape
+    z = z_ref[...]
+    for lo in range(0, feat, 512):
+        part = slice(lo, min(feat, lo + 512))
+        out_ref[:, part] = fold(dot(z, og_ref[part, :], 1, 1), 3) + more_ref[:, part]
+
+
+def right_factor(z3, og, more):
+    vmem = pl.BlockSpec(memory_space=pltpu.VMEM)
+    return pl.pallas_call(
+        right_rows,
+        out_shape=jax.ShapeDtypeStruct(more.shape, F32),
+        in_specs=[vmem] * 3,
+        out_specs=vmem,
+        compiler_params=pltpu.CompilerParams(vmem_limit_bytes=12 * 2**20),
+    )(z3, og, more)
 
 
 def tie(*values):
@@ -225,17 +244,20 @@
     b1 = around(b0)
     pre_two = (pre_pad, partner(pre_pad))
     w_two = (w_mine, partner(w_give))
+    a2 = beyond(*a1)
     y_all = y_all.transpose(1, 0, 2).reshape(rank, toks)
     y3 = jnp.concatenate(split(y_all, 3), axis=0)
     e2 = split(error, 2)
     p_err = sum(fold(dot(q3, e, 0, 1), 3) for e in e2)
     p_local = fold(dot(y3, act, 1, 1), 3) + p_err
-    p_local, b1, pre_two = tie(spread(p_local, "z"), b1, pre_two)
-    a2, b2 = beyond(*a1), beyond(*b1)
+    p_local, b1, a2, pre_two = tie(spread(p_local, "z"), b1, a2, pre_two)
+    b2 = beyond(*b1)
+    a3 = peer(a2[0])
     pbar = jnp.sum(p_local, axis=0)
     pbar = (pbar + other_core(pbar)) / groups
 
     l3 = jnp.concatenate(split(pbar, 3), axis=0)
+    r_error = sum(fold(dot(l3, e, 1, 0), 3) for e in e2)
     z_part = fold(dot(l3, act, 1, 0), 3)
     gram_part = jnp.dot(pbar, pbar.T, precision=hi)
     quarter = 128 // rank
@@ -247,38 +269,34 @@
         ],
         axis=1,
     )
-    sent, a2, w_two = tie(sent, a2, w_two)
-    a3 = peer(a2[0])
     keys = [[(0, 0), (0, 1), (0, -1), (1, 0)], [(0, 2), (1, 1), (1, -1)], [(1, 2)]]
     places = [spot(k) for k in keys]
     turns = [[x] for both in zip((a0,) + a1, (b0,) + b1) for x in both]
+    took, b2, w_two = tie(lax.all_to_all(sent, MP, 0, 0, tiled=True), b2, w_two)
+    b3 = shift(b2[1], "y", 1)
     keep_1, send_1, total = add_products(places[0], pre_two, w_two, turns, None)
-    took = lax.all_to_all(sent, MP, 0, 0, tiled=True)
     took = jnp.sum(took, axis=0)
     z = took[:rank]
     gram = jnp.concatenate(jnp.split(took[rank:], quarter, axis=1), axis=0)
 
     z3 = jnp.concatenate(split(z, 3), axis=0)
-    r_local = fold(dot(z3, out_grad, 1, 0), 3) + sum(fold(dot(l3, e, 1, 0), 3) for e in e2)
+    r_local = right_factor(z3, og, r_error)
     low, high = r_local[:half], r_local[half:]
     keep = jnp.where(core == 0, low, high) + other_core(jnp.where(core == 0, high, low))
     r_part = lax.all_to_all(keep.reshape(nz, half // nz, feat), "z", 0, 0, tiled=True)
-    r_part, b2, a3, total = tie(r_part, b2, a3, total)
-    b3 = shift(b2[1], "y", 1)
+    r_part, a3, b3, total, send_1 = tie(r_part, a3, b3, total, send_1)
     came_1 = partner(send_1)
     turns = [[x] for both in zip(a2, b2) for x in both]
     keep_2, send_2, total = add_products(places[1], pre_two, w_two, turns, total)
+    keep_3, send_3, grad_mine, grad_give = add_products(places[2], pre_two, w_two, [[a3], [b3]], total, True)
     r_part = jnp.sum(r_part, axis=0)
-    r_part, b3, total = tie(spread(r_part, MP), b3, total)
-    came_2 = partner(send_2)
-    keep_3, send_3, grad_mine, grad_give = add_products(places[2], pre_two, w_two, [[a3], [b3]], total, True)
-    r_part, grad_give, send_3 = tie(jnp.sum(r_part, axis=0) / groups, grad_give, send_3)
-    grad_came = partner(grad_give)
-    came_3 = partner(send_3)
-    mine, grad_came = tie(spread(r_part, "z"), grad_came)
-    mine = mine.reshape(half, feat)
+    r_part, grad_give, send_2, send_3 = tie(spread(r_part, MP), grad_give, send_2, send_3)
+    came_2, came_3, grad_came = partner(send_2), partner(send_3), partner(grad_give)
+    r_part = jnp.sum(r_part, axis=0) / groups
     halves = [(keep_1, came_1), (keep_2, came_2), (keep_3, came_3)]
     pre_grad = pre_grads(jnp.concatenate(places), pre_pad, hid, own, halves)
+    mine, grad_came, pre_grad = tie(spread(r_part, "z"), grad_came, pre_grad)
+    mine = mine.reshape(half, feat)
     theirs = other_core(mine)
     r_all = jnp.concatenate([jnp.where(core == 0, mine, theirs), jnp.where(core == 0, theirs, mine)], axis=0)
 
@@ -291,7 +309,8 @@
     qh, ql = split(q_t, 2)
     left = jnp.concatenate([ph, ph, pw], axis=0).T
     right = jnp.concatenate([qh, ql, qh], axis=0)
-    new_error = new_errors(side.reshape(1), grad_mine, grad_came, error, left, right)[None]
+    new_error = new_errors(side.reshape(1), grad_mine, grad_came, error[:, None], left, right)
+    new_error = new_error.transpose(1, 0, 2)
     return (pre_grad, new_error, q_t.T)
 
 

time: 212 us -> 198 us (0.934)
  local copies, waits for them, and re-layouts: 35.7 us -> 26.4 us
  waiting for transfers between devices: 43.6 us -> 34.8 us
  Pallas kernels: 17.3 us -> 23.3 us
  matrix products: 15.1 us -> 12.1 us
  other arithmetic: 19.6 us -> 22.6 us
    ppermute x5, waiting for transfers between devices: 18.8 us -> 0.01 us  [peer(): return lax.ppermute(x, 'x', [(i, n - 1 - i) for i in range(n)])]
    unnamed x72 -> x68, local copies, waits for them, and re-layouts: 29.3 us -> 17.4 us
    ppermute x7, waiting for transfers between devices: 7.42 us -> 15.1 us  [partner(): return lax.ppermute(x, 'x', [(i, i ^ 1) for i in range(lax.axis_size('x'))])]
    ppermute x9, waiting for transfers between devices: 1.36 us -> 7.36 us  [shift(): return lax.ppermute(x, axis, [((i + step) % n, i) for i in range(n)])]
    all_to_all x3, waiting for transfers between devices: 11.6 us -> 6.73 us  [spread(): lax.all_to_all(jnp.broadcast_to(x, (n,) + x.shape), axis, 0, 0, tiled=True)]
    pallas_call x1, Pallas kernels: 0.63 us -> 4.34 us  [new_errors(): pl.pallas_call(finish, out_shape=jax.ShapeDtypeStruct(error.shape, F32),...]
    all_to_all x3, starting transfers between devices: 12.9 us -> 16.1 us  [spread(): lax.all_to_all(jnp.broadcast_to(x, (n,) + x.shape), axis, 0, 0, tiled=True)]
    dot_general x8 -> x7, matrix products: 12.3 us -> 9.44 us  [dot(): lax.dot_general(a, b, (((ca,), (cb,)), ((), ())), preferred_element_type=...]
  transfers between devices with their start and end apart: 29 -> 29, of which waited for: 9 -> 9; matrix products, arithmetic and copies ran while one was open for 17% -> 17% of each run, Pallas kernels for 8% -> 9%
where the time goes in v6:
time: 198 us; the launch traced here: 197 us
  starting transfers between devices  58.9 us (30%)
  waiting for transfers between devices  34.8 us (18%)
  local copies, waits for them, and re-layouts  26.4 us (13%)
  Pallas kernels  23.3 us (12%)
  other arithmetic  22.6 us (11%)
  blocking collectives  17.3 us (9%)
  matrix products  12.1 us (6%)
    unnamed x68, local copies, waits for them, and re-layouts  17.4 us
    all_to_all x1, blocking collectives, spread(): lax.all_to_all(jnp.broadcast_to(x, (n,) + x.shape), axis, 0, 0, tiled=True)  17.3 us
    all_to_all x3, starting transfers between devices, spread(): lax.all_to_all(jnp.broadcast_to(x, (n,) + x.shape), axis, 0, 0, tiled=True)  16.1 us
    pallas_call x3, Pallas kernels, add_products(): pl.pallas_call(functools.partial(products, [len(b) for b in blocks], tota...  15.2 us
    ppermute x7, waiting for transfers between devices, partner(): return lax.ppermute(x, 'x', [(i, i ^ 1) for i in range(lax.axis_size('x'))])  15.1 us
    ppermute x3, starting transfers between devices, other_core(): return lax.ppermute(x, 'core', [(0, 1), (1, 0)])  11.9 us
    ppermute x9, starting transfers between devices, shift(): return lax.ppermute(x, axis, [((i + step) % n, i) for i in range(n)])  11.1 us
    dot_general x7, matrix products, dot(): lax.dot_general(a, b, (((ca,), (cb,)), ((), ())), preferred_element_type=...  9.44 us
  transfers between devices with their start and end apart: 29, of which 9 were waited for; matrix products, arithmetic and copies ran while one was open for 17% of the time, Pallas kernels for 9%

profile of v6, /device:TPU:1, one launch (start us, length us, event | category | flops | bytes accessed | tf_op | source)
XLA Modules:
  0.0 196.6 jit_solution(5368831504938829103)
XLA Ops:
  0.7 2.5 %broadcast_select_fusion.2 = (bf16[2496,128]{1,0:T(8,128)(2,1)}, bf16[2496,128]{1,0:T(8,128)(2,1)}) fusion(pred[]{:T(512)S(6)} %eq.5, bf16[4800,128]{1,0:T(8,128)(2,1)} %bitcast.64), kind=kLoop, calls=%fused_computation.27 | loop fusion | flops 638976 | bytes 2555905 | tf_op jit(solution)/shard_map/jit(_where)/select_n | solution.py:214
  3.2 3.6 %collective-permute-start.1 = (bf16[2496,128]{1,0:T(8,128)(2,1)}, bf16[2496,128]{1,0:T(8,128)(2,1)}, u32[]{:S(2)}, u32[]{:S(2)}) collective-permute-start(bf16[2496,128]{1,0:T(8,128)(2,1)} %get-tuple-element.64.refs_0_), channel_id=1, source_target_pairs={{4,0},{8,4},{12,8},{0,12},{5,1},{9,5},{13,9},{1,13},{6,2},{10,6},{... | collective-permute-start | bytes 1916936 | tf_op jit(solution)/shard_map/ppermute | solution.py:54
  6.8 2.5 %collective-permute-start.3 = (bf16[2496,128]{1,0:T(8,128)(2,1)}, bf16[2496,128]{1,0:T(8,128)(2,1)}, u32[]{:S(2)}, u32[]{:S(2)}) collective-permute-start(bf16[2496,128]{1,0:T(8,128)(2,1)} %get-tuple-element.64.refs_0_), channel_id=1, source_target_pairs={{0,3},{1,2},{2,1},{3,0},{4,7},{5,6},{6,5},{7,4},{8,11},{9,10},{10,... | collective-permute-start | bytes 1916936 | tf_op jit(solution)/shard_map/ppermute | solution.py:63
  10.6 5.2 %all-to-all-start = ((f32[16,32,128]{2,1,0:T(8,128)}), f32[16,32,128]{2,1,0:T(8,128)S(1)}, u32[]{:S(2)}, u32[]{:S(2)}) async-start(f32[16,32,128]{2,1,0:T(8,128)} %broadcast_in_dim.24), calls=%async_computation | async-start | bytes 524288 | tf_op jit(solution)/shard_map/all_to_all | solution.py:45
  15.9 3.6 %broadcast_select_fusion = (bf16[160,2496]{1,0:T(8,128)(2,1)}, bf16[160,2496]{1,0:T(8,128)(2,1)}) fusion(pred[]{:T(512)S(6)} %eq.5, bf16[150,4800]{1,0:T(8,128)(2,1)} %param.7, pred[2496]{0:T(1024)(128)(4,1)S(1)} %iota_compare_fusion.3), kind=kLoop, calls=%fused_computation.25 | loop fusion | flops 1597440 | bytes 3039937 | tf_op jit(solution)/shard_map/jit(_where)/select_n | solution.py:220
  20.4 1.5 fusion.33
  22.0 6.7 %all-to-all-done = f32[16,32,128]{2,1,0:T(8,128)S(1)} async-done(((f32[16,32,128]{2,1,0:T(8,128)}), f32[16,32,128]{2,1,0:T(8,128)S(1)}, u32[]{:S(2)}, u32[]{:S(2)}) %all-to-all-start) | async-done | bytes 262176 | tf_op jit(solution)/shard_map/all_to_all | solution.py:45
  30.3 1.7 fusion.19
  32.0 1.6 collective-permute-start.6
  33.6 2.7 %collective-permute-start.7 = (bf16[2496,128]{1,0:T(8,128)(2,1)}, bf16[2496,128]{1,0:T(8,128)(2,1)}, u32[]{:S(2)}, u32[]{:S(2)}) collective-permute-start(bf16[2496,128]{1,0:T(8,128)(2,1)} %collective-permute-done.1.refs_2_), channel_id=1, source_target_pairs={{4,0},{8,4},{12,8},{0,12},{5,1},{9,5},{13,9},{1,13},{6,2},{10,6},{... | collective-permute-start | bytes 1916936 | tf_op jit(solution)/shard_map/ppermute | solution.py:54
  36.4 5.9 %collective-permute-done.4.refs_3_ = bf16[2496,128]{1,0:T(8,128)(2,1)S(1)} collective-permute-done((bf16[2496,128]{1,0:T(8,128)(2,1)}, bf16[2496,128]{1,0:T(8,128)(2,1)S(1)}, u32[]{:S(2)}, u32[]{:S(2)}) %collective-permute-start.4) | collective-permute-done | bytes 639008 | tf_op jit(solution)/shard_map/ppermute | solution.py:54
  42.4 1.4 collective-permute-done.5.refs_5_
  44.9 17.3 %all_to_all.30 = f32[8,32,150]{2,1,0:T(8,128)S(1)} all-to-all(f32[8,32,150]{2,1,0:T(8,128)S(1)} %broadcast_in_dim.27), channel_id=1, replica_groups=mesh['z'=8,'core'=2,'y'=4,'x'=4] {'z'}, dimensions={0} | all-to-all | bytes 307200 | tf_op jit(solution)/shard_map/all_to_all | solution.py:45
  62.3 7.4 %collective-permute-start.11 = (f32[32,150]{1,0:T(8,128)S(1)}, f32[32,150]{1,0:T(8,128)S(1)}, u32[]{:S(2)}, u32[]{:S(2)}) collective-permute-start(f32[32,150]{1,0:T(8,128)S(1)} %reduce_sum.36), channel_id=1, source_target_pairs={{0,16},{16,0},{1,17},{17,1},{2,18},{18,2},{3,19},{19,3},{4,20},{20... | collective-permute-start | bytes 57608 | tf_op jit(solution)/shard_map/ppermute | solution.py:49
  69.7 1.3 collective-permute-start.15
  71.0 2.5 %collective-permute-start.12 = (bf16[2496,128]{1,0:T(8,128)(2,1)}, bf16[2496,128]{1,0:T(8,128)(2,1)}, u32[]{:S(2)}, u32[]{:S(2)}) collective-permute-start(bf16[2496,128]{1,0:T(8,128)(2,1)} %copy-done.11), channel_id=1, source_target_pairs={{4,0},{8,4},{12,8},{0,12},{5,1},{9,5},{13,9},{1,13},{6,2},{10,6},{... | collective-permute-start | bytes 1916936 | tf_op jit(solution)/shard_map/ppermute | solution.py:54
  73.5 1.3 collective-permute-start.13
  75.6 1.7 fusion.45
  77.3 1.7 fusion.18
  79.0 1.7 fusion.31
  81.7 5.2 %all-to-all-start.2 = ((f32[16,40,128]{2,1,0:T(8,128)}), f32[16,40,128]{2,1,0:T(8,128)}, u32[]{:S(2)}, u32[]{:S(2)}) async-start(f32[16,40,128]{2,1,0:T(8,128)} %pad_maximum_fusion.2), calls=%async_computation.2 | async-start | bytes 655360 | tf_op jit(solution)/shard_map/all_to_all | solution.py:275
  86.9 2.2 %fusion.13.more_ref = f32[32,4800]{1,0:T(8,128)S(1)} fusion(f32[96,4800]{1,0:T(8,128)} %fusion.31, f32[96,4800]{1,0:T(8,128)} %fusion.18), kind=kLoop, calls=%fused_computation.34 | loop fusion | flops 768000 | bytes 4300800 | tf_op jit(solution)/shard_map/add | solution.py:260
  89.8 5.3 %all-to-all-done.2 = f32[16,40,128]{2,1,0:T(8,128)} async-done(((f32[16,40,128]{2,1,0:T(8,128)}), f32[16,40,128]{2,1,0:T(8,128)}, u32[]{:S(2)}, u32[]{:S(2)}) %all-to-all-start.2) | async-done | bytes 327712 | tf_op jit(solution)/shard_map/all_to_all | solution.py:275
  95.1 1.6 reduce_sum.37
  97.4 1.3 copy-done.4
  99.3 2.5 %collective-permute-start.16 = (f32[16,4800]{1,0:T(8,128)S(1)}, f32[16,4800]{1,0:T(8,128)S(1)}, u32[]{:S(2)}, u32[]{:S(2)}) collective-permute-start(f32[16,4800]{1,0:T(8,128)S(1)} %slice_select_fusion), channel_id=1, source_target_pairs={{0,16},{16,0},{1,17},{17,1},{2,18},{18,2},{3,19},{19,3},{4,20},{20... | collective-permute-start | bytes 921608 | tf_op jit(solution)/shard_map/ppermute | solution.py:49
  104.3 4.1 %all-to-all-start.3 = ((f32[8,2,4800]{2,1,0:T(2,128)}), f32[8,2,4800]{2,1,0:T(2,128)}, u32[]{:S(2)}, u32[]{:S(2)}) async-start(f32[8,2,4800]{2,1,0:T(2,128)} %reshape.33), calls=%async_computation.3 | async-start | bytes 622592 | tf_op jit(solution)/shard_map/all_to_all | solution.py:286
  108.8 1.1 copy-done.1
  112.1 6.5 %shard_map.77 = (f32[160,1024]{1,0:T(8,128)S(1)}, bf16[160,1024]{1,0:T(8,128)(2,1)S(1)}, f32[320,2496]{1,0:T(8,128)S(1)}) custom-call(s32[8]{0:T(128)S(1)} %stack.65.where, bf16[160,2048]{1,0:T(8,128)(2,1)} %pad.8.pre_a.pre_ref, bf16[160,2048]{1,0:T(8,128)(2,1)} %collective-permute-done.10.pre_b, bf16[160,2496]{1,0:T(8,128)(2,1)S(1)} %copy-done.1, ...), custom_call_target="tpu_custom_call" | custom-call | tf_op jit(solution)/shard_map/pallas_call | solution.py:112
  118.6 1.7 copy-done.5
  123.3 4.5 %all-to-all-start.4 = ((f32[16,2,4800]{2,1,0:T(2,128)}), f32[16,2,4800]{2,1,0:T(2,128)}, u32[]{:S(2)}, u32[]{:S(2)}) async-start(f32[16,2,4800]{2,1,0:T(2,128)} %broadcast_in_dim.29), calls=%async_computation.4 | async-start | bytes 1245184 | tf_op jit(solution)/shard_map/all_to_all | solution.py:45
  128.4 2.9 %cholesky.17 = f32[32,32]{1,0:T(8,128)S(1)} custom-call(f32[32,32]{1,0:T(8,128)S(1)} %fusion.42), custom_call_target="Cholesky" | custom-call | tf_op jit(solution)/shard_map/jit(cholesky)/cholesky | solution.py:303
  133.2 1.9 copy-done.6
  135.2 5.7 %shard_map.78 = (f32[160,768]{1,0:T(8,128)S(1)}, bf16[160,768]{1,0:T(8,128)(2,1)S(1)}, f32[320,2496]{1,0:T(8,128)S(1)}) custom-call(s32[6]{0:T(128)S(1)} %stack.75.where, bf16[160,2048]{1,0:T(8,128)(2,1)} %pad.8.pre_a.pre_ref, bf16[160,2048]{1,0:T(8,128)(2,1)} %collective-permute-done.10.pre_b, bf16[160,2496]{1,0:T(8,128)(2,1)S(1)} %copy-done.2, ...), custom_call_target="tpu_custom_call" | custom-call | tf_op jit(solution)/shard_map/pallas_call | solution.py:112
  141.6 3.0 %shard_map.79 = (f32[160,256]{1,0:T(8,128)S(1)}, bf16[160,256]{1,0:T(8,128)(2,1)S(1)}, f32[160,2496]{1,0:T(8,128)S(1)}, bf16[160,2496]{1,0:T(8,128)(2,1)S(1)}) custom-call(s32[2]{0:T(128)S(1)} %pad_add_fusion.where, bf16[160,2048]{1,0:T(8,128)(2,1)} %pad.8.pre_a.pre_ref, bf16[160,2048]{1,0:T(8,128)(2,1)} %collective-permute-done.10.pre_b, ...), custom_call_target="tpu_custom_call" | custom-call | tf_op jit(solution)/shard_map/pallas_call | solution.py:112
  144.6 1.2 copy-done.7
  149.0 1.3 reduce_sum.39
  151.1 6.4 %all-to-all-start.5 = ((f32[8,2,4800]{2,1,0:T(2,128)}), f32[8,2,4800]{2,1,0:T(2,128)}, u32[]{:S(2)}, u32[]{:S(2)}) async-start(f32[8,2,4800]{2,1,0:T(2,128)} %broadcast_in_dim.30), calls=%async_computation.5 | async-start | bytes 622592 | tf_op jit(solution)/shard_map/all_to_all | solution.py:45
  158.2 2.4 %custom-call.7 = f32[1,32,32]{1,2,0:T(8,128)S(1)} custom-call(f32[1,32,32]{2,1,0:T(8,128)S(1)} %fusion.37), custom_call_target="InvertDiagBlocksLowerTriangular" | custom-call | tf_op jit(solution)/shard_map/jit(_solve_triangular)/triangular_solve | solution.py:304
  163.6 1.5 copy.38
  165.1 1.5 copy.39
  166.6 7.4 %collective-permute-done.20.refs_1_ = bf16[160,1024]{1,0:T(8,128)(2,1)} collective-permute-done((bf16[160,1024]{1,0:T(8,128)(2,1)}, bf16[160,1024]{1,0:T(8,128)(2,1)}, u32[]{:S(2)}, u32[]{:S(2)}) %collective-permute-start.20) | collective-permute-done | bytes 327712 | tf_op jit(solution)/shard_map/ppermute | solution.py:58
  174.0 7.0 %collective-permute-done.22.refs_5_ = bf16[160,256]{1,0:T(8,128)(2,1)S(1)} collective-permute-done((bf16[160,256]{1,0:T(8,128)(2,1)}, bf16[160,256]{1,0:T(8,128)(2,1)S(1)}, u32[]{:S(2)}, u32[]{:S(2)}) %collective-permute-start.22) | collective-permute-done | bytes 81952 | tf_op jit(solution)/shard_map/ppermute | solution.py:58
  183.0 3.2 %shard_map.80 = bf16[150,2048]{1,0:T(8,128)(2,1)} custom-call(s32[16]{0:T(128)S(1)} %concatenate.40.where, bf16[160,2048]{1,0:T(8,128)(2,1)} %pad.8.pre_a.pre_ref, f32[160,1024]{1,0:T(8,128)S(1)} %copy-done.10, bf16[160,1024]{1,0:T(8,128)(2,1)} %collective-permute-done.20.refs_1_, f32[160,768]{1,0:T(8,128)S(1)} %get-tuple-element.85.refs_2_, ...), custom_call_target="tpu_custom_call" | custom-call | tf_op jit(solution)/shard_map/pallas_call | solution.py:137
  186.2 1.2 reshape.35
  187.4 1.9 collective-permute-start.23
  190.6 1.5 fusion.12
  192.2 4.3 %shard_map.81 = f32[150,1,4800]{2,1,0:T(1,128)} custom-call(s32[1]{0:T(128)} %bitcast.19.side, f32[160,2496]{1,0:T(8,128)S(1)} %copy-done.8, bf16[160,2496]{1,0:T(8,128)(2,1)} %collective-permute-done.19.came_ref, f32[150,1,4800]{2,1,0:T(1,128)S(1)} %bitcast.63, bf16[150,96]{1,0:T(8,128)(2,1)S(1)} %maximum_bitcast_fusion.left_ref, ...), custom_call_target="tpu_custom_call" | custom-call | tf_op jit(solution)/shard_map/pallas_call | solution.py:163
  (147 shorter events, 31.0 us)
Async XLA Ops:
  0.6 8.6 %copy-start.23 = (f32[4800,32]{0,1:T(8,128)S(1)}, f32[4800,32]{0,1:T(8,128)}, u32[]{:S(2)}) copy-start(f32[4800,32]{0,1:T(8,128)} %param.9) | copy-start | bytes 1843204
  0.7 8.8 %copy-start.3 = (bf16[128,4800]{0,1:T(8,128)(2,1)S(1)}, bf16[128,4800]{0,1:T(8,128)(2,1)}, u32[]{:S(2)}) copy-start(bf16[128,4800]{0,1:T(8,128)(2,1)} %param.6) | copy-start | bytes 3686404
  3.2 25.5 %collective-permute-start.1 = (bf16[2496,128]{1,0:T(8,128)(2,1)}, bf16[2496,128]{1,0:T(8,128)(2,1)}, u32[]{:S(2)}, u32[]{:S(2)}) collective-permute-start(bf16[2496,128]{1,0:T(8,128)(2,1)} %get-tuple-element.64.refs_0_), channel_id=1, source_target_pairs={{4,0},{8,4},{12,8},{0,12},{5,1},{9,5},{13,9},{1,13},{6,2},{10,6},{... | collective-permute-start | bytes 1916936 | tf_op jit(solution)/shard_map/ppermute | solution.py:54
  6.7 22.0 %collective-permute-start.2 = (bf16[2496,128]{1,0:T(8,128)(2,1)}, bf16[2496,128]{1,0:T(8,128)(2,1)}, u32[]{:S(2)}, u32[]{:S(2)}) collective-permute-start(bf16[2496,128]{1,0:T(8,128)(2,1)} %get-tuple-element.64.refs_0_), channel_id=1, source_target_pairs={{12,0},{0,4},{4,8},{8,12},{13,1},{1,5},{5,9},{9,13},{14,2},{2,6},{... | collective-permute-start | bytes 1916936 | tf_op jit(solution)/shard_map/ppermute | solution.py:54
  6.8 22.0 %collective-permute-start.3 = (bf16[2496,128]{1,0:T(8,128)(2,1)}, bf16[2496,128]{1,0:T(8,128)(2,1)}, u32[]{:S(2)}, u32[]{:S(2)}) collective-permute-start(bf16[2496,128]{1,0:T(8,128)(2,1)} %get-tuple-element.64.refs_0_), channel_id=1, source_target_pairs={{0,3},{1,2},{2,1},{3,0},{4,7},{5,6},{6,5},{7,4},{8,11},{9,10},{10,... | collective-permute-start | bytes 1916936 | tf_op jit(solution)/shard_map/ppermute | solution.py:63
  9.2 19.5 %collective-permute-start = (bf16[2496,128]{1,0:T(8,128)(2,1)}, bf16[2496,128]{1,0:T(8,128)(2,1)}, u32[]{:S(2)}, u32[]{:S(2)}) collective-permute-start(bf16[2496,128]{1,0:T(8,128)(2,1)} %get-tuple-element.97), channel_id=1, source_target_pairs={{0,1},{1,0},{2,3},{3,2},{4,5},{5,4},{6,7},{7,6},{8,9},{9,8},{10,11... | collective-permute-start | bytes 1916936 | tf_op jit(solution)/shard_map/ppermute | solution.py:58
  9.4 1.2 copy-start.26
  9.4 1.2 copy-start.28
  9.4 1.2 copy-start.30
  10.6 18.1 %all-to-all-start = ((f32[16,32,128]{2,1,0:T(8,128)}), f32[16,32,128]{2,1,0:T(8,128)S(1)}, u32[]{:S(2)}, u32[]{:S(2)}) async-start(f32[16,32,128]{2,1,0:T(8,128)} %broadcast_in_dim.24), calls=%async_computation | async-start | bytes 524288 | tf_op jit(solution)/shard_map/all_to_all | solution.py:45
  15.8 3.7 %copy-start.24 = (bf16[150,2048]{1,0:T(8,128)(2,1)S(1)}, bf16[150,2048]{1,0:T(8,128)(2,1)}, u32[]{:S(2)}) copy-start(bf16[150,2048]{1,0:T(8,128)(2,1)} %param.5) | copy-start | bytes 1843204
  15.8 4.6 %copy-start = (f32[1,150,4800]{2,0,1:T(1,128)S(1)}, f32[1,150,4800]{2,0,1:T(1,128)}, u32[]{:S(2)}) copy-start(f32[1,150,4800]{2,0,1:T(1,128)} %param.8) | copy-start | bytes 8640004
  15.8 4.6 %copy-start.27 = (bf16[4800,32]{0,1:T(8,128)(2,1)S(1)}, bf16[4800,32]{0,1:T(8,128)(2,1)}, u32[]{:S(2)}) copy-start(bf16[4800,32]{0,1:T(8,128)(2,1)} %copy-done.26) | copy-start | bytes 921604
  15.9 4.6 %copy-start.29 = (bf16[4800,32]{0,1:T(8,128)(2,1)S(1)}, bf16[4800,32]{0,1:T(8,128)(2,1)}, u32[]{:S(2)}) copy-start(bf16[4800,32]{0,1:T(8,128)(2,1)} %copy-done.28) | copy-start | bytes 921604
  28.7 15.0 %copy-start.25 = (bf16[150,2048]{1,0:T(8,128)(2,1)S(1)}, bf16[150,2048]{1,0:T(8,128)(2,1)}, u32[]{:S(2)}) copy-start(bf16[150,2048]{1,0:T(8,128)(2,1)} %param.5) | copy-start | bytes 1843204
  28.7 13.6 %collective-permute-start.4 = (bf16[2496,128]{1,0:T(8,128)(2,1)}, bf16[2496,128]{1,0:T(8,128)(2,1)S(1)}, u32[]{:S(2)}, u32[]{:S(2)}) collective-permute-start(bf16[2496,128]{1,0:T(8,128)(2,1)} %collective-permute-done.refs_1_), channel_id=1, source_target_pairs={{4,0},{8,4},{12,8},{0,12},{5,1},{9,5},{13,9},{1,13},{6,2},{10,6},{... | collective-permute-start | bytes 1916936 | tf_op jit(solution)/shard_map/ppermute | solution.py:54
  29.1 14.6 %collective-permute-start.5 = (bf16[2496,128]{1,0:T(8,128)(2,1)}, bf16[2496,128]{1,0:T(8,128)(2,1)S(1)}, u32[]{:S(2)}, u32[]{:S(2)}) collective-permute-start(bf16[2496,128]{1,0:T(8,128)(2,1)} %collective-permute-done.refs_1_), channel_id=1, source_target_pairs={{12,0},{0,4},{4,8},{8,12},{13,1},{1,5},{5,9},{9,13},{14,2},{2,6},{... | collective-permute-start | bytes 1916936 | tf_op jit(solution)/shard_map/ppermute | solution.py:54
  32.0 30.2 %collective-permute-start.6 = (bf16[2496,128]{1,0:T(8,128)(2,1)}, bf16[2496,128]{1,0:T(8,128)(2,1)}, u32[]{:S(2)}, u32[]{:S(2)}) collective-permute-start(bf16[2496,128]{1,0:T(8,128)(2,1)} %collective-permute-done.refs_1_), channel_id=1, source_target_pairs={{0,3},{1,2},{2,1},{3,0},{4,7},{5,6},{6,5},{7,4},{8,11},{9,10},{10,... | collective-permute-start | bytes 1916936 | tf_op jit(solution)/shard_map/ppermute | solution.py:63
  33.6 28.6 %collective-permute-start.7 = (bf16[2496,128]{1,0:T(8,128)(2,1)}, bf16[2496,128]{1,0:T(8,128)(2,1)}, u32[]{:S(2)}, u32[]{:S(2)}) collective-permute-start(bf16[2496,128]{1,0:T(8,128)(2,1)} %collective-permute-done.1.refs_2_), channel_id=1, source_target_pairs={{4,0},{8,4},{12,8},{0,12},{5,1},{9,5},{13,9},{1,13},{6,2},{10,6},{... | collective-permute-start | bytes 1916936 | tf_op jit(solution)/shard_map/ppermute | solution.py:54
  36.3 26.0 %collective-permute-start.8 = (bf16[2496,128]{1,0:T(8,128)(2,1)}, bf16[2496,128]{1,0:T(8,128)(2,1)}, u32[]{:S(2)}, u32[]{:S(2)}) collective-permute-start(bf16[2496,128]{1,0:T(8,128)(2,1)} %collective-permute-done.1.refs_2_), channel_id=1, source_target_pairs={{0,3},{1,2},{2,1},{3,0},{4,7},{5,6},{6,5},{7,4},{8,11},{9,10},{10,... | collective-permute-start | bytes 1916936 | tf_op jit(solution)/shard_map/ppermute | solution.py:63
  42.3 2.0 %copy-start.11 = (bf16[2496,128]{1,0:T(8,128)(2,1)}, bf16[2496,128]{1,0:T(8,128)(2,1)S(1)}, u32[]{:S(2)}) copy-start(bf16[2496,128]{1,0:T(8,128)(2,1)S(1)} %collective-permute-done.4.refs_3_) | copy-start | bytes 1916932
  42.3 19.9 %collective-permute-start.10 = (bf16[160,2048]{1,0:T(8,128)(2,1)}, bf16[160,2048]{1,0:T(8,128)(2,1)}, u32[]{:S(2)}, u32[]{:S(2)}) collective-permute-start(bf16[160,2048]{1,0:T(8,128)(2,1)} %pad.8.pre_a.pre_ref), channel_id=1, source_target_pairs={{0,1},{1,0},{2,3},{3,2},{4,5},{5,4},{6,7},{7,6},{8,9},{9,8},{10,11... | collective-permute-start | bytes 1966088 | tf_op jit(solution)/shard_map/ppermute | solution.py:58
  43.8 18.5 %collective-permute-start.9 = (bf16[2496,128]{1,0:T(8,128)(2,1)}, bf16[2496,128]{1,0:T(8,128)(2,1)}, u32[]{:S(2)}, u32[]{:S(2)}) collective-permute-start(bf16[2496,128]{1,0:T(8,128)(2,1)} %collective-permute-done.3.refs_6_), channel_id=1, source_target_pairs={{12,0},{0,4},{4,8},{8,12},{13,1},{1,5},{5,9},{9,13},{14,2},{2,6},{... | collective-permute-start | bytes 1916936 | tf_op jit(solution)/shard_map/ppermute | solution.py:54
  62.3 12.5 %collective-permute-start.11 = (f32[32,150]{1,0:T(8,128)S(1)}, f32[32,150]{1,0:T(8,128)S(1)}, u32[]{:S(2)}, u32[]{:S(2)}) collective-permute-start(f32[32,150]{1,0:T(8,128)S(1)} %reduce_sum.36), channel_id=1, source_target_pairs={{0,16},{16,0},{1,17},{17,1},{2,18},{18,2},{3,19},{19,3},{4,20},{20... | collective-permute-start | bytes 57608 | tf_op jit(solution)/shard_map/ppermute | solution.py:49
  69.7 20.1 %collective-permute-start.15 = (bf16[160,2496]{1,0:T(8,128)(2,1)}, bf16[160,2496]{1,0:T(8,128)(2,1)}, u32[]{:S(2)}, u32[]{:S(2)}) collective-permute-start(bf16[160,2496]{1,0:T(8,128)(2,1)} %get-tuple-element.56), channel_id=1, source_target_pairs={{0,1},{1,0},{2,3},{3,2},{4,5},{5,4},{6,7},{7,6},{8,9},{9,8},{10,11... | collective-permute-start | bytes 2396168 | tf_op jit(solution)/shard_map/ppermute | solution.py:58
  71.0 24.1 %collective-permute-start.12 = (bf16[2496,128]{1,0:T(8,128)(2,1)}, bf16[2496,128]{1,0:T(8,128)(2,1)}, u32[]{:S(2)}, u32[]{:S(2)}) collective-permute-start(bf16[2496,128]{1,0:T(8,128)(2,1)} %copy-done.11), channel_id=1, source_target_pairs={{4,0},{8,4},{12,8},{0,12},{5,1},{9,5},{13,9},{1,13},{6,2},{10,6},{... | collective-permute-start | bytes 1916936 | tf_op jit(solution)/shard_map/ppermute | solution.py:54
  73.5 21.5 %collective-permute-start.13 = (bf16[2496,128]{1,0:T(8,128)(2,1)}, bf16[2496,128]{1,0:T(8,128)(2,1)}, u32[]{:S(2)}, u32[]{:S(2)}) collective-permute-start(bf16[2496,128]{1,0:T(8,128)(2,1)} %copy-done.11), channel_id=1, source_target_pairs={{0,3},{1,2},{2,1},{3,0},{4,7},{5,6},{6,5},{7,4},{8,11},{9,10},{10,... | collective-permute-start | bytes 1916936 | tf_op jit(solution)/shard_map/ppermute | solution.py:63
  74.8 20.3 %collective-permute-start.14 = (bf16[2496,128]{1,0:T(8,128)(2,1)}, bf16[2496,128]{1,0:T(8,128)(2,1)}, u32[]{:S(2)}, u32[]{:S(2)}) collective-permute-start(bf16[2496,128]{1,0:T(8,128)(2,1)} %collective-permute-done.6.refs_7_), channel_id=1, source_target_pairs={{12,0},{0,4},{4,8},{8,12},{13,1},{1,5},{5,9},{9,13},{14,2},{2,6},{... | collective-permute-start | bytes 1916936 | tf_op jit(solution)/shard_map/ppermute | solution.py:54
  81.7 13.4 %all-to-all-start.2 = ((f32[16,40,128]{2,1,0:T(8,128)}), f32[16,40,128]{2,1,0:T(8,128)}, u32[]{:S(2)}, u32[]{:S(2)}) async-start(f32[16,40,128]{2,1,0:T(8,128)} %pad_maximum_fusion.2), calls=%async_computation.2 | async-start | bytes 655360 | tf_op jit(solution)/shard_map/all_to_all | solution.py:275
  97.4 1.3 copy-start.4
  99.3 4.1 %collective-permute-start.16 = (f32[16,4800]{1,0:T(8,128)S(1)}, f32[16,4800]{1,0:T(8,128)S(1)}, u32[]{:S(2)}, u32[]{:S(2)}) collective-permute-start(f32[16,4800]{1,0:T(8,128)S(1)} %slice_select_fusion), channel_id=1, source_target_pairs={{0,16},{16,0},{1,17},{17,1},{2,18},{18,2},{3,19},{19,3},{4,20},{20... | collective-permute-start | bytes 921608 | tf_op jit(solution)/shard_map/ppermute | solution.py:49
  101.8 19.2 %collective-permute-start.17 = (bf16[2496,128]{1,0:T(8,128)(2,1)}, bf16[2496,128]{1,0:T(8,128)(2,1)}, u32[]{:S(2)}, u32[]{:S(2)}) collective-permute-start(bf16[2496,128]{1,0:T(8,128)(2,1)} %collective-permute-done.7.refs_0_), channel_id=1, source_target_pairs={{0,3},{1,2},{2,1},{3,0},{4,7},{5,6},{6,5},{7,4},{8,11},{9,10},{10,... | collective-permute-start | bytes 1916936 | tf_op jit(solution)/shard_map/ppermute | solution.py:63
  102.6 18.4 %collective-permute-start.18 = (bf16[2496,128]{1,0:T(8,128)(2,1)}, bf16[2496,128]{1,0:T(8,128)(2,1)}, u32[]{:S(2)}, u32[]{:S(2)}) collective-permute-start(bf16[2496,128]{1,0:T(8,128)(2,1)} %collective-permute-done.13.refs_3_), channel_id=1, source_target_pairs={{4,0},{8,4},{12,8},{0,12},{5,1},{9,5},{13,9},{1,13},{6,2},{10,6},{... | collective-permute-start | bytes 1916936 | tf_op jit(solution)/shard_map/ppermute | solution.py:54
  104.3 16.9 %all-to-all-start.3 = ((f32[8,2,4800]{2,1,0:T(2,128)}), f32[8,2,4800]{2,1,0:T(2,128)}, u32[]{:S(2)}, u32[]{:S(2)}) async-start(f32[8,2,4800]{2,1,0:T(2,128)} %reshape.33), calls=%async_computation.3 | async-start | bytes 622592 | tf_op jit(solution)/shard_map/all_to_all | solution.py:286
  118.5 1.7 copy-start.5
  121.0 10.3 %copy-start.18 = (bf16[160,1024]{1,0:T(8,128)(2,1)}, bf16[160,1024]{1,0:T(8,128)(2,1)S(1)}, u32[]{:S(2)}) copy-start(bf16[160,1024]{1,0:T(8,128)(2,1)S(1)} %get-tuple-element.84) | copy-start | bytes 983044
  121.0 6.7 %copy-start.31 = (f32[40,128]{1,0:T(8,128)S(1)}, f32[40,128]{1,0:T(8,128)}, u32[]{:S(2)}) copy-start(f32[40,128]{1,0:T(8,128)} %reduce_sum.37) | copy-start | bytes 61444
  123.3 24.7 %all-to-all-start.4 = ((f32[16,2,4800]{2,1,0:T(2,128)}), f32[16,2,4800]{2,1,0:T(2,128)}, u32[]{:S(2)}, u32[]{:S(2)}) async-start(f32[16,2,4800]{2,1,0:T(2,128)} %broadcast_in_dim.29), calls=%async_computation.4 | async-start | bytes 1245184 | tf_op jit(solution)/shard_map/all_to_all | solution.py:45
  133.2 1.9 copy-start.6
  141.5 21.3 %copy-start.22 = (f32[32,150]{1,0:T(8,128)S(1)}, f32[32,150]{1,0:T(8,128)}, u32[]{:S(2)}) copy-start(f32[32,150]{1,0:T(8,128)} %copy-done.21) | copy-start | bytes 57604
  144.6 1.2 copy-start.7
  148.0 38.3 %collective-permute-start.19 = (bf16[160,2496]{1,0:T(8,128)(2,1)}, bf16[160,2496]{1,0:T(8,128)(2,1)}, u32[]{:S(2)}, u32[]{:S(2)}) collective-permute-start(bf16[160,2496]{1,0:T(8,128)(2,1)} %copy-done.17), channel_id=1, source_target_pairs={{0,1},{1,0},{2,3},{3,2},{4,5},{5,4},{6,7},{7,6},{8,9},{9,8},{10,11... | collective-permute-start | bytes 2396168 | tf_op jit(solution)/shard_map/ppermute | solution.py:58
  151.1 35.1 %all-to-all-start.5 = ((f32[8,2,4800]{2,1,0:T(2,128)}), f32[8,2,4800]{2,1,0:T(2,128)}, u32[]{:S(2)}, u32[]{:S(2)}) async-start(f32[8,2,4800]{2,1,0:T(2,128)} %broadcast_in_dim.30), calls=%async_computation.5 | async-start | bytes 622592 | tf_op jit(solution)/shard_map/all_to_all | solution.py:45
  160.6 13.4 %collective-permute-start.20 = (bf16[160,1024]{1,0:T(8,128)(2,1)}, bf16[160,1024]{1,0:T(8,128)(2,1)}, u32[]{:S(2)}, u32[]{:S(2)}) collective-permute-start(bf16[160,1024]{1,0:T(8,128)(2,1)} %copy-done.18), channel_id=1, source_target_pairs={{0,1},{1,0},{2,3},{3,2},{4,5},{5,4},{6,7},{7,6},{8,9},{9,8},{10,11... | collective-permute-start | bytes 983048 | tf_op jit(solution)/shard_map/ppermute | solution.py:58
  161.2 19.9 %collective-permute-start.21 = (bf16[160,768]{1,0:T(8,128)(2,1)}, bf16[160,768]{1,0:T(8,128)(2,1)}, u32[]{:S(2)}, u32[]{:S(2)}) collective-permute-start(bf16[160,768]{1,0:T(8,128)(2,1)} %copy-done.19), channel_id=1, source_target_pairs={{0,1},{1,0},{2,3},{3,2},{4,5},{5,4},{6,7},{7,6},{8,9},{9,8},{10,11... | collective-permute-start | bytes 737288 | tf_op jit(solution)/shard_map/ppermute | solution.py:58
  162.3 18.7 %collective-permute-start.22 = (bf16[160,256]{1,0:T(8,128)(2,1)}, bf16[160,256]{1,0:T(8,128)(2,1)S(1)}, u32[]{:S(2)}, u32[]{:S(2)}) collective-permute-start(bf16[160,256]{1,0:T(8,128)(2,1)} %copy-done.20), channel_id=1, source_target_pairs={{0,1},{1,0},{2,3},{3,2},{4,5},{5,4},{6,7},{7,6},{8,9},{9,8},{10,11... | collective-permute-start | bytes 245768 | tf_op jit(solution)/shard_map/ppermute | solution.py:58
  187.4 3.2 %collective-permute-start.23 = (f32[16,4800]{1,0:T(8,128)S(1)}, f32[16,4800]{1,0:T(8,128)S(1)}, u32[]{:S(2)}, u32[]{:S(2)}) collective-permute-start(f32[16,4800]{1,0:T(8,128)S(1)} %reshape.35), channel_id=1, source_target_pairs={{0,16},{16,0},{1,17},{17,1},{2,18},{18,2},{3,19},{19,3},{4,20},{20... | collective-permute-start | bytes 921608 | tf_op jit(solution)/shard_map/ppermute | solution.py:49
  190.6 1.6 copy-start.8
  (13 other events, 11.6 us)

commit v7 on v6

--- a/solution.py
+++ b/solution.py
@@ -114,7 +114,7 @@
         out_shape=out,
         in_specs=[pl.BlockSpec(memory_space=pltpu.SMEM)] + [vmem] * (4 + len(flat)),
         out_specs=[vmem] * len(out),
-        compiler_params=pltpu.CompilerParams(vmem_limit_bytes=20 * 2**20),
+        compiler_params=pltpu.CompilerParams(vmem_limit_bytes=12 * 2**20),
     )(where, *pre, *weight, *flat)
 
 
@@ -124,8 +124,7 @@
     for n, keep, came in zip(counts, halves[::2], halves[1::2]):
         for i in range(n):
             s = pl.ds(pl.multiple_of(where[k] * own, own), own)
-            j = i ^ 1
-            back = keep[:, i * own:(i + 1) * own] + came[:, j * own:(j + 1) * own].astype(F32)
+            back = keep[:, i * own:(i + 1) * own] + came[:, i * own:(i + 1) * own].astype(F32)
             out = gelu_back(pre_ref[:, s].astype(F32), back).astype(BF16)
             out_ref[:, s] = out[:out_ref.shape[0]]
             k += 1
@@ -139,7 +138,7 @@
         out_shape=jax.ShapeDtypeStruct((rows, pre.shape[1]), BF16),
         in_specs=[pl.BlockSpec(memory_space=pltpu.SMEM)] + [vmem] * (1 + 2 * len(halves)),
         out_specs=vmem,
-        compiler_params=pltpu.CompilerParams(vmem_limit_bytes=20 * 2**20),
+        compiler_params=pltpu.CompilerParams(vmem_limit_bytes=12 * 2**20),
     )(where, pre, *[x for pair in halves for x in pair])
 
 
@@ -165,7 +164,7 @@
         out_shape=jax.ShapeDtypeStruct(error.shape, F32),
         in_specs=[pl.BlockSpec(memory_space=pltpu.SMEM)] + [vmem] * 5,
         out_specs=vmem,
-        compiler_params=pltpu.CompilerParams(vmem_limit_bytes=20 * 2**20),
+        compiler_params=pltpu.CompilerParams(vmem_limit_bytes=12 * 2**20),
     )(side, own, came, error, left, right)
 
 
@@ -221,12 +220,7 @@
     w_give = jnp.where(side == 0, w_last, w_first)
 
     def spot(keys):
-        out = []
-        for j, dy in keys:
-            at = (nx - 1 - ix) if j else ix
-            row = ((iy + dy) & (ny - 1)) * nx
-            out += [row + at, row + (at ^ 1)]
-        return jnp.stack(out)
+        return jnp.stack([((iy + dy) & (ny - 1)) * (nx // 2) + ((ix >> 1) ^ j) for j, dy in keys])
 
     def around(x):
         return shift(x, "y", 1), shift(x, "y", -1), peer(x)
@@ -234,27 +228,34 @@
     def beyond(up, down, over):
         return shift(up, "y", 1), peer(up), shift(over, "y", -1)
 
-    a0, b0 = og_mine, partner(og_give)
-    a1 = around(a0)
+    def corner(far, over_up, over_down):
+        cut = (width // 3 + 64) // 128 * 128
+        return (
+            peer(far[:cut]),
+            shift(over_up[cut:2 * cut], "y", 1),
+            shift(over_down[2 * cut:], "y", -1),
+        )
+
+    og_came = partner(og_give)
+    pair = 2 * own
 
     act = gelu16(pre_act)
     q3 = jnp.concatenate(split(q_init, 3), axis=1)
     y = fold(dot(q3, out_grad, 0, 1), 3)
-    y_all, a0, b0, a1, pre_pad, w_give = tie(spread(y, MP), a0, b0, a1, pre_pad, w_give)
-    b1 = around(b0)
+    y_all, og_mine, og_came, pre_pad, w_give = tie(spread(y, MP), og_mine, og_came, pre_pad, w_give)
+    below = jnp.where((ix & 1) == 0, og_mine, og_came)
+    above = jnp.where((ix & 1) == 0, og_came, og_mine)
+    block = jnp.concatenate([below, above], axis=1)
+    one = around(block)
     pre_two = (pre_pad, partner(pre_pad))
     w_two = (w_mine, partner(w_give))
-    a2 = beyond(*a1)
     y_all = y_all.transpose(1, 0, 2).reshape(rank, toks)
     y3 = jnp.concatenate(split(y_all, 3), axis=0)
     e2 = split(error, 2)
     p_err = sum(fold(dot(q3, e, 0, 1), 3) for e in e2)
     p_local = fold(dot(y3, act, 1, 1), 3) + p_err
-    p_local, b1, a2, pre_two = tie(spread(p_local, "z"), b1, a2, pre_two)
-    b2 = beyond(*b1)
-    a3 = peer(a2[0])
-    pbar = jnp.sum(p_local, axis=0)
-    pbar = (pbar + other_core(pbar)) / groups
+    pbar = jnp.sum(spread(p_local, "z"), axis=0)
+    pbar, one, pre_two = tie((pbar + other_core(pbar)) / groups, one, pre_two)
 
     l3 = jnp.concatenate(split(pbar, 3), axis=0)
     r_error = sum(fold(dot(l3, e, 1, 0), 3) for e in e2)
@@ -271,10 +272,9 @@
     )
     keys = [[(0, 0), (0, 1), (0, -1), (1, 0)], [(0, 2), (1, 1), (1, -1)], [(1, 2)]]
     places = [spot(k) for k in keys]
-    turns = [[x] for both in zip((a0,) + a1, (b0,) + b1) for x in both]
-    took, b2, w_two = tie(lax.all_to_all(sent, MP, 0, 0, tiled=True), b2, w_two)
-    b3 = shift(b2[1], "y", 1)
-    keep_1, send_1, total = add_products(places[0], pre_two, w_two, turns, None)
+    took, one, w_two = tie(lax.all_to_all(sent, MP, 0, 0, tiled=True), one, w_two)
+    two = beyond(*one)
+    keep_1, send_1, total = add_products(places[0], pre_two, w_two, [[x] for x in (block,) + one], None)
     took = jnp.sum(took, axis=0)
     z = took[:rank]
     gram = jnp.concatenate(jnp.split(took[rank:], quarter, axis=1), axis=0)
@@ -284,17 +284,20 @@
     low, high = r_local[:half], r_local[half:]
     keep = jnp.where(core == 0, low, high) + other_core(jnp.where(core == 0, high, low))
     r_part = lax.all_to_all(keep.reshape(nz, half // nz, feat), "z", 0, 0, tiled=True)
-    r_part, a3, b3, total, send_1 = tie(r_part, a3, b3, total, send_1)
+    r_part, two, total, send_1 = tie(r_part, two, total, send_1)
+    last = corner(*two)
     came_1 = partner(send_1)
-    turns = [[x] for both in zip(a2, b2) for x in both]
-    keep_2, send_2, total = add_products(places[1], pre_two, w_two, turns, total)
-    keep_3, send_3, grad_mine, grad_give = add_products(places[2], pre_two, w_two, [[a3], [b3]], total, True)
+    keep_2, send_2, total = add_products(places[1], pre_two, w_two, [[x] for x in two], total)
+    came_2 = partner(send_2)
     r_part = jnp.sum(r_part, axis=0)
-    r_part, grad_give, send_2, send_3 = tie(spread(r_part, MP), grad_give, send_2, send_3)
-    came_2, came_3, grad_came = partner(send_2), partner(send_3), partner(grad_give)
+    r_part, last, total, came_1, came_2 = tie(spread(r_part, MP), last, total, came_1, came_2)
+    keep_3, send_3, grad_mine, grad_give = add_products(places[2], pre_two, w_two, [list(last)], total, True)
+    came_3 = partner(send_3)
     r_part = jnp.sum(r_part, axis=0) / groups
+    r_part, grad_give = tie(r_part, grad_give)
+    grad_came = partner(grad_give)
     halves = [(keep_1, came_1), (keep_2, came_2), (keep_3, came_3)]
-    pre_grad = pre_grads(jnp.concatenate(places), pre_pad, hid, own, halves)
+    pre_grad = pre_grads(jnp.concatenate(places), pre_pad, hid, pair, halves)
     mine, grad_came, pre_grad = tie(spread(r_part, "z"), grad_came, pre_grad)
     mine = mine.reshape(half, feat)
     theirs = other_core(mine)

time: 198 us -> 208 us (1.051)
  local copies, waits for them, and re-layouts: 26.4 us -> 33.6 us
  Pallas kernels: 23.3 us -> 25.9 us
  starting transfers between devices: 58.9 us -> 56.4 us
    ppermute x9 -> x6, starting transfers between devices: 11.1 us -> 5 us  [shift(): return lax.ppermute(x, axis, [((i + step) % n, i) for i in range(n)])]
    ppermute x9 -> x6, waiting for transfers between devices: 7.36 us -> 13.1 us  [shift(): return lax.ppermute(x, axis, [((i + step) % n, i) for i in range(n)])]
    slice x0 -> x3, local copies, waits for them, and re-layouts: none -> 5.41 us  [the longest x1 1.82 us: corner(): far[:cut]]
    ppermute x7, waiting for transfers between devices: 15.1 us -> 9.94 us  [partner(): return lax.ppermute(x, 'x', [(i, i ^ 1) for i in range(lax.axis_size('x'))])]
    all_to_all x1, starting transfers between devices: 4.07 us -> 8.18 us  [shards(): lax.all_to_all(keep.reshape(nz, half // nz, feat), 'z', 0, 0, tiled=True)]
    ppermute x5 -> x3, starting transfers between devices: 6.21 us -> 3.1 us  [peer(): return lax.ppermute(x, 'x', [(i, n - 1 - i) for i in range(n)])]
    all_to_all x3, starting transfers between devices: 16.1 us -> 18.8 us  [spread(): lax.all_to_all(jnp.broadcast_to(x, (n,) + x.shape), axis, 0, 0, tiled=True)]
    pallas_call x3, Pallas kernels: 15.2 us -> 17.5 us  [add_products(): pl.pallas_call(functools.partial(products, [len(b) for b in blocks], tota...]
  transfers between devices with their start and end apart: 29 -> 24, of which waited for: 9 -> 13; matrix products, arithmetic and copies ran while one was open for 17% -> 19% of each run, Pallas kernels for 9% -> 8%
where the time goes in v7:
time: 208 us; the launch traced here: 206 us
  starting transfers between devices  56.4 us (27%)
  waiting for transfers between devices  36.1 us (17%)
  local copies, waits for them, and re-layouts  33.6 us (16%)
  Pallas kernels  25.9 us (12%)
  other arithmetic  24.3 us (12%)
  blocking collectives  17.4 us (8%)
  matrix products  11.2 us (5%)
    all_to_all x3, starting transfers between devices, spread(): lax.all_to_all(jnp.broadcast_to(x, (n,) + x.shape), axis, 0, 0, tiled=True)  18.8 us
    unnamed x60, local copies, waits for them, and re-layouts  18.2 us
    pallas_call x3, Pallas kernels, add_products(): pl.pallas_call(functools.partial(products, [len(b) for b in blocks], tota...  17.5 us
    all_to_all x1, blocking collectives, spread(): lax.all_to_all(jnp.broadcast_to(x, (n,) + x.shape), axis, 0, 0, tiled=True)  17.4 us
    ppermute x6, waiting for transfers between devices, shift(): return lax.ppermute(x, axis, [((i + step) % n, i) for i in range(n)])  13.1 us
    ppermute x3, starting transfers between devices, other_core(): return lax.ppermute(x, 'core', [(0, 1), (1, 0)])  10.5 us
    ppermute x7, waiting for transfers between devices, partner(): return lax.ppermute(x, 'x', [(i, i ^ 1) for i in range(lax.axis_size('x'))])  9.94 us
    dot_general x7, matrix products, dot(): lax.dot_general(a, b, (((ca,), (cb,)), ((), ())), preferred_element_type=...  8.56 us
  transfers between devices with their start and end apart: 24, of which 13 were waited for; matrix products, arithmetic and copies ran while one was open for 19% of the time, Pallas kernels for 8%

profile of v7, /device:TPU:1, one launch (start us, length us, event | category | flops | bytes accessed | tf_op | source)
XLA Modules:
  0.0 205.9 jit_solution(13238029699087679089)
XLA Ops:
  0.7 2.5 %broadcast_select_fusion.4 = (bf16[2496,128]{1,0:T(8,128)(2,1)}, bf16[2496,128]{1,0:T(8,128)(2,1)}) fusion(pred[]{:T(512)S(6)} %eq.7, bf16[4800,128]{1,0:T(8,128)(2,1)} %bitcast.56), kind=kLoop, calls=%fused_computation.30 | loop fusion | flops 638976 | bytes 2555905 | tf_op jit(solution)/shard_map/jit(_where)/select_n | solution.py:213
  3.2 2.0 collective-permute-start
  7.0 6.5 %all-to-all-start = ((f32[16,32,128]{2,1,0:T(8,128)}), f32[16,32,128]{2,1,0:T(8,128)S(1)}, u32[]{:S(2)}, u32[]{:S(2)}) async-start(f32[16,32,128]{2,1,0:T(8,128)} %broadcast_in_dim.24), calls=%async_computation | async-start | bytes 524288 | tf_op jit(solution)/shard_map/all_to_all | solution.py:45
  13.5 3.7 %broadcast_select_fusion = (bf16[160,2496]{1,0:T(8,128)(2,1)}, bf16[160,2496]{1,0:T(8,128)(2,1)}) fusion(pred[]{:T(512)S(6)} %eq.7, bf16[150,4800]{1,0:T(8,128)(2,1)} %param.7, pred[2496]{0:T(1024)(128)(4,1)S(1)} %iota_compare_fusion.3), kind=kLoop, calls=%fused_computation.26 | loop fusion | flops 1597440 | bytes 3039937 | tf_op jit(solution)/shard_map/jit(_where)/select_n | solution.py:219
  17.2 2.0 pad.8.pre_a.pre_ref
  19.2 1.8 fusion.33
  21.6 5.4 %all-to-all-done = f32[16,32,128]{2,1,0:T(8,128)S(1)} async-done(((f32[16,32,128]{2,1,0:T(8,128)}), f32[16,32,128]{2,1,0:T(8,128)S(1)}, u32[]{:S(2)}, u32[]{:S(2)}) %all-to-all-start) | async-done | bytes 262176 | tf_op jit(solution)/shard_map/all_to_all | solution.py:45
  32.0 17.4 %all_to_all.30 = f32[8,32,150]{2,1,0:T(8,128)S(1)} all-to-all(f32[8,32,150]{2,1,0:T(8,128)S(1)} %broadcast_in_dim.27), channel_id=1, replica_groups=mesh['z'=8,'core'=2,'y'=4,'x'=4] {'z'}, dimensions={0} | all-to-all | bytes 307200 | tf_op jit(solution)/shard_map/all_to_all | solution.py:45
  49.4 4.0 %collective-permute-start.1 = (f32[32,150]{1,0:T(8,128)S(1)}, f32[32,150]{1,0:T(8,128)S(1)}, u32[]{:S(2)}, u32[]{:S(2)}) collective-permute-start(f32[32,150]{1,0:T(8,128)S(1)} %reduce_sum.36), channel_id=1, source_target_pairs={{0,16},{16,0},{1,17},{17,1},{2,18},{18,2},{3,19},{19,3},{4,20},{20... | collective-permute-start | bytes 57608 | tf_op jit(solution)/shard_map/ppermute | solution.py:49
  54.2 1.7 collective-permute-start.6
  55.9 1.9 collective-permute-done.2.refs_1_
  57.9 1.4 collective-permute-done.3.refs_2_
  60.2 1.7 fusion.45
  61.9 1.8 fusion.18
  63.7 1.7 fusion.31
  66.3 4.2 %all-to-all-start.2 = ((f32[16,40,128]{2,1,0:T(8,128)}), f32[16,40,128]{2,1,0:T(8,128)}, u32[]{:S(2)}, u32[]{:S(2)}) async-start(f32[16,40,128]{2,1,0:T(8,128)} %pad_maximum_fusion.3), calls=%async_computation.2 | async-start | bytes 655360 | tf_op jit(solution)/shard_map/all_to_all | solution.py:275
  70.5 2.2 %fusion.13.more_ref = f32[32,4800]{1,0:T(8,128)S(1)} fusion(f32[96,4800]{1,0:T(8,128)} %fusion.31, f32[96,4800]{1,0:T(8,128)} %fusion.18), kind=kLoop, calls=%fused_computation.37 | loop fusion | flops 768000 | bytes 4300800 | tf_op jit(solution)/shard_map/add | solution.py:261
  72.7 1.8 collective-permute-done.6.w_b
  74.5 5.9 %all-to-all-done.2 = f32[16,40,128]{2,1,0:T(8,128)} async-done(((f32[16,40,128]{2,1,0:T(8,128)}), f32[16,40,128]{2,1,0:T(8,128)}, u32[]{:S(2)}, u32[]{:S(2)}) %all-to-all-start.2) | async-done | bytes 327712 | tf_op jit(solution)/shard_map/all_to_all | solution.py:275
  80.4 1.6 reduce_sum.37
  84.6 2.3 %collective-permute-start.7 = (f32[16,4800]{1,0:T(8,128)S(1)}, f32[16,4800]{1,0:T(8,128)S(1)}, u32[]{:S(2)}, u32[]{:S(2)}) collective-permute-start(f32[16,4800]{1,0:T(8,128)S(1)} %slice_select_fusion), channel_id=1, source_target_pairs={{0,16},{16,0},{1,17},{17,1},{2,18},{18,2},{3,19},{19,3},{4,20},{20... | collective-permute-start | bytes 921608 | tf_op jit(solution)/shard_map/ppermute | solution.py:49
  89.6 8.2 %all-to-all-start.3 = ((f32[8,2,4800]{2,1,0:T(2,128)}), f32[8,2,4800]{2,1,0:T(2,128)S(1)}, u32[]{:S(2)}, u32[]{:S(2)}) async-start(f32[8,2,4800]{2,1,0:T(2,128)} %reshape.33), calls=%async_computation.3 | async-start | bytes 622592 | tf_op jit(solution)/shard_map/all_to_all | solution.py:286
  99.0 7.2 %shard_map.77 = (f32[160,1024]{1,0:T(8,128)S(1)}, bf16[160,1024]{1,0:T(8,128)(2,1)}, f32[320,2496]{1,0:T(8,128)S(1)}) custom-call(s32[4]{0:T(128)S(1)} %pad_add_fusion.where, bf16[160,2048]{1,0:T(8,128)(2,1)} %pad.8.pre_a.pre_ref, bf16[160,2048]{1,0:T(8,128)(2,1)} %collective-permute-done.5.pre_b, bf16[160,2496]{1,0:T(8,128)(2,1)S(1)} %copy-done.1, ...), custom_call_target="tpu_custom_call" | custom-call | tf_op jit(solution)/shard_map/pallas_call | solution.py:112
  106.2 1.8 copy-done.6
  108.9 9.8 %collective-permute-done.10.refs_2_ = bf16[2496,256]{1,0:T(8,128)(2,1)} collective-permute-done((bf16[2496,256]{1,0:T(8,128)(2,1)}, bf16[2496,256]{1,0:T(8,128)(2,1)}, u32[]{:S(2)}, u32[]{:S(2)}) %collective-permute-start.10) | collective-permute-done | bytes 1277984 | tf_op jit(solution)/shard_map/ppermute | solution.py:54
  119.8 4.3 %all-to-all-start.4 = ((f32[16,2,4800]{2,1,0:T(2,128)}), f32[16,2,4800]{2,1,0:T(2,128)}, u32[]{:S(2)}, u32[]{:S(2)}) async-start(f32[16,2,4800]{2,1,0:T(2,128)} %broadcast_in_dim.29), calls=%async_computation.4 | async-start | bytes 1245184 | tf_op jit(solution)/shard_map/all_to_all | solution.py:45
  124.2 1.8 slice.140
  126.0 2.4 %collective-permute-start.11 = (bf16[896,256]{1,0:T(8,128)(2,1)}, bf16[896,256]{1,0:T(8,128)(2,1)}, u32[]{:S(2)}, u32[]{:S(2)}) collective-permute-start(bf16[896,256]{1,0:T(8,128)(2,1)} %slice.140), channel_id=1, source_target_pairs={{0,3},{1,2},{2,1},{3,0},{4,7},{5,6},{6,5},{7,4},{8,11},{9,10},{10,... | collective-permute-start | bytes 1376264 | tf_op jit(solution)/shard_map/ppermute | solution.py:63
  128.4 1.8 slice.141
  130.3 2.5 %collective-permute-start.12 = (bf16[896,256]{1,0:T(8,128)(2,1)}, bf16[896,256]{1,0:T(8,128)(2,1)}, u32[]{:S(2)}, u32[]{:S(2)}) collective-permute-start(bf16[896,256]{1,0:T(8,128)(2,1)} %slice.141), channel_id=1, source_target_pairs={{4,0},{8,4},{12,8},{0,12},{5,1},{9,5},{13,9},{1,13},{6,2},{10,6},{... | collective-permute-start | bytes 1376264 | tf_op jit(solution)/shard_map/ppermute | solution.py:54
  132.7 1.8 slice.142
  136.0 1.9 copy-done.7
  138.0 6.3 %shard_map.78 = (f32[160,768]{1,0:T(8,128)S(1)}, bf16[160,768]{1,0:T(8,128)(2,1)}, f32[320,2496]{1,0:T(8,128)S(1)}) custom-call(s32[3]{0:T(128)S(1)} %pad_add_fusion.1.where, bf16[160,2048]{1,0:T(8,128)(2,1)} %pad.8.pre_a.pre_ref, bf16[160,2048]{1,0:T(8,128)(2,1)} %collective-permute-done.5.pre_b, bf16[160,2496]{1,0:T(8,128)(2,1)S(1)} %copy-done.2, ...), custom_call_target="tpu_custom_call" | custom-call | tf_op jit(solution)/shard_map/pallas_call | solution.py:112
  144.3 1.8 copy-done.8
  146.1 1.5 collective-permute-start.14
  147.8 2.9 %cholesky.17 = f32[32,32]{1,0:T(8,128)S(1)} custom-call(f32[32,32]{1,0:T(8,128)S(1)} %fusion.42), custom_call_target="Cholesky" | custom-call | tf_op jit(solution)/shard_map/jit(cholesky)/cholesky | solution.py:306
  151.5 7.1 %collective-permute-done.14.refs_1_ = bf16[160,1024]{1,0:T(8,128)(2,1)} collective-permute-done((bf16[160,1024]{1,0:T(8,128)(2,1)}, bf16[160,1024]{1,0:T(8,128)(2,1)}, u32[]{:S(2)}, u32[]{:S(2)}) %collective-permute-start.14) | collective-permute-done | bytes 327712 | tf_op jit(solution)/shard_map/ppermute | solution.py:58
  161.0 1.9 copy-done.9
  162.9 4.0 %shard_map.79 = (f32[160,256]{1,0:T(8,128)S(1)}, bf16[160,256]{1,0:T(8,128)(2,1)S(1)}, f32[160,2496]{1,0:T(8,128)S(1)}, bf16[160,2496]{1,0:T(8,128)(2,1)}) custom-call(s32[1]{0:T(128)} %bitcast.10.where, bf16[160,2048]{1,0:T(8,128)(2,1)} %pad.8.pre_a.pre_ref, bf16[160,2048]{1,0:T(8,128)(2,1)} %collective-permute-done.5.pre_b, ...), custom_call_target="tpu_custom_call" | custom-call | tf_op jit(solution)/shard_map/pallas_call | solution.py:112
  171.0 8.1 %all-to-all-start.5 = ((f32[8,2,4800]{2,1,0:T(2,128)}), f32[8,2,4800]{2,1,0:T(2,128)}, u32[]{:S(2)}, u32[]{:S(2)}) async-start(f32[8,2,4800]{2,1,0:T(2,128)} %broadcast_in_dim.30), calls=%async_computation.5 | async-start | bytes 622592 | tf_op jit(solution)/shard_map/all_to_all | solution.py:45
  179.8 2.4 %custom-call.7 = f32[1,32,32]{1,2,0:T(8,128)S(1)} custom-call(f32[1,32,32]{2,1,0:T(8,128)S(1)} %fusion.37), custom_call_target="InvertDiagBlocksLowerTriangular" | custom-call | tf_op jit(solution)/shard_map/jit(_solve_triangular)/triangular_solve | solution.py:307
  182.4 1.4 collective-permute-start.17
  184.7 1.5 copy.49
  186.1 1.5 copy.50
  189.9 3.4 %shard_map.80 = bf16[150,2048]{1,0:T(8,128)(2,1)} custom-call(s32[8]{0:T(128)S(1)} %concatenate.44.where, bf16[160,2048]{1,0:T(8,128)(2,1)} %pad.8.pre_a.pre_ref, f32[160,1024]{1,0:T(8,128)S(1)} %copy-done.13, bf16[160,1024]{1,0:T(8,128)(2,1)} %collective-permute-done.14.refs_1_, f32[160,768]{1,0:T(8,128)S(1)} %get-tuple-element.85.refs_2_, ...), custom_call_target="tpu_custom_call" | custom-call | tf_op jit(solution)/shard_map/pallas_call | solution.py:136
  194.5 4.2 %collective-permute-start.18 = (f32[16,4800]{1,0:T(8,128)S(1)}, f32[16,4800]{1,0:T(8,128)S(1)}, u32[]{:S(2)}, u32[]{:S(2)}) collective-permute-start(f32[16,4800]{1,0:T(8,128)S(1)} %reshape.35), channel_id=1, source_target_pairs={{0,16},{16,0},{1,17},{17,1},{2,18},{18,2},{3,19},{19,3},{4,20},{20... | collective-permute-start | bytes 921608 | tf_op jit(solution)/shard_map/ppermute | solution.py:49
  200.0 1.5 fusion.12
  201.6 4.4 %shard_map.81 = f32[150,1,4800]{2,1,0:T(1,128)} custom-call(s32[1]{0:T(128)} %bitcast.11.side, f32[160,2496]{1,0:T(8,128)S(1)} %copy-done.11, bf16[160,2496]{1,0:T(8,128)(2,1)} %collective-permute-done.16.came_ref, f32[150,1,4800]{2,1,0:T(1,128)S(1)} %bitcast.55, bf16[150,96]{1,0:T(8,128)(2,1)S(1)} %maximum_bitcast_fusion.left_ref, ...), custom_call_target="tpu_custom_call" | custom-call | tf_op jit(solution)/shard_map/pallas_call | solution.py:162
  (133 shorter events, 34.2 us)
Async XLA Ops:
  0.6 4.6 %copy-start.19 = (f32[4800,32]{0,1:T(8,128)S(1)}, f32[4800,32]{0,1:T(8,128)}, u32[]{:S(2)}) copy-start(f32[4800,32]{0,1:T(8,128)} %param.9) | copy-start | bytes 1843204
  0.7 4.8 %copy-start.4 = (bf16[128,4800]{0,1:T(8,128)(2,1)S(1)}, bf16[128,4800]{0,1:T(8,128)(2,1)}, u32[]{:S(2)}) copy-start(bf16[128,4800]{0,1:T(8,128)(2,1)} %param.6) | copy-start | bytes 3686404
  3.2 23.7 %collective-permute-start = (bf16[2496,128]{1,0:T(8,128)(2,1)}, bf16[2496,128]{1,0:T(8,128)(2,1)}, u32[]{:S(2)}, u32[]{:S(2)}) collective-permute-start(bf16[2496,128]{1,0:T(8,128)(2,1)} %get-tuple-element.97), channel_id=1, source_target_pairs={{0,1},{1,0},{2,3},{3,2},{4,5},{5,4},{6,7},{7,6},{8,9},{9,8},{10,11... | collective-permute-start | bytes 1916936 | tf_op jit(solution)/shard_map/ppermute | solution.py:58
  5.4 0.9 copy-start.25
  7.0 19.9 %all-to-all-start = ((f32[16,32,128]{2,1,0:T(8,128)}), f32[16,32,128]{2,1,0:T(8,128)S(1)}, u32[]{:S(2)}, u32[]{:S(2)}) async-start(f32[16,32,128]{2,1,0:T(8,128)} %broadcast_in_dim.24), calls=%async_computation | async-start | bytes 524288 | tf_op jit(solution)/shard_map/all_to_all | solution.py:45
  13.5 5.7 %copy-start = (f32[1,150,4800]{2,0,1:T(1,128)S(1)}, f32[1,150,4800]{2,0,1:T(1,128)}, u32[]{:S(2)}) copy-start(f32[1,150,4800]{2,0,1:T(1,128)} %param.8) | copy-start | bytes 8640004
  19.2 1.8 copy-start.22
  19.2 1.8 copy-start.24
  19.2 1.8 copy-start.26
  28.3 2.7 %copy-start.20 = (bf16[150,2048]{1,0:T(8,128)(2,1)S(1)}, bf16[150,2048]{1,0:T(8,128)(2,1)}, u32[]{:S(2)}) copy-start(bf16[150,2048]{1,0:T(8,128)(2,1)} %param.5) | copy-start | bytes 1843204
  29.5 28.3 %collective-permute-start.2 = (bf16[2496,256]{1,0:T(8,128)(2,1)}, bf16[2496,256]{1,0:T(8,128)(2,1)}, u32[]{:S(2)}, u32[]{:S(2)}) collective-permute-start(bf16[2496,256]{1,0:T(8,128)(2,1)} %pad_maximum_fusion.refs_0_), channel_id=1, source_target_pairs={{4,0},{8,4},{12,8},{0,12},{5,1},{9,5},{13,9},{1,13},{6,2},{10,6},{... | collective-permute-start | bytes 3833864 | tf_op jit(solution)/shard_map/ppermute | solution.py:54
  30.0 29.3 %collective-permute-start.3 = (bf16[2496,256]{1,0:T(8,128)(2,1)}, bf16[2496,256]{1,0:T(8,128)(2,1)}, u32[]{:S(2)}, u32[]{:S(2)}) collective-permute-start(bf16[2496,256]{1,0:T(8,128)(2,1)} %pad_maximum_fusion.refs_0_), channel_id=1, source_target_pairs={{12,0},{0,4},{4,8},{8,12},{13,1},{1,5},{5,9},{9,13},{14,2},{2,6},{... | collective-permute-start | bytes 3833864 | tf_op jit(solution)/shard_map/ppermute | solution.py:54
  31.0 29.0 %collective-permute-start.4 = (bf16[2496,256]{1,0:T(8,128)(2,1)}, bf16[2496,256]{1,0:T(8,128)(2,1)}, u32[]{:S(2)}, u32[]{:S(2)}) collective-permute-start(bf16[2496,256]{1,0:T(8,128)(2,1)} %pad_maximum_fusion.refs_0_), channel_id=1, source_target_pairs={{0,3},{1,2},{2,1},{3,0},{4,7},{5,6},{6,5},{7,4},{8,11},{9,10},{10,... | collective-permute-start | bytes 3833864 | tf_op jit(solution)/shard_map/ppermute | solution.py:63
  31.0 24.9 %collective-permute-start.5 = (bf16[160,2048]{1,0:T(8,128)(2,1)}, bf16[160,2048]{1,0:T(8,128)(2,1)}, u32[]{:S(2)}, u32[]{:S(2)}) collective-permute-start(bf16[160,2048]{1,0:T(8,128)(2,1)} %pad.8.pre_a.pre_ref), channel_id=1, source_target_pairs={{0,1},{1,0},{2,3},{3,2},{4,5},{5,4},{6,7},{7,6},{8,9},{9,8},{10,11... | collective-permute-start | bytes 1966088 | tf_op jit(solution)/shard_map/ppermute | solution.py:58
  49.4 4.8 %collective-permute-start.1 = (f32[32,150]{1,0:T(8,128)S(1)}, f32[32,150]{1,0:T(8,128)S(1)}, u32[]{:S(2)}, u32[]{:S(2)}) collective-permute-start(f32[32,150]{1,0:T(8,128)S(1)} %reduce_sum.36), channel_id=1, source_target_pairs={{0,16},{16,0},{1,17},{17,1},{2,18},{18,2},{3,19},{19,3},{4,20},{20... | collective-permute-start | bytes 57608 | tf_op jit(solution)/shard_map/ppermute | solution.py:49
  54.2 20.3 %collective-permute-start.6 = (bf16[160,2496]{1,0:T(8,128)(2,1)}, bf16[160,2496]{1,0:T(8,128)(2,1)}, u32[]{:S(2)}, u32[]{:S(2)}) collective-permute-start(bf16[160,2496]{1,0:T(8,128)(2,1)} %get-tuple-element.56), channel_id=1, source_target_pairs={{0,1},{1,0},{2,3},{3,2},{4,5},{5,4},{6,7},{7,6},{8,9},{9,8},{10,11... | collective-permute-start | bytes 2396168 | tf_op jit(solution)/shard_map/ppermute | solution.py:58
  55.9 4.1 %copy-start.17 = (f32[32,150]{1,0:T(8,128)}, f32[32,150]{1,0:T(8,128)S(1)}, u32[]{:S(2)}) copy-start(f32[32,150]{1,0:T(8,128)S(1)} %add_multiply_fusion) | copy-start | bytes 57604
  66.3 14.1 %all-to-all-start.2 = ((f32[16,40,128]{2,1,0:T(8,128)}), f32[16,40,128]{2,1,0:T(8,128)}, u32[]{:S(2)}, u32[]{:S(2)}) async-start(f32[16,40,128]{2,1,0:T(8,128)} %pad_maximum_fusion.3), calls=%async_computation.2 | async-start | bytes 655360 | tf_op jit(solution)/shard_map/all_to_all | solution.py:275
  82.7 1.3 copy-start.5
  84.6 4.0 %collective-permute-start.7 = (f32[16,4800]{1,0:T(8,128)S(1)}, f32[16,4800]{1,0:T(8,128)S(1)}, u32[]{:S(2)}, u32[]{:S(2)}) collective-permute-start(f32[16,4800]{1,0:T(8,128)S(1)} %slice_select_fusion), channel_id=1, source_target_pairs={{0,16},{16,0},{1,17},{17,1},{2,18},{18,2},{3,19},{19,3},{4,20},{20... | collective-permute-start | bytes 921608 | tf_op jit(solution)/shard_map/ppermute | solution.py:49
  86.9 31.8 %collective-permute-start.8 = (bf16[2496,256]{1,0:T(8,128)(2,1)}, bf16[2496,256]{1,0:T(8,128)(2,1)}, u32[]{:S(2)}, u32[]{:S(2)}) collective-permute-start(bf16[2496,256]{1,0:T(8,128)(2,1)} %collective-permute-done.2.refs_1_), channel_id=1, source_target_pairs={{4,0},{8,4},{12,8},{0,12},{5,1},{9,5},{13,9},{1,13},{6,2},{10,6},{... | collective-permute-start | bytes 3833864 | tf_op jit(solution)/shard_map/ppermute | solution.py:54
  87.5 31.2 %collective-permute-start.9 = (bf16[2496,256]{1,0:T(8,128)(2,1)}, bf16[2496,256]{1,0:T(8,128)(2,1)}, u32[]{:S(2)}, u32[]{:S(2)}) collective-permute-start(bf16[2496,256]{1,0:T(8,128)(2,1)} %collective-permute-done.2.refs_1_), channel_id=1, source_target_pairs={{0,3},{1,2},{2,1},{3,0},{4,7},{5,6},{6,5},{7,4},{8,11},{9,10},{10,... | collective-permute-start | bytes 3833864 | tf_op jit(solution)/shard_map/ppermute | solution.py:63
  88.2 30.5 %collective-permute-start.10 = (bf16[2496,256]{1,0:T(8,128)(2,1)}, bf16[2496,256]{1,0:T(8,128)(2,1)}, u32[]{:S(2)}, u32[]{:S(2)}) collective-permute-start(bf16[2496,256]{1,0:T(8,128)(2,1)} %collective-permute-done.4.refs_3_), channel_id=1, source_target_pairs={{12,0},{0,4},{4,8},{8,12},{13,1},{1,5},{5,9},{9,13},{14,2},{2,6},{... | collective-permute-start | bytes 3833864 | tf_op jit(solution)/shard_map/ppermute | solution.py:54
  89.6 19.3 %all-to-all-start.3 = ((f32[8,2,4800]{2,1,0:T(2,128)}), f32[8,2,4800]{2,1,0:T(2,128)S(1)}, u32[]{:S(2)}, u32[]{:S(2)}) async-start(f32[8,2,4800]{2,1,0:T(2,128)} %reshape.33), calls=%async_computation.3 | async-start | bytes 622592 | tf_op jit(solution)/shard_map/all_to_all | solution.py:286
  97.9 1.1 copy-start.1
  106.2 1.8 copy-start.6
  108.0 0.8 copy-start.12
  119.8 38.8 %all-to-all-start.4 = ((f32[16,2,4800]{2,1,0:T(2,128)}), f32[16,2,4800]{2,1,0:T(2,128)}, u32[]{:S(2)}, u32[]{:S(2)}) async-start(f32[16,2,4800]{2,1,0:T(2,128)} %broadcast_in_dim.29), calls=%async_computation.4 | async-start | bytes 1245184 | tf_op jit(solution)/shard_map/all_to_all | solution.py:45
  124.0 10.5 %copy-start.27 = (f32[40,128]{1,0:T(8,128)S(1)}, f32[40,128]{1,0:T(8,128)}, u32[]{:S(2)}) copy-start(f32[40,128]{1,0:T(8,128)} %reduce_sum.37) | copy-start | bytes 61444
  126.0 32.5 %collective-permute-start.11 = (bf16[896,256]{1,0:T(8,128)(2,1)}, bf16[896,256]{1,0:T(8,128)(2,1)}, u32[]{:S(2)}, u32[]{:S(2)}) collective-permute-start(bf16[896,256]{1,0:T(8,128)(2,1)} %slice.140), channel_id=1, source_target_pairs={{0,3},{1,2},{2,1},{3,0},{4,7},{5,6},{6,5},{7,4},{8,11},{9,10},{10,... | collective-permute-start | bytes 1376264 | tf_op jit(solution)/shard_map/ppermute | solution.py:63
  130.3 28.3 %collective-permute-start.12 = (bf16[896,256]{1,0:T(8,128)(2,1)}, bf16[896,256]{1,0:T(8,128)(2,1)}, u32[]{:S(2)}, u32[]{:S(2)}) collective-permute-start(bf16[896,256]{1,0:T(8,128)(2,1)} %slice.141), channel_id=1, source_target_pairs={{4,0},{8,4},{12,8},{0,12},{5,1},{9,5},{13,9},{1,13},{6,2},{10,6},{... | collective-permute-start | bytes 1376264 | tf_op jit(solution)/shard_map/ppermute | solution.py:54
  134.5 24.0 %collective-permute-start.13 = (bf16[704,256]{1,0:T(8,128)(2,1)}, bf16[704,256]{1,0:T(8,128)(2,1)}, u32[]{:S(2)}, u32[]{:S(2)}) collective-permute-start(bf16[704,256]{1,0:T(8,128)(2,1)} %slice.142), channel_id=1, source_target_pairs={{12,0},{0,4},{4,8},{8,12},{13,1},{1,5},{5,9},{9,13},{14,2},{2,6},{... | collective-permute-start | bytes 1081352 | tf_op jit(solution)/shard_map/ppermute | solution.py:54
  134.9 1.1 copy-start.2
  136.0 1.9 copy-start.7
  144.3 1.8 copy-start.8
  146.1 5.4 %collective-permute-start.15 = (bf16[160,768]{1,0:T(8,128)(2,1)}, bf16[160,768]{1,0:T(8,128)(2,1)}, u32[]{:S(2)}, u32[]{:S(2)}) collective-permute-start(bf16[160,768]{1,0:T(8,128)(2,1)} %get-tuple-element.74), channel_id=1, source_target_pairs={{0,1},{1,0},{2,3},{3,2},{4,5},{5,4},{6,7},{7,6},{8,9},{9,8},{10,11... | collective-permute-start | bytes 737288 | tf_op jit(solution)/shard_map/ppermute | solution.py:58
  146.1 12.4 %collective-permute-start.14 = (bf16[160,1024]{1,0:T(8,128)(2,1)}, bf16[160,1024]{1,0:T(8,128)(2,1)}, u32[]{:S(2)}, u32[]{:S(2)}) collective-permute-start(bf16[160,1024]{1,0:T(8,128)(2,1)} %get-tuple-element.73), channel_id=1, source_target_pairs={{0,1},{1,0},{2,3},{3,2},{4,5},{5,4},{6,7},{7,6},{8,9},{9,8},{10,11... | collective-permute-start | bytes 983048 | tf_op jit(solution)/shard_map/ppermute | solution.py:58
  159.9 1.1 copy-start.3
  161.0 1.9 copy-start.9
  162.9 20.9 %copy-start.18 = (f32[32,150]{1,0:T(8,128)S(1)}, f32[32,150]{1,0:T(8,128)}, u32[]{:S(2)}) copy-start(f32[32,150]{1,0:T(8,128)} %copy-done.17) | copy-start | bytes 57604
  166.9 1.2 copy-start.10
  169.4 24.0 %collective-permute-start.16 = (bf16[160,2496]{1,0:T(8,128)(2,1)}, bf16[160,2496]{1,0:T(8,128)(2,1)}, u32[]{:S(2)}, u32[]{:S(2)}) collective-permute-start(bf16[160,2496]{1,0:T(8,128)(2,1)} %get-tuple-element.82), channel_id=1, source_target_pairs={{0,1},{1,0},{2,3},{3,2},{4,5},{5,4},{6,7},{7,6},{8,9},{9,8},{10,11... | collective-permute-start | bytes 2396168 | tf_op jit(solution)/shard_map/ppermute | solution.py:58
  171.0 22.4 %all-to-all-start.5 = ((f32[8,2,4800]{2,1,0:T(2,128)}), f32[8,2,4800]{2,1,0:T(2,128)}, u32[]{:S(2)}, u32[]{:S(2)}) async-start(f32[8,2,4800]{2,1,0:T(2,128)} %broadcast_in_dim.30), calls=%async_computation.5 | async-start | bytes 622592 | tf_op jit(solution)/shard_map/all_to_all | solution.py:45
  182.4 5.5 %collective-permute-start.17 = (bf16[160,256]{1,0:T(8,128)(2,1)}, bf16[160,256]{1,0:T(8,128)(2,1)S(1)}, u32[]{:S(2)}, u32[]{:S(2)}) collective-permute-start(bf16[160,256]{1,0:T(8,128)(2,1)} %copy-done.16), channel_id=1, source_target_pairs={{0,1},{1,0},{2,3},{3,2},{4,5},{5,4},{6,7},{7,6},{8,9},{9,8},{10,11... | collective-permute-start | bytes 245768 | tf_op jit(solution)/shard_map/ppermute | solution.py:58
  187.9 1.1 copy-start.13
  189.0 0.9 copy-start.15
  194.5 5.4 %collective-permute-start.18 = (f32[16,4800]{1,0:T(8,128)S(1)}, f32[16,4800]{1,0:T(8,128)S(1)}, u32[]{:S(2)}, u32[]{:S(2)}) collective-permute-start(f32[16,4800]{1,0:T(8,128)S(1)} %reshape.35), channel_id=1, source_target_pairs={{0,16},{16,0},{1,17},{17,1},{2,18},{18,2},{3,19},{19,3},{4,20},{20... | collective-permute-start | bytes 921608 | tf_op jit(solution)/shard_map/ppermute | solution.py:49
  200.0 1.6 copy-start.11
  (4 other events, 2.8 us)

commit v8 on v3

--- a/solution.py
+++ b/solution.py
@@ -1,6 +1,7 @@
+import functools
+
 import jax
 import jax.numpy as jnp
-import numpy as np
 from jax import lax
 from jax.experimental import pallas as pl
 from jax.experimental.pallas import tpu as pltpu
@@ -53,11 +54,12 @@
     return lax.ppermute(x, axis, [((i + step) % n, i) for i in range(n)])
 
 
-def products(where, pre_ref, weight_ref, *refs):
-    *blocks, mat_in, grad_in, mat_ref, grad_ref = refs
-    grad_ref[...] = grad_in[...]
+def products(n, where, pre_ref, weight_ref, *refs):
+    blocks, held, (mat_ref, grad_ref) = refs[:n], refs[n:-2], refs[-2:]
+    if held:
+        grad_ref[...] = held[1][...]
     own = blocks[0].shape[1]
-    spots = [pl.ds(pl.multiple_of(where[i] * own, own), own) for i in range(len(blocks))]
+    spots = [pl.ds(pl.multiple_of(where[i] * own, own), own) for i in range(n)]
     pre = jnp.concatenate([pre_ref[:, s] for s in spots], axis=1).astype(F32)
     act, pull = jax.vjp(jax.nn.gelu, pre)
     act = act.astype(BF16)
@@ -67,23 +69,63 @@
         part = slice(lo, min(feat, lo + 512))
         piece = jnp.concatenate([b[part, :] for b in blocks], axis=1)
         back = back + dot(weight_ref[:, part], piece, 1, 0)
-        mat_ref[:, part] = mat_in[:, part] + dot(act, piece, 1, 1)
+        more = dot(act, piece, 1, 1)
+        mat_ref[:, part] = more + held[0][:, part] if held else more
     out = pull(back)[0].astype(BF16)
     for i, s in enumerate(spots):
         grad_ref[:, s] = out[:, i * own:(i + 1) * own]
 
 
-def add_products(where, pre_act, weight, blocks, mat, pre_grad):
+def add_products(where, pre_act, weight, blocks, held):
     vmem = pl.BlockSpec(memory_space=pltpu.VMEM)
     n = len(blocks)
+    mat = jax.ShapeDtypeStruct(weight.shape, F32)
     return pl.pallas_call(
-        products,
-        out_shape=(jax.ShapeDtypeStruct(mat.shape, F32), jax.ShapeDtypeStruct(pre_grad.shape, BF16)),
-        in_specs=[pl.BlockSpec(memory_space=pltpu.SMEM)] + [vmem] * (n + 4),
+        functools.partial(products, n),
+        out_shape=(mat, jax.ShapeDtypeStruct(pre_act.shape, BF16)),
+        in_specs=[pl.BlockSpec(memory_space=pltpu.SMEM)] + [vmem] * (n + 2 + len(held)),
         out_specs=(vmem, vmem),
-        input_output_aliases={n + 3: 0, n + 4: 1},
-        compiler_params=pltpu.CompilerParams(vmem_limit_bytes=40 * 2**20),
-    )(where, pre_act, weight, *blocks, mat, pre_grad)
+        input_output_aliases={n + 3: 0, n + 4: 1} if held else {},
+        compiler_params=pltpu.CompilerParams(vmem_limit_bytes=12 * 2**20),
+    )(where, pre_act, weight, *blocks, *held)
+
+
+def finish(mat_ref, error_ref, left_ref, right_ref, out_ref):
+    feat = mat_ref.shape[1]
+    left = left_ref[...]
+    for lo in range(0, feat, 512):
+        part = slice(lo, min(feat, lo + 512))
+        out_ref[:, 0, part] = mat_ref[:, part] + error_ref[:, 0, part] - dot(left, right_ref[:, part], 1, 0)
+
+
+def new_errors(mat, error, left, right):
+    vmem = pl.BlockSpec(memory_space=pltpu.VMEM)
+    return pl.pallas_call(
+        finish,
+        out_shape=jax.ShapeDtypeStruct(error.shape, F32),
+        in_specs=[vmem] * 4,
+        out_specs=vmem,
+        compiler_params=pltpu.CompilerParams(vmem_limit_bytes=12 * 2**20),
+    )(mat, error, left, right)
+
+
+def right_rows(z_ref, og_ref, more_ref, out_ref):
+    rank, feat = out_ref.shape
+    z = z_ref[...]
+    for lo in range(0, feat, 512):
+        part = slice(lo, min(feat, lo + 512))
+        out_ref[:, part] = fold(dot(z, og_ref[part, :], 1, 1), 3) + more_ref[:, part]
+
+
+def right_factor(z3, og, more):
+    vmem = pl.BlockSpec(memory_space=pltpu.VMEM)
+    return pl.pallas_call(
+        right_rows,
+        out_shape=jax.ShapeDtypeStruct(more.shape, F32),
+        in_specs=[vmem] * 3,
+        out_specs=vmem,
+        compiler_params=pltpu.CompilerParams(vmem_limit_bytes=12 * 2**20),
+    )(z3, og, more)
 
 
 def shards(sizes, pre_act, out_grad, weight, error, q_init):
@@ -98,9 +140,10 @@
     error = error[0]
     core = lax.axis_index("core")
 
-    got = {(0, 0): out_grad.T}
+    og = out_grad.T
+    got = {(0, 0): og}
     iy, ix = lax.axis_index("y"), lax.axis_index("x")
-    state = [error, jnp.zeros_like(pre_act)]
+    state = []
 
     def fetch(*moves):
         new = {}
@@ -119,22 +162,26 @@
 
     def use(keys):
         where = jnp.stack([((iy + dy) & (ny - 1)) * nx + ((ix + dx) & (nx - 1)) for dy, dx in keys])
-        state[:] = add_products(where, pre_act, weight, [got[k] for k in keys], *state)
+        state[:] = add_products(where, pre_act, weight, [got[k] for k in keys], state)
+
+    one = fetch(((0, 0), "x", 1), ((0, 0), "x", -1), ((0, 0), "y", 1), ((0, 0), "y", -1))
 
     act = gelu16(pre_act)
     q3 = jnp.concatenate(split(q_init, 3), axis=1)
     y = fold(dot(q3, out_grad, 0, 1), 3)
-    y_all = tie(spread(y, MP), [(0, 0)])
-    one = fetch(((0, 0), "x", 1), ((0, 0), "x", -1), ((0, 0), "y", 1), ((0, 0), "y", -1))
+    y_all = tie(spread(y, MP), one)
+    two = fetch(((0, 1), "y", 1), ((0, -1), "y", -1), ((1, 0), "x", -1), ((-1, 0), "x", 1))
+    use([(0, 0)] + one)
     y_all = y_all.transpose(1, 0, 2).reshape(rank, toks)
     y3 = jnp.concatenate(split(y_all, 3), axis=0)
     e2 = split(error, 2)
     p_err = sum(fold(dot(q3, e, 0, 1), 3) for e in e2)
     p_local = fold(dot(y3, act, 1, 1), 3) + p_err
-    pbar = jnp.sum(spread(p_local, "z"), axis=0)
-    pbar = tie((pbar + other_core(pbar)) / groups, one)
+    pbar = jnp.sum(tie(spread(p_local, "z"), [], True), axis=0)
+    pbar = tie((pbar + other_core(pbar)) / groups, two)
 
     l3 = jnp.concatenate(split(pbar, 3), axis=0)
+    r_error = sum(fold(dot(l3, e, 1, 0), 3) for e in e2)
     z_part = fold(dot(l3, act, 1, 0), 3)
     gram_part = jnp.dot(pbar, pbar.T, precision=hi)
     side = 128 // rank
@@ -146,26 +193,23 @@
         ],
         axis=1,
     )
-    took = tie(lax.all_to_all(sent, MP, 0, 0, tiled=True), one)
-    two = fetch(((0, 1), "y", 1), ((0, -1), "y", -1), ((1, 0), "x", -1), ((-1, 0), "x", 1))
-    use([(0, 0)] + one)
+    took = tie(lax.all_to_all(sent, MP, 0, 0, tiled=True), two + [(0, 1), (1, 0)])
+    three = fetch(((0, 1), "x", 1), ((1, 0), "y", 1), ((1, -1), "x", -1), ((-1, 1), "y", -1))
+    use(two)
     took = jnp.sum(took, axis=0)
     z = took[:rank]
     gram = jnp.concatenate(jnp.split(took[rank:], side, axis=1), axis=0)
 
     z3 = jnp.concatenate(split(z, 3), axis=0)
-    r_local = fold(dot(z3, out_grad, 1, 0), 3) + sum(fold(dot(l3, e, 1, 0), 3) for e in e2)
+    r_local = right_factor(z3, og, r_error)
     low, high = r_local[:half], r_local[half:]
     keep = jnp.where(core == 0, low, high) + other_core(jnp.where(core == 0, high, low))
     r_part = lax.all_to_all(keep.reshape(nz, half // nz, feat), "z", 0, 0, tiled=True)
-    r_part = tie(jnp.sum(r_part, axis=0), two, True)
-    r_part = tie(spread(r_part, MP), two)
-    three = fetch(((0, 1), "x", 1), ((1, 0), "y", 1), ((1, -1), "x", -1), ((-1, 1), "y", -1))
-    use(two)
-    r_part = jnp.sum(r_part, axis=0) / groups
-    mine = tie(spread(r_part, "z"), three, True).reshape(half, feat)
+    r_part = jnp.sum(tie(r_part, three + [(3, 1), (3, 3)], True), axis=0)
     four = fetch(((-1, 1), "x", 1), ((1, 2), "y", 1), ((-1, -1), "y", -1))
     use(three)
+    r_part = jnp.sum(spread(r_part, MP), axis=0) / groups
+    mine = tie(spread(r_part, "z"), four, True).reshape(half, feat)
     use(four)
     theirs = other_core(mine)
     r_all = jnp.concatenate([jnp.where(core == 0, mine, theirs), jnp.where(core == 0, theirs, mine)], axis=0)
@@ -178,9 +222,9 @@
     mat, pre_grad = state
     ph, pw = split(phat, 2)
     qh, ql = split(q_t, 2)
-    left = jnp.concatenate([ph, ph, pw], axis=0)
+    left = jnp.concatenate([ph, ph, pw], axis=0).T
     right = jnp.concatenate([qh, ql, qh], axis=0)
-    new_error = (mat - dot(left, right, 0, 0))[None]
+    new_error = new_errors(mat, error[:, None], left, right).transpose(1, 0, 2)
     return (pre_grad, new_error, q_t.T)
 
 

time: 196 us -> 187 us (0.954)
  blocking collectives: 17.4 us -> 0 us
  starting transfers between devices: 64.2 us -> 70.3 us
  Pallas kernels: 24.3 us -> 28.5 us
  local copies, waits for them, and re-layouts: 23.2 us -> 20.6 us
  other arithmetic: 13.1 us -> 15.1 us
    all_to_all x1 -> x0, blocking collectives: 17.4 us -> none  [spread(): lax.all_to_all(jnp.broadcast_to(x, (n,) + x.shape), axis, 0, 0, tiled=True)]
    ppermute x15, waiting for transfers between devices: 23.1 us -> 10.9 us  [shift(): return lax.ppermute(x, axis, [((i + step) % n, i) for i in range(n)])]
    all_to_all x3 -> x4, waiting for transfers between devices: 9.55 us -> 18.7 us  [spread(): lax.all_to_all(jnp.broadcast_to(x, (n,) + x.shape), axis, 0, 0, tiled=True)]
    all_to_all x3 -> x4, starting transfers between devices: 21 us -> 27.3 us  [spread(): lax.all_to_all(jnp.broadcast_to(x, (n,) + x.shape), axis, 0, 0, tiled=True)]
    pallas_call x4 -> x6, Pallas kernels: 24.3 us -> 28.5 us  [the longest x4 24.9 us: add_products(): pl.pallas_call(functools.partial(products, n), out_shape=(mat, jax.ShapeD...]
    unnamed x46 -> x50, local copies, waits for them, and re-layouts: 17.7 us -> 15 us
    ppermute x3, starting transfers between devices: 14.7 us -> 12.4 us  [other_core(): return lax.ppermute(x, 'core', [(0, 1), (1, 0)])]
    dot_general x9 -> x7, matrix products: 11.9 us -> 11 us  [dot(): lax.dot_general(a, b, (((ca,), (cb,)), ((), ())), preferred_element_type=...]
  transfers between devices with their start and end apart: 23 -> 24, of which waited for: 12 -> 10; matrix products, arithmetic and copies ran while one was open for 12% -> 13% of each run, Pallas kernels for 10% -> 13%
where the time goes in v8:
time: 187 us; the launch traced here: 186 us
  starting transfers between devices  70.3 us (38%)
  waiting for transfers between devices  37.4 us (20%)
  Pallas kernels  28.5 us (15%)
  local copies, waits for them, and re-layouts  20.6 us (11%)
  other arithmetic  15.1 us (8%)
  matrix products  13 us (7%)
    all_to_all x4, starting transfers between devices, spread(): lax.all_to_all(jnp.broadcast_to(x, (n,) + x.shape), axis, 0, 0, tiled=True)  27.3 us
    pallas_call x4, Pallas kernels, add_products(): pl.pallas_call(functools.partial(products, n), out_shape=(mat, jax.ShapeD...  24.9 us
    all_to_all x4, waiting for transfers between devices, spread(): lax.all_to_all(jnp.broadcast_to(x, (n,) + x.shape), axis, 0, 0, tiled=True)  18.7 us
    ppermute x15, starting transfers between devices, shift(): return lax.ppermute(x, axis, [((i + step) % n, i) for i in range(n)])  18.6 us
    unnamed x50, local copies, waits for them, and re-layouts  15 us
    ppermute x3, starting transfers between devices, other_core(): return lax.ppermute(x, 'core', [(0, 1), (1, 0)])  12.4 us
    dot_general x7, matrix products, dot(): lax.dot_general(a, b, (((ca,), (cb,)), ((), ())), preferred_element_type=...  11 us
    ppermute x15, waiting for transfers between devices, shift(): return lax.ppermute(x, axis, [((i + step) % n, i) for i in range(n)])  10.9 us
  transfers between devices with their start and end apart: 24, of which 10 were waited for; matrix products, arithmetic and copies ran while one was open for 13% of the time, Pallas kernels for 13%

profile of v8, /device:TPU:1, one launch (start us, length us, event | category | flops | bytes accessed | tf_op | source)
XLA Modules:
  0.0 186.0 jit_solution(6574645749375602711)
XLA Ops:
  0.6 3.4 %collective-permute-start = (bf16[4800,128]{1,0:T(8,128)(2,1)}, bf16[4800,128]{1,0:T(8,128)(2,1)}, u32[]{:S(2)}, u32[]{:S(2)}) collective-permute-start(bf16[4800,128]{1,0:T(8,128)(2,1)} %bitcast.63), channel_id=1, source_target_pairs={{1,0},{2,1},{3,2},{0,3},{5,4},{6,5},{7,6},{4,7},{9,8},{10,9},{11,1... | collective-permute-start | bytes 3686408 | tf_op jit(solution)/shard_map/ppermute | solution.py:54
  4.0 2.7 %collective-permute-start.2 = (bf16[4800,128]{1,0:T(8,128)(2,1)}, bf16[4800,128]{1,0:T(8,128)(2,1)}, u32[]{:S(2)}, u32[]{:S(2)}) collective-permute-start(bf16[4800,128]{1,0:T(8,128)(2,1)} %bitcast.65), channel_id=1, source_target_pairs={{4,0},{8,4},{12,8},{0,12},{5,1},{9,5},{13,9},{1,13},{6,2},{10,6},{... | collective-permute-start | bytes 3686408 | tf_op jit(solution)/shard_map/ppermute | solution.py:54
  6.8 1.2 reduce-precision_convert_fusion.3
  9.4 6.5 %all-to-all-start = ((f32[16,32,128]{2,1,0:T(8,128)}), f32[16,32,128]{2,1,0:T(8,128)}, u32[]{:S(2)}, u32[]{:S(2)}) async-start(f32[16,32,128]{2,1,0:T(8,128)} %broadcast_in_dim.17), calls=%async_computation | async-start | bytes 524288 | tf_op jit(solution)/shard_map/all_to_all | solution.py:45
  16.0 2.2 %fusion.32 = f32[96,150]{0,1:T(8,128)} fusion(f32[1,150,4800]{2,0,1:T(1,128)S(1)} %copy-done, bf16[4800,32]{0,1:T(8,128)(2,1)S(1)} %get-tuple-element.94, bf16[4800,32]{0,1:T(8,128)(2,1)} %copy-done.21, bf16[4800,32]{0,1:T(8,128)(2,1)S(1)} %get-tuple-element.93), kind=kOutput, calls=%fused_computation.68 | convolution fusion | flops 143884800 | bytes 3859200 | tf_op jit(solution)/shard_map/dot_general | solution.py:35
  18.2 2.3 %fusion.18 = f32[96,150]{0,1:T(8,128)} fusion(f32[1,150,4800]{2,0,1:T(1,128)S(1)} %copy-done, bf16[4800,32]{0,1:T(8,128)(2,1)} %copy-done.20, bf16[4800,32]{0,1:T(8,128)(2,1)S(1)} %copy-done.22, bf16[4800,32]{0,1:T(8,128)(2,1)} %copy-done.19), kind=kOutput, calls=%fused_computation.36 | convolution fusion | flops 142444800 | bytes 3859200 | tf_op jit(solution)/shard_map/dot_general | solution.py:35
  20.5 17.0 %all-to-all-done = f32[16,32,128]{2,1,0:T(8,128)} async-done(((f32[16,32,128]{2,1,0:T(8,128)}), f32[16,32,128]{2,1,0:T(8,128)}, u32[]{:S(2)}, u32[]{:S(2)}) %all-to-all-start) | async-done | bytes 262176 | tf_op jit(solution)/shard_map/all_to_all | solution.py:45
  39.2 3.0 %collective-permute-start.8 = (bf16[4800,128]{1,0:T(8,128)(2,1)}, bf16[4800,128]{1,0:T(8,128)(2,1)}, u32[]{:S(2)}, u32[]{:S(2)}) collective-permute-start(bf16[4800,128]{1,0:T(8,128)(2,1)} %collective-permute-done.3.refs_4_), channel_id=1, source_target_pairs={{1,0},{2,1},{3,2},{0,3},{5,4},{6,5},{7,6},{4,7},{9,8},{10,9},{11,1... | collective-permute-start | bytes 3686408 | tf_op jit(solution)/shard_map/ppermute | solution.py:54
  45.1 8.2 %all-to-all-start.1 = ((f32[8,32,150]{2,1,0:T(8,128)}), f32[8,32,150]{2,1,0:T(8,128)S(1)}, u32[]{:S(2)}, u32[]{:S(2)}) async-start(f32[8,32,150]{2,1,0:T(8,128)} %broadcast_in_dim.18), calls=%async_computation.1 | async-start | bytes 524288 | tf_op jit(solution)/shard_map/all_to_all | solution.py:45
  53.4 1.4 copy-done.3
  54.8 1.1 copy-done.8
  55.8 1.3 copy-done.13
  57.1 6.7 %shard_map.76 = (f32[150,4800]{1,0:T(8,128)S(1)}, bf16[150,2048]{1,0:T(8,128)(2,1)}) custom-call(s32[5]{0:T(128)S(1)} %stack.69.where, bf16[150,2048]{1,0:T(8,128)(2,1)S(1)} %copy-done.8, bf16[150,4800]{1,0:T(8,128)(2,1)S(1)} %copy-done.3, bf16[4800,128]{1,0:T(8,128)(2,1)S(1)} %bitcast.67, bf16[4800,128]{1,0:T(8,128)(2,1)} %collective-permute-done.refs_1_, ...), custom_call_target="tpu_custom_call" | custom-call | tf_op jit(solution)/shard_map/pallas_call | solution.py:83
  63.9 4.3 %collective-permute-start.4 = (f32[32,150]{1,0:T(8,128)S(1)}, f32[32,150]{1,0:T(8,128)S(1)}, u32[]{:S(2)}, u32[]{:S(2)}) collective-permute-start(f32[32,150]{1,0:T(8,128)S(1)} %reduce_sum.36), channel_id=1, source_target_pairs={{0,16},{16,0},{1,17},{17,1},{2,18},{18,2},{3,19},{19,3},{4,20},{20... | collective-permute-start | bytes 57608 | tf_op jit(solution)/shard_map/ppermute | solution.py:49
  69.3 1.9 %fusion.44 = f32[96,2048]{1,0:T(8,128)S(1)} fusion(bf16[32,150]{1,0:T(8,128)(2,1)S(1)} %get-tuple-element.102, bf16[32,150]{1,0:T(8,128)(2,1)S(1)} %get-tuple-element.103, bf16[32,150]{1,0:T(8,128)(2,1)S(1)} %get-tuple-element.101, bf16[150,2048]{1,0:T(8,128)(2,1)} %pre_ref.7), kind=kOutput, calls=%fused_computation.105 | convolution fusion | flops 62140800 | bytes 1429632 | tf_op jit(solution)/shard_map/dot_general | solution.py:35
  71.3 1.8 fusion.17
  73.1 1.8 fusion.30
  75.7 3.8 %all-to-all-start.2 = ((f32[16,40,128]{2,1,0:T(8,128)}), f32[16,40,128]{2,1,0:T(8,128)S(1)}, u32[]{:S(2)}, u32[]{:S(2)}) async-start(f32[16,40,128]{2,1,0:T(8,128)} %pad_maximum_fusion.2), calls=%async_computation.2 | async-start | bytes 655360 | tf_op jit(solution)/shard_map/all_to_all | solution.py:196
  79.5 3.0 %fusion.12.more_ref = f32[32,4800]{1,0:T(8,128)} fusion(f32[96,4800]{1,0:T(8,128)} %fusion.30, f32[96,4800]{1,0:T(8,128)} %fusion.17), kind=kLoop, calls=%fused_computation.27 | loop fusion | flops 768000 | bytes 4300800 | tf_op jit(solution)/shard_map/add | solution.py:184
  82.5 5.0 %all-to-all-done.2 = f32[16,40,128]{2,1,0:T(8,128)S(1)} async-done(((f32[16,40,128]{2,1,0:T(8,128)}), f32[16,40,128]{2,1,0:T(8,128)S(1)}, u32[]{:S(2)}, u32[]{:S(2)}) %all-to-all-start.2) | async-done | bytes 327712 | tf_op jit(solution)/shard_map/all_to_all | solution.py:196
  87.6 1.3 copy-done.14
  88.8 1.1 copy-done.15
  90.5 4.6 %collective-permute-start.9 = (f32[16,4800]{1,0:T(8,128)S(1)}, f32[16,4800]{1,0:T(8,128)S(1)}, u32[]{:S(2)}, u32[]{:S(2)}) collective-permute-start(f32[16,4800]{1,0:T(8,128)S(1)} %slice_select_fusion), channel_id=1, source_target_pairs={{0,16},{16,0},{1,17},{17,1},{2,18},{18,2},{3,19},{19,3},{4,20},{20... | collective-permute-start | bytes 921608 | tf_op jit(solution)/shard_map/ppermute | solution.py:49
  99.0 8.2 %all-to-all-start.3 = ((f32[8,2,4800]{2,1,0:T(2,128)}), f32[8,2,4800]{2,1,0:T(2,128)S(1)}, u32[]{:S(2)}, u32[]{:S(2)}) async-start(f32[8,2,4800]{2,1,0:T(2,128)} %reshape.30), calls=%async_computation.3 | async-start | bytes 622592 | tf_op jit(solution)/shard_map/all_to_all | solution.py:207
  107.4 1.4 copy-done.4
  108.8 1.1 copy-done.9
  109.9 6.3 %shard_map.78 = (f32[150,4800]{1,0:T(8,128)S(1)}, bf16[150,2048]{1,0:T(8,128)(2,1)}) custom-call(s32[4]{0:T(128)S(1)} %pad_add_fusion.1.where, bf16[150,2048]{1,0:T(8,128)(2,1)S(1)} %copy-done.9, bf16[150,4800]{1,0:T(8,128)(2,1)S(1)} %copy-done.4, bf16[4800,128]{1,0:T(8,128)(2,1)} %collective-permute-done.5.refs_0_, ...), custom_call_target="tpu_custom_call", output_to_operand_aliasing={{0}: (7, {}), {1}: (8, {})} | custom-call | tf_op jit(solution)/shard_map/pallas_call | solution.py:83
  116.2 1.9 %all-to-all-done.3 = f32[8,2,4800]{2,1,0:T(2,128)S(1)} async-done(((f32[8,2,4800]{2,1,0:T(2,128)}), f32[8,2,4800]{2,1,0:T(2,128)S(1)}, u32[]{:S(2)}, u32[]{:S(2)}) %all-to-all-start.3) | async-done | bytes 307232 | tf_op jit(solution)/shard_map/all_to_all | solution.py:207
  118.1 5.9 %collective-permute-done.10.refs_0_ = bf16[4800,128]{1,0:T(8,128)(2,1)} collective-permute-done((bf16[4800,128]{1,0:T(8,128)(2,1)}, bf16[4800,128]{1,0:T(8,128)(2,1)}, u32[]{:S(2)}, u32[]{:S(2)}) %collective-permute-start.10) | collective-permute-done | bytes 1228832 | tf_op jit(solution)/shard_map/ppermute | solution.py:54
  124.0 1.8 collective-permute-done.12.refs_2_
  127.4 4.3 %all-to-all-start.4 = ((f32[16,2,4800]{2,1,0:T(2,128)}), f32[16,2,4800]{2,1,0:T(2,128)}, u32[]{:S(2)}, u32[]{:S(2)}) async-start(f32[16,2,4800]{2,1,0:T(2,128)} %broadcast_in_dim.20), calls=%async_computation.4 | async-start | bytes 1245184 | tf_op jit(solution)/shard_map/all_to_all | solution.py:45
  132.3 2.9 %cholesky.17 = f32[32,32]{1,0:T(8,128)S(1)} custom-call(f32[32,32]{1,0:T(8,128)S(1)} %fusion.41), custom_call_target="Cholesky" | custom-call | tf_op jit(solution)/shard_map/jit(cholesky)/cholesky | solution.py:217
  135.9 2.4 %collective-permute-start.14 = (bf16[4800,128]{1,0:T(8,128)(2,1)}, bf16[4800,128]{1,0:T(8,128)(2,1)}, u32[]{:S(2)}, u32[]{:S(2)}) collective-permute-start(bf16[4800,128]{1,0:T(8,128)(2,1)} %collective-permute-done.8.refs_3_), channel_id=1, source_target_pairs={{1,0},{2,1},{3,2},{0,3},{5,4},{6,5},{7,6},{4,7},{9,8},{10,9},{11,1... | collective-permute-start | bytes 3686408 | tf_op jit(solution)/shard_map/ppermute | solution.py:54
  138.3 2.5 %collective-permute-start.15 = (bf16[4800,128]{1,0:T(8,128)(2,1)}, bf16[4800,128]{1,0:T(8,128)(2,1)}, u32[]{:S(2)}, u32[]{:S(2)}) collective-permute-start(bf16[4800,128]{1,0:T(8,128)(2,1)} %collective-permute-done.12.refs_2_), channel_id=1, source_target_pairs={{4,0},{8,4},{12,8},{0,12},{5,1},{9,5},{13,9},{1,13},{6,2},{10,6},{... | collective-permute-start | bytes 3686408 | tf_op jit(solution)/shard_map/ppermute | solution.py:54
  140.8 1.7 all-to-all-done.4
  142.5 1.3 reduce_sum.39
  144.6 8.4 %all-to-all-start.5 = ((f32[8,2,4800]{2,1,0:T(2,128)}), f32[8,2,4800]{2,1,0:T(2,128)S(1)}, u32[]{:S(2)}, u32[]{:S(2)}) async-start(f32[8,2,4800]{2,1,0:T(2,128)} %broadcast_in_dim.21), calls=%async_computation.5 | async-start | bytes 622592 | tf_op jit(solution)/shard_map/all_to_all | solution.py:45
  153.7 2.4 %custom-call.7 = f32[1,32,32]{1,2,0:T(8,128)S(1)} custom-call(f32[1,32,32]{2,1,0:T(8,128)S(1)} %fusion.36), custom_call_target="InvertDiagBlocksLowerTriangular" | custom-call | tf_op jit(solution)/shard_map/jit(_solve_triangular)/triangular_solve | solution.py:218
  156.7 1.4 copy-done.5
  158.1 1.1 copy-done.10
  159.2 6.3 %shard_map.79 = (f32[150,4800]{1,0:T(8,128)S(1)}, bf16[150,2048]{1,0:T(8,128)(2,1)}) custom-call(s32[4]{0:T(128)S(1)} %pad_add_fusion.2.where, bf16[150,2048]{1,0:T(8,128)(2,1)S(1)} %copy-done.10, bf16[150,4800]{1,0:T(8,128)(2,1)S(1)} %copy-done.5, bf16[4800,128]{1,0:T(8,128)(2,1)} %collective-permute-done.10.refs_0_, ...), custom_call_target="tpu_custom_call", output_to_operand_aliasing={{0}: (7, {}), {1}: (8, {})} | custom-call | tf_op jit(solution)/shard_map/pallas_call | solution.py:83
  165.5 2.1 %collective-permute-done.15.refs_1_ = bf16[4800,128]{1,0:T(8,128)(2,1)} collective-permute-done((bf16[4800,128]{1,0:T(8,128)(2,1)}, bf16[4800,128]{1,0:T(8,128)(2,1)}, u32[]{:S(2)}, u32[]{:S(2)}) %collective-permute-start.15) | collective-permute-done | bytes 1228832 | tf_op jit(solution)/shard_map/ppermute | solution.py:54
  169.1 3.6 %collective-permute-start.17 = (f32[16,4800]{1,0:T(8,128)}, f32[16,4800]{1,0:T(8,128)S(1)}, u32[]{:S(2)}, u32[]{:S(2)}) collective-permute-start(f32[16,4800]{1,0:T(8,128)} %reshape.31), channel_id=1, source_target_pairs={{0,16},{16,0},{1,17},{17,1},{2,18},{18,2},{3,19},{19,3},{4,20},{20... | collective-permute-start | bytes 921608 | tf_op jit(solution)/shard_map/ppermute | solution.py:49
  172.8 1.4 copy-done.6
  174.2 1.1 copy-done.11
  175.2 5.6 %shard_map.80 = (f32[150,4800]{1,0:T(8,128)S(1)}, bf16[150,2048]{1,0:T(8,128)(2,1)}) custom-call(s32[3]{0:T(128)S(1)} %pad_add_fusion.where, bf16[150,2048]{1,0:T(8,128)(2,1)S(1)} %copy-done.11, bf16[150,4800]{1,0:T(8,128)(2,1)S(1)} %copy-done.6, bf16[4800,128]{1,0:T(8,128)(2,1)} %collective-permute-done.14.refs_0_, ...), custom_call_target="tpu_custom_call", output_to_operand_aliasing={{0}: (6, {}), {1}: (7, {})} | custom-call | tf_op jit(solution)/shard_map/pallas_call | solution.py:83
  180.9 1.5 fusion.11
  182.9 3.1 %shard_map.81 = f32[150,1,4800]{2,1,0:T(1,128)} custom-call(f32[150,4800]{1,0:T(8,128)S(1)} %get-tuple-element.87.mat_ref, f32[150,1,4800]{2,1,0:T(1,128)S(1)} %bitcast.62, bf16[150,96]{1,0:T(8,128)(2,1)S(1)} %maximum_bitcast_fusion.left_ref, bf16[96,4800]{1,0:T(8,128)(2,1)S(1)} %pad_maximum_fusion.1.right_ref), custom_call_target="tpu_custom_call" | custom-call | tf_op jit(solution)/shard_map/pallas_call | solution.py:103
  (114 shorter events, 20.2 us)
Async XLA Ops:
  0.6 7.4 %copy-start.12 = (bf16[128,4800]{0,1:T(8,128)(2,1)S(1)}, bf16[128,4800]{0,1:T(8,128)(2,1)}, u32[]{:S(2)}) copy-start(bf16[128,4800]{0,1:T(8,128)(2,1)} %param.6) | copy-start | bytes 3686404
  0.6 36.9 %collective-permute-start = (bf16[4800,128]{1,0:T(8,128)(2,1)}, bf16[4800,128]{1,0:T(8,128)(2,1)}, u32[]{:S(2)}, u32[]{:S(2)}) collective-permute-start(bf16[4800,128]{1,0:T(8,128)(2,1)} %bitcast.63), channel_id=1, source_target_pairs={{1,0},{2,1},{3,2},{0,3},{5,4},{6,5},{7,6},{4,7},{9,8},{10,9},{11,1... | collective-permute-start | bytes 3686408 | tf_op jit(solution)/shard_map/ppermute | solution.py:54
  4.0 33.5 %collective-permute-start.1 = (bf16[4800,128]{1,0:T(8,128)(2,1)}, bf16[4800,128]{1,0:T(8,128)(2,1)}, u32[]{:S(2)}, u32[]{:S(2)}) collective-permute-start(bf16[4800,128]{1,0:T(8,128)(2,1)} %bitcast.64), channel_id=1, source_target_pairs={{3,0},{0,1},{1,2},{2,3},{7,4},{4,5},{5,6},{6,7},{11,8},{8,9},{9,10... | collective-permute-start | bytes 3686408 | tf_op jit(solution)/shard_map/ppermute | solution.py:54
  4.0 33.5 %collective-permute-start.2 = (bf16[4800,128]{1,0:T(8,128)(2,1)}, bf16[4800,128]{1,0:T(8,128)(2,1)}, u32[]{:S(2)}, u32[]{:S(2)}) collective-permute-start(bf16[4800,128]{1,0:T(8,128)(2,1)} %bitcast.65), channel_id=1, source_target_pairs={{4,0},{8,4},{12,8},{0,12},{5,1},{9,5},{13,9},{1,13},{6,2},{10,6},{... | collective-permute-start | bytes 3686408 | tf_op jit(solution)/shard_map/ppermute | solution.py:54
  6.8 30.7 %collective-permute-start.3 = (bf16[4800,128]{1,0:T(8,128)(2,1)}, bf16[4800,128]{1,0:T(8,128)(2,1)}, u32[]{:S(2)}, u32[]{:S(2)}) collective-permute-start(bf16[4800,128]{1,0:T(8,128)(2,1)} %bitcast.66), channel_id=1, source_target_pairs={{12,0},{0,4},{4,8},{8,12},{13,1},{1,5},{5,9},{9,13},{14,2},{2,6},{... | collective-permute-start | bytes 3686408 | tf_op jit(solution)/shard_map/ppermute | solution.py:54
  8.0 0.7 copy-start.21
  8.0 8.0 %copy-start.19 = (bf16[4800,32]{0,1:T(8,128)(2,1)}, bf16[4800,32]{0,1:T(8,128)(2,1)S(1)}, u32[]{:S(2)}) copy-start(bf16[4800,32]{0,1:T(8,128)(2,1)S(1)} %get-tuple-element.93) | copy-start | bytes 921604
  8.0 7.9 %copy-start.20 = (bf16[4800,32]{0,1:T(8,128)(2,1)}, bf16[4800,32]{0,1:T(8,128)(2,1)S(1)}, u32[]{:S(2)}) copy-start(bf16[4800,32]{0,1:T(8,128)(2,1)S(1)} %get-tuple-element.94) | copy-start | bytes 921604
  8.0 7.9 %copy-start = (f32[1,150,4800]{2,0,1:T(1,128)S(1)}, f32[1,150,4800]{2,0,1:T(1,128)}, u32[]{:S(2)}) copy-start(f32[1,150,4800]{2,0,1:T(1,128)} %param.8) | copy-start | bytes 8640004
  9.4 28.1 %all-to-all-start = ((f32[16,32,128]{2,1,0:T(8,128)}), f32[16,32,128]{2,1,0:T(8,128)}, u32[]{:S(2)}, u32[]{:S(2)}) async-start(f32[16,32,128]{2,1,0:T(8,128)} %broadcast_in_dim.17), calls=%async_computation | async-start | bytes 524288 | tf_op jit(solution)/shard_map/all_to_all | solution.py:45
  16.0 2.2 %copy-start.22 = (bf16[4800,32]{0,1:T(8,128)(2,1)S(1)}, bf16[4800,32]{0,1:T(8,128)(2,1)}, u32[]{:S(2)}) copy-start(bf16[4800,32]{0,1:T(8,128)(2,1)} %copy-done.21) | copy-start | bytes 921604
  18.2 25.0 %copy-start.7 = (bf16[150,2048]{1,0:T(8,128)(2,1)S(1)}, bf16[150,2048]{1,0:T(8,128)(2,1)}, u32[]{:S(2)}) copy-start(bf16[150,2048]{1,0:T(8,128)(2,1)} %pre_ref.7) | copy-start | bytes 1843204
  37.5 31.5 %collective-permute-start.5 = (bf16[4800,128]{1,0:T(8,128)(2,1)}, bf16[4800,128]{1,0:T(8,128)(2,1)}, u32[]{:S(2)}, u32[]{:S(2)}) collective-permute-start(bf16[4800,128]{1,0:T(8,128)(2,1)} %collective-permute-done.refs_1_), channel_id=1, source_target_pairs={{4,0},{8,4},{12,8},{0,12},{5,1},{9,5},{13,9},{1,13},{6,2},{10,6},{... | collective-permute-start | bytes 3686408 | tf_op jit(solution)/shard_map/ppermute | solution.py:54
  38.6 30.4 %collective-permute-start.7 = (bf16[4800,128]{1,0:T(8,128)(2,1)}, bf16[4800,128]{1,0:T(8,128)(2,1)}, u32[]{:S(2)}, u32[]{:S(2)}) collective-permute-start(bf16[4800,128]{1,0:T(8,128)(2,1)} %collective-permute-done.2.refs_3_), channel_id=1, source_target_pairs={{3,0},{0,1},{1,2},{2,3},{7,4},{4,5},{5,6},{6,7},{11,8},{8,9},{9,10... | collective-permute-start | bytes 3686408 | tf_op jit(solution)/shard_map/ppermute | solution.py:54
  38.6 30.4 %collective-permute-start.6 = (bf16[4800,128]{1,0:T(8,128)(2,1)}, bf16[4800,128]{1,0:T(8,128)(2,1)}, u32[]{:S(2)}, u32[]{:S(2)}) collective-permute-start(bf16[4800,128]{1,0:T(8,128)(2,1)} %collective-permute-done.1.refs_2_), channel_id=1, source_target_pairs={{12,0},{0,4},{4,8},{8,12},{13,1},{1,5},{5,9},{9,13},{14,2},{2,6},{... | collective-permute-start | bytes 3686408 | tf_op jit(solution)/shard_map/ppermute | solution.py:54
  39.2 29.9 %collective-permute-start.8 = (bf16[4800,128]{1,0:T(8,128)(2,1)}, bf16[4800,128]{1,0:T(8,128)(2,1)}, u32[]{:S(2)}, u32[]{:S(2)}) collective-permute-start(bf16[4800,128]{1,0:T(8,128)(2,1)} %collective-permute-done.3.refs_4_), channel_id=1, source_target_pairs={{1,0},{2,1},{3,2},{0,3},{5,4},{6,5},{7,6},{4,7},{9,8},{10,9},{11,1... | collective-permute-start | bytes 3686408 | tf_op jit(solution)/shard_map/ppermute | solution.py:54
  43.2 0.9 copy-start.17
  43.2 0.9 copy-start.18
  45.1 18.7 %all-to-all-start.1 = ((f32[8,32,150]{2,1,0:T(8,128)}), f32[8,32,150]{2,1,0:T(8,128)S(1)}, u32[]{:S(2)}, u32[]{:S(2)}) async-start(f32[8,32,150]{2,1,0:T(8,128)} %broadcast_in_dim.18), calls=%async_computation.1 | async-start | bytes 524288 | tf_op jit(solution)/shard_map/all_to_all | solution.py:45
  53.4 1.4 copy-start.3
  54.8 1.1 copy-start.8
  55.8 1.3 copy-start.13
  63.9 5.1 %collective-permute-start.4 = (f32[32,150]{1,0:T(8,128)S(1)}, f32[32,150]{1,0:T(8,128)S(1)}, u32[]{:S(2)}, u32[]{:S(2)}) collective-permute-start(f32[32,150]{1,0:T(8,128)S(1)} %reduce_sum.36), channel_id=1, source_target_pairs={{0,16},{16,0},{1,17},{17,1},{2,18},{18,2},{3,19},{19,3},{4,20},{20... | collective-permute-start | bytes 57608 | tf_op jit(solution)/shard_map/ppermute | solution.py:49
  69.2 2.0 %copy-start.1 = (f32[1,150,4800]{2,0,1:T(1,128)S(1)}, f32[1,150,4800]{2,0,1:T(1,128)}, u32[]{:S(2)}) copy-start(f32[1,150,4800]{2,0,1:T(1,128)} %param.8) | copy-start | bytes 8640004
  75.7 11.8 %all-to-all-start.2 = ((f32[16,40,128]{2,1,0:T(8,128)}), f32[16,40,128]{2,1,0:T(8,128)S(1)}, u32[]{:S(2)}, u32[]{:S(2)}) async-start(f32[16,40,128]{2,1,0:T(8,128)} %pad_maximum_fusion.2), calls=%async_computation.2 | async-start | bytes 655360 | tf_op jit(solution)/shard_map/all_to_all | solution.py:196
  87.6 1.3 copy-start.14
  88.8 1.1 copy-start.15
  90.5 7.5 %collective-permute-start.9 = (f32[16,4800]{1,0:T(8,128)S(1)}, f32[16,4800]{1,0:T(8,128)S(1)}, u32[]{:S(2)}, u32[]{:S(2)}) collective-permute-start(f32[16,4800]{1,0:T(8,128)S(1)} %slice_select_fusion), channel_id=1, source_target_pairs={{0,16},{16,0},{1,17},{17,1},{2,18},{18,2},{3,19},{19,3},{4,20},{20... | collective-permute-start | bytes 921608 | tf_op jit(solution)/shard_map/ppermute | solution.py:49
  95.1 28.9 %collective-permute-start.10 = (bf16[4800,128]{1,0:T(8,128)(2,1)}, bf16[4800,128]{1,0:T(8,128)(2,1)}, u32[]{:S(2)}, u32[]{:S(2)}) collective-permute-start(bf16[4800,128]{1,0:T(8,128)(2,1)} %collective-permute-done.refs_1_), channel_id=1, source_target_pairs={{1,0},{2,1},{3,2},{0,3},{5,4},{6,5},{7,6},{4,7},{9,8},{10,9},{11,1... | collective-permute-start | bytes 3686408 | tf_op jit(solution)/shard_map/ppermute | solution.py:54
  95.4 28.6 %collective-permute-start.11 = (bf16[4800,128]{1,0:T(8,128)(2,1)}, bf16[4800,128]{1,0:T(8,128)(2,1)}, u32[]{:S(2)}, u32[]{:S(2)}) collective-permute-start(bf16[4800,128]{1,0:T(8,128)(2,1)} %collective-permute-done.2.refs_3_), channel_id=1, source_target_pairs={{4,0},{8,4},{12,8},{0,12},{5,1},{9,5},{13,9},{1,13},{6,2},{10,6},{... | collective-permute-start | bytes 3686408 | tf_op jit(solution)/shard_map/ppermute | solution.py:54
  96.3 29.5 %collective-permute-start.12 = (bf16[4800,128]{1,0:T(8,128)(2,1)}, bf16[4800,128]{1,0:T(8,128)(2,1)}, u32[]{:S(2)}, u32[]{:S(2)}) collective-permute-start(bf16[4800,128]{1,0:T(8,128)(2,1)} %collective-permute-done.7.refs_2_), channel_id=1, source_target_pairs={{3,0},{0,1},{1,2},{2,3},{7,4},{4,5},{5,6},{6,7},{11,8},{8,9},{9,10... | collective-permute-start | bytes 3686408 | tf_op jit(solution)/shard_map/ppermute | solution.py:54
  97.1 29.1 %collective-permute-start.13 = (bf16[4800,128]{1,0:T(8,128)(2,1)}, bf16[4800,128]{1,0:T(8,128)(2,1)}, u32[]{:S(2)}, u32[]{:S(2)}) collective-permute-start(bf16[4800,128]{1,0:T(8,128)(2,1)} %collective-permute-done.8.refs_3_), channel_id=1, source_target_pairs={{12,0},{0,4},{4,8},{8,12},{13,1},{1,5},{5,9},{9,13},{14,2},{2,6},{... | collective-permute-start | bytes 3686408 | tf_op jit(solution)/shard_map/ppermute | solution.py:54
  99.0 19.1 %all-to-all-start.3 = ((f32[8,2,4800]{2,1,0:T(2,128)}), f32[8,2,4800]{2,1,0:T(2,128)S(1)}, u32[]{:S(2)}, u32[]{:S(2)}) async-start(f32[8,2,4800]{2,1,0:T(2,128)} %reshape.30), calls=%async_computation.3 | async-start | bytes 622592 | tf_op jit(solution)/shard_map/all_to_all | solution.py:207
  107.4 1.4 copy-start.4
  108.8 1.1 copy-start.9
  127.4 15.1 %all-to-all-start.4 = ((f32[16,2,4800]{2,1,0:T(2,128)}), f32[16,2,4800]{2,1,0:T(2,128)}, u32[]{:S(2)}, u32[]{:S(2)}) async-start(f32[16,2,4800]{2,1,0:T(2,128)} %broadcast_in_dim.20), calls=%async_computation.4 | async-start | bytes 1245184 | tf_op jit(solution)/shard_map/all_to_all | solution.py:45
  135.9 29.6 %collective-permute-start.14 = (bf16[4800,128]{1,0:T(8,128)(2,1)}, bf16[4800,128]{1,0:T(8,128)(2,1)}, u32[]{:S(2)}, u32[]{:S(2)}) collective-permute-start(bf16[4800,128]{1,0:T(8,128)(2,1)} %collective-permute-done.8.refs_3_), channel_id=1, source_target_pairs={{1,0},{2,1},{3,2},{0,3},{5,4},{6,5},{7,6},{4,7},{9,8},{10,9},{11,1... | collective-permute-start | bytes 3686408 | tf_op jit(solution)/shard_map/ppermute | solution.py:54
  138.3 29.2 %collective-permute-start.15 = (bf16[4800,128]{1,0:T(8,128)(2,1)}, bf16[4800,128]{1,0:T(8,128)(2,1)}, u32[]{:S(2)}, u32[]{:S(2)}) collective-permute-start(bf16[4800,128]{1,0:T(8,128)(2,1)} %collective-permute-done.12.refs_2_), channel_id=1, source_target_pairs={{4,0},{8,4},{12,8},{0,12},{5,1},{9,5},{13,9},{1,13},{6,2},{10,6},{... | collective-permute-start | bytes 3686408 | tf_op jit(solution)/shard_map/ppermute | solution.py:54
  140.8 27.4 %collective-permute-start.16 = (bf16[4800,128]{1,0:T(8,128)(2,1)}, bf16[4800,128]{1,0:T(8,128)(2,1)}, u32[]{:S(2)}, u32[]{:S(2)}) collective-permute-start(bf16[4800,128]{1,0:T(8,128)(2,1)} %collective-permute-done.6.refs_1_), channel_id=1, source_target_pairs={{12,0},{0,4},{4,8},{8,12},{13,1},{1,5},{5,9},{9,13},{14,2},{2,6},{... | collective-permute-start | bytes 3686408 | tf_op jit(solution)/shard_map/ppermute | solution.py:54
  144.6 20.9 %all-to-all-start.5 = ((f32[8,2,4800]{2,1,0:T(2,128)}), f32[8,2,4800]{2,1,0:T(2,128)S(1)}, u32[]{:S(2)}, u32[]{:S(2)}) async-start(f32[8,2,4800]{2,1,0:T(2,128)} %broadcast_in_dim.21), calls=%async_computation.5 | async-start | bytes 622592 | tf_op jit(solution)/shard_map/all_to_all | solution.py:45
  156.7 1.4 copy-start.5
  158.1 1.1 copy-start.10
  169.1 11.7 %collective-permute-start.17 = (f32[16,4800]{1,0:T(8,128)}, f32[16,4800]{1,0:T(8,128)S(1)}, u32[]{:S(2)}, u32[]{:S(2)}) collective-permute-start(f32[16,4800]{1,0:T(8,128)} %reshape.31), channel_id=1, source_target_pairs={{0,16},{16,0},{1,17},{17,1},{2,18},{18,2},{3,19},{19,3},{4,20},{20... | collective-permute-start | bytes 921608 | tf_op jit(solution)/shard_map/ppermute | solution.py:49
  172.8 1.4 copy-start.6
  174.2 1.1 copy-start.11
  175.2 5.6 %copy-start.16 = (f32[16,4800]{1,0:T(8,128)S(1)}, f32[16,4800]{1,0:T(8,128)}, u32[]{:S(2)}) copy-start(f32[16,4800]{1,0:T(8,128)} %reshape.31) | copy-start | bytes 921604
  180.8 2.1 %copy-start.2 = (f32[1,150,4800]{2,0,1:T(1,128)S(1)}, f32[1,150,4800]{2,0,1:T(1,128)}, u32[]{:S(2)}) copy-start(f32[1,150,4800]{2,0,1:T(1,128)} %param.8) | copy-start | bytes 8640004
